TPU v7x, 32 devices: a whole 2x2x4 slice. The times are simulated.
32 devices in a mesh: fact: 8 (over z, y), feat: 4 (over x, core).
Axes of the slice: x: 2, y: 2, z: 4, core: 2. Of those that a mesh axis runs over, the one named last changes fastest.
Arguments:
- fact_x: bfloat16 [8192, 512], P('fact', 'feat'), may hold values from -6 to 6
- dim_owner: int32 [8192, 1], P('fact'), may hold values from 0 to 7; in each aligned block of 1024 rows (0 to 1023, 1024 to 2047, ...) at most 384 rows name the same one
- dim_slot: int32 [8192], P('fact'), may hold values from 0 to 1023
- fact_owner: int32 [8192, 1], P('fact'), may hold values from 0 to 7; in each aligned block of 1024 rows (0 to 1023, 1024 to 2047, ...) at most 384 rows name the same one
- fact_slot: int32 [8192], P('fact'), may hold values from 0 to 127
- dim_table: bfloat16 [8192, 512], P('fact', 'feat'), may hold values from -6 to 6
- entity_h: bfloat16 [1024, 512], P('fact', 'feat'), may hold values from -6 to 6
- w_msg: bfloat16 [512, 512], P(None, 'feat'), may hold values from -0.25 to 0.25
- w_self: bfloat16 [512, 512], P(None, 'feat'), may hold values from -0.25 to 0.25
- w_neigh: bfloat16 [512, 512], P(None, 'feat'), may hold values from -0.25 to 0.25
- cotangent: bfloat16 [1024, 512], P('fact', 'feat'), may hold values from -0.59765625 to 0.59765625
Outputs:
- output_h: bfloat16 [1024, 512], P('fact', 'feat')
- grad_w_msg: float32 [512, 512], P('fact', 'feat')
- grad_w_self: float32 [512, 512], P('fact', 'feat')
- grad_w_neigh: float32 [512, 512], P('fact', 'feat')
- grad_dim: float32 [8192, 512], P('fact', 'feat')
Inputs may be any that keep to these rules, and one draw needn't show every extreme that they name: `fact_owner`: among the fact rows of one index of fact, no key range is named by more than 384 rows, and some key range by exactly 384. `dim_owner`: among the fact rows of one index of fact, no block of the dimension table is named by more than 384 rows, and some block by exactly 384.
All inputs are finite; a program needn't handle non-finite values.
Results may differ from a plain program's by a relative error of at most 0.0059.
Values may be sent and summed in bfloat16 or wider, within the bound.
No kernel may reach another device: no remote copies, remote signals or barrier semaphores. Data moves between devices by JAX's collectives and lax.ppermute only.
A program may use at most 64 MiB of HBM per device.

v0:
```python
import functools

import jax
import jax.numpy as jnp
from jax import lax
from jax.experimental import pallas as pl
from jax.experimental.pallas import tpu as pltpu
from jax.sharding import PartitionSpec as P

LANES = 128
BF = jnp.bfloat16
F32 = jnp.float32
VMEM_LIMIT = 16 * 1024 * 1024
VMEM_LIMIT_LARGE = 40 * 1024 * 1024


def call(kernel, out_shape, scratch, flops, name, limit=VMEM_LIMIT):
    return pl.pallas_call(
        kernel,
        out_shape=out_shape,
        scratch_shapes=scratch,
        compiler_params=pltpu.CompilerParams(vmem_limit_bytes=limit),
        cost_estimate=pl.CostEstimate(flops=flops, bytes_accessed=1 << 20, transcendentals=0),
        name=name,
    )


def shape(dims, dtype):
    return jax.ShapeDtypeStruct(dims, dtype)


def nt(a, b):
    return lax.dot_general(a, b, (((1,), (1,)), ((), ())), preferred_element_type=F32)


def tn(a, b):
    return lax.dot_general(a, b, (((0,), (0,)), ((), ())), preferred_element_type=F32)


def dot(a, b):
    return jnp.dot(a, b, preferred_element_type=F32)


def flag(condition):
    return jnp.where(condition, 1.0, 0.0).astype(BF)


def column_codes(row):
    keys = jnp.broadcast_to(row, (LANES, LANES)).astype(F32).T.astype(jnp.int32)
    lane = lax.broadcasted_iota(jnp.int32, (LANES, LANES), 1)
    return flag((keys & (LANES - 1)) == lane), (keys >> 7).astype(F32).astype(BF)


def row_codes(row):
    keys = jnp.broadcast_to(row, (LANES, LANES))
    sub = lax.broadcasted_iota(jnp.int32, (LANES, LANES), 0)
    high = jnp.broadcast_to((row >> 7).astype(F32), (16, LANES)).astype(BF)
    return flag((keys & (LANES - 1)) == sub), high


def pick_block(low, high, block):
    zero = jnp.zeros((), BF)
    return jnp.where(high == block, low, zero)


def pick_rows(low, high, block):
    wide = low.reshape(LANES // 16, 16, low.shape[1])
    picked = pick_block(wide, high[None], block)
    return picked.reshape(low.shape)


def route_kernel(n, cap, ents, dims, do_ref, ds_ref, fo_ref, fs_ref, out_ref, pos_ref, ent_ref, dlow_ref, dhigh_ref):
    chunks = do_ref.shape[0]
    owner = do_ref[...]
    kind = lax.broadcasted_iota(jnp.int32, (n, chunks, LANES), 0)
    held = jnp.where(kind == owner[None], 1.0, 0.0).reshape(n * chunks, LANES)
    held_bf = held.astype(BF)
    i0 = lax.broadcasted_iota(jnp.int32, (LANES, LANES), 0)
    i1 = lax.broadcasted_iota(jnp.int32, (LANES, LANES), 1)
    inside = dot(held_bf, flag(i0 < i1))
    r0 = lax.broadcasted_iota(jnp.int32, (n * chunks, n * chunks), 0)
    r1 = lax.broadcasted_iota(jnp.int32, (n * chunks, n * chunks), 1)
    earlier = flag((r0 // chunks == r1 // chunks) & (r1 < r0))
    before = dot(dot(earlier, held_bf).astype(BF), jnp.ones((LANES, LANES), BF))
    rank = jnp.sum((held * (inside + before)).reshape(n, chunks, LANES), axis=0)
    rank = rank.astype(jnp.int32)
    entity_owner = fo_ref[...]
    entity_slot = fs_ref[...]
    value = ds_ref[...]
    pos_ref[...] = owner * cap + rank
    ent_ref[...] = entity_owner * ents + entity_slot
    fact_dim = owner * dims + value
    high = (value >> 5).astype(F32)
    low = (value & 31).astype(F32)
    names = lax.broadcasted_iota(jnp.int32, (n, LANES), 0)
    places = lax.broadcasted_iota(jnp.int32, (cap, LANES), 0)
    slots = lax.broadcasted_iota(jnp.int32, (ents, LANES), 0)
    asked_high = jnp.zeros((n, cap), F32)
    asked_low = jnp.zeros((n, cap), F32)
    hits = jnp.zeros((n, ents), F32)
    for k in range(chunks):
        here = slice(k * LANES, (k + 1) * LANES)
        mine = jnp.where(names == owner[k : k + 1], 1.0, 0.0)
        at = flag(places == rank[k : k + 1])
        asked_high += nt((mine * high[k : k + 1]).astype(BF), at)
        asked_low += nt((mine * low[k : k + 1]).astype(BF), at)
        hits += nt(flag(names == entity_owner[k : k + 1]), flag(slots == entity_slot[k : k + 1]))
        dlow_ref[here, :], dhigh_ref[here, :] = column_codes(fact_dim[k : k + 1])
    asked = (asked_high * 32.0 + asked_low).astype(jnp.int32)
    for r in range(cap // LANES):
        out_ref[:, r, :] = asked[:, r * LANES : (r + 1) * LANES]
    out_ref[:, cap // LANES, :] = hits.astype(jnp.int32)


def gather_rows(low_ref, high_ref, rows, table_refs, firsts, hot_ref):
    at = 0
    low, high = low_ref[rows, :], high_ref[rows, :]
    for table, first in zip(table_refs, firsts):
        for k in range(table.shape[0] // LANES):
            hot_ref[:, at : at + LANES] = pick_block(low, high, (first + k).astype(F32).astype(BF))
            at += LANES
    total, at = None, 0
    for table in table_refs:
        part = dot(hot_ref[:, at : at + table.shape[0]], table[...])
        total = part if total is None else total + part
        at += table.shape[0]
    return total


def ring_at(place, n):
    place = lax.rem(place + 2 * n, n)
    return jnp.where(place < n // 2, 2 * place, 2 * (n - 1 - place) + 1)


def ring_place(index, n):
    half = lax.div(index, 2)
    return jnp.where(lax.rem(index, 2) == 0, half, n - 1 - half)


def look_kernel(n, pieces, low_ref, high_ref, *refs):
    count = len(pieces)
    tables, base_ref, out_ref, hot_ref = refs[:count], refs[count], refs[-2], refs[-1]
    facts = low_ref.shape[0]
    step = hot_ref.shape[0]
    place = ring_place(lax.axis_index("fact"), n)
    firsts = [lax.div(ring_at(place + hops, n) * dims + row, LANES) for hops, row, dims in pieces]
    for c in range(facts // step):
        rows = slice(c * step, (c + 1) * step)
        out_ref[rows, :] = base_ref[rows, :] + gather_rows(low_ref, high_ref, rows, tables, firsts, hot_ref)


def message_kernel(n, pieces, low_ref, high_ref, *refs):
    count = len(pieces)
    tables, refs = refs[:count], refs[count:]
    base_ref, xw_ref, ent_ref, slope_ref, part_ref, hot_ref, msg_ref, erlow_ref, erhigh_ref = refs
    facts = low_ref.shape[0]
    step = hot_ref.shape[0]
    place = ring_place(lax.axis_index("fact"), n)
    firsts = [lax.div(ring_at(place + hops, n) * dims + row, LANES) for hops, row, dims in pieces]
    for k in range(ent_ref.shape[0]):
        here = slice(k * LANES, (k + 1) * LANES)
        erlow_ref[:, here], erhigh_ref[:, here] = row_codes(ent_ref[k : k + 1, :])
    for c in range(facts // step):
        rows = slice(c * step, (c + 1) * step)
        pre = xw_ref[rows, :] + base_ref[rows, :]
        if count:
            pre = pre + gather_rows(low_ref, high_ref, rows, tables, firsts, hot_ref)
        gate = jax.nn.sigmoid(pre)
        msg_ref[rows, :] = (pre * gate).astype(BF)
        slope_ref[rows, :] = gate * (1.0 + pre * (1.0 - gate))

    def add(pair, carry):
        hot = jnp.concatenate(
            [pick_rows(erlow_ref[...], erhigh_ref[...], (pair * 2 + i).astype(F32).astype(BF)) for i in range(2)], axis=0
        )
        rows = pl.ds(pl.multiple_of(pair * 256, 256), 256)
        part_ref[rows, :] = dot(hot, msg_ref[...]).astype(BF)
        return carry

    lax.fori_loop(0, part_ref.shape[0] // 256, add, 0)


def project_kernel(m, w_ref, *refs):
    blocks, out_ref = refs[:m], refs[m]
    me = lax.axis_index("feat")
    total = None
    for j, ref in enumerate(blocks):
        rows = pl.ds(pl.multiple_of((me ^ j) * LANES, LANES), LANES)
        part = dot(ref[...], w_ref[rows, :])
        total = part if total is None else total + part
    out_ref[...] = total


def ready_kernel(m, width, ents, idx_ref, *refs):
    x_refs, all_refs, (hidden_ref, div_ref, xt_ref, hold_ref) = refs[:m], refs[m : 2 * m], refs[2 * m :]
    rows_each = ents // m
    me = lax.axis_index("feat")
    hits = jnp.sum(idx_ref[:, idx_ref.shape[1] - 1, :], axis=0, keepdims=True).astype(F32)
    hold_ref[...] = jnp.maximum(jnp.broadcast_to(hits, (LANES, ents)).T, 1.0)
    div_ref[...] = hold_ref[pl.ds(pl.multiple_of(me * rows_each, rows_each), rows_each), :]
    for j in range(m):
        hidden_ref[me ^ j] = all_refs[j][2 * width : 2 * width + ents, :]
        xt_ref[pl.ds(pl.multiple_of((me ^ j) * LANES, LANES), LANES), :] = x_refs[j][...].T


def entity_kernel(n, m, width, ents, sums_ref, div_ref, *refs):
    all_refs, (back_ref, out_ref, pre_ref, agg_ref, own_ref) = refs[:m], refs[m:]
    rows_each = ents // m
    me = lax.axis_index("feat")
    divisor = div_ref[...]
    for b in range(m):
        total = sums_ref[b].astype(F32)
        for f in range(1, n):
            total += sums_ref[f * m + b].astype(F32)
        agg_ref[b * rows_each : (b + 1) * rows_each, :] = (total / divisor).astype(BF)
    at = pl.multiple_of(2 * width + me * rows_each, rows_each)
    for j in range(m):
        own_ref[me ^ j] = all_refs[j][pl.ds(at, rows_each), :]
    aggregate = jnp.concatenate([agg_ref[b * rows_each : (b + 1) * rows_each, :] for b in range(m)], axis=1)
    hidden = jnp.concatenate([own_ref[b] for b in range(m)], axis=1)
    d_agg = None
    for j in range(m):
        pre = dot(hidden, all_refs[j][0:width, :]) + dot(aggregate, all_refs[j][width : 2 * width, :])
        gate = jax.nn.sigmoid(pre)
        cot = all_refs[j][pl.ds(at + ents, rows_each), :].astype(F32)
        d_pre = (cot * (gate * (1.0 + pre * (1.0 - gate)))).astype(BF)
        out_ref[me ^ j] = (pre * gate).astype(BF)
        pre_ref[me ^ j] = d_pre
        term = nt(d_pre, all_refs[j][width : 2 * width, :])
        d_agg = term if d_agg is None else d_agg + term
    for b in range(m):
        scaled = (d_agg[:, b * LANES : (b + 1) * LANES] / divisor).astype(BF)
        for f in range(n):
            back_ref[f * m + b] = scaled


def share_kernel(m, out_ref, pre_ref, agg_ref, *share_refs):
    rows_each = out_ref.shape[1]
    me = lax.axis_index("feat")
    for j, ref in enumerate(share_refs):
        ref[0:rows_each, :] = out_ref[me ^ j]
        ref[rows_each : 2 * rows_each, :] = pre_ref[me ^ j]
        ref[2 * rows_each :, :] = agg_ref[...]


def weight_kernel(n, m, width, stride, hidden_ref, *refs):
    got, (out_ref, back_ref, total_ref, pre_ref, agg_ref) = refs[:m], refs[m:]
    rows_each = got[0].shape[0] // (2 + m)
    own = width // n
    me = lax.axis_index("feat")
    for j, ref in enumerate(got):
        here = pl.ds(pl.multiple_of((me ^ j) * rows_each, rows_each), rows_each)
        out_ref[here, :] = ref[0:rows_each, :]
        pre_ref[here, :] = ref[rows_each : 2 * rows_each, :]
        for b in range(m):
            agg_ref[b, here, :] = ref[(2 + b) * rows_each : (3 + b) * rows_each, :]
    d_pre = pre_ref[...]
    for which, blocks in enumerate((hidden_ref, agg_ref)):
        for b in range(m):
            total_ref[b * LANES : (b + 1) * LANES, :] = tn(blocks[b], d_pre)
        for d in range(n):
            back_ref[d % 2, d // 2, which * stride : (which + 1) * stride, :] = padded(
                total_ref[d * own : (d + 1) * own, :], stride
            )


def halves_kernel(back_ref, keep_ref, give_ref):
    odd = lax.rem(lax.axis_index("fact"), 2)
    keep_ref[...] = back_ref[odd]
    give_ref[...] = back_ref[1 - odd].astype(BF)


def padded(piece, rows):
    if piece.shape[0] == rows:
        return piece
    return jnp.concatenate([piece, jnp.zeros((rows - piece.shape[0], LANES), F32)], axis=0)


def codes_kernel(pos_ref, ent_ref, plow_ref, phigh_ref, elow_ref, ehigh_ref):
    for k in range(pos_ref.shape[0]):
        here = slice(k * LANES, (k + 1) * LANES)
        plow_ref[:, here], phigh_ref[:, here] = row_codes(pos_ref[k : k + 1, :])
        elow_ref[here, :], ehigh_ref[here, :] = column_codes(ent_ref[k : k + 1, :])


def request_kernel(n, cap, req_ref, low_ref, high_ref):
    for s in range(n):
        for r in range(cap // LANES):
            at = s * cap + r * LANES
            low_ref[:, at : at + LANES], high_ref[:, at : at + LANES] = row_codes(req_ref[s, r : r + 1, :])


def backward_kernel(n, stride, scaled_ref, slope_ref, low_ref, high_ref, xt_ref, dmsg_ref, share_ref, hot_ref):
    facts = slope_ref.shape[0]
    own = xt_ref.shape[0] // n
    step = hot_ref.shape[0]
    for c in range(facts // step):
        rows = slice(c * step, (c + 1) * step)
        found = gather_rows(low_ref, high_ref, rows, [scaled_ref], [jnp.int32(0)], hot_ref)
        dmsg_ref[rows, :] = (found * slope_ref[rows, :]).astype(BF)
    total = dot(xt_ref[...], dmsg_ref[...])
    for d in range(n):
        share_ref[d] = padded(total[d * own : (d + 1) * own, :], stride).astype(BF)


def spread_kernel(n, cap, stride, offsets, plow_ref, phigh_ref, dmsg_ref, share_ref, *refs):
    pair_refs, out_refs = refs[:-len(offsets)], refs[-len(offsets) :]
    me = lax.axis_index("fact")
    for offset, out_ref in zip(offsets, out_refs):
        d = lax.rem(me + offset, n)
        hot = jnp.concatenate(
            [
                pick_rows(plow_ref[...], phigh_ref[...], (d * (cap // LANES) + i).astype(F32).astype(BF))
                for i in range(cap // LANES)
            ],
            axis=0,
        )
        out_ref[0:cap, :] = dot(hot, dmsg_ref[...]).astype(BF)
        out_ref[cap : cap + stride, :] = share_ref[d]
        if out_ref.shape[0] > cap + stride:
            pair = pair_refs[0][lax.div(d, 2)]
            for ref in pair_refs[1:]:
                pair = pair + ref[lax.div(d, 2)].astype(F32)
            out_ref[cap + stride :, :] = pair.astype(BF)


def table_kernel(n, cap, stride, offsets, first, low_ref, high_ref, *refs):
    count = len(offsets)
    got, refs = refs[:count], refs[count:]
    if not first:
        (base_ref, weight_base_ref), refs = refs[:2], refs[2:]
    out_ref, weight_ref, rows_ref, klow_ref, khigh_ref = refs
    me = lax.axis_index("fact")
    if first:
        weight_ref[...] = jnp.zeros(weight_ref.shape, F32)
    else:
        weight_ref[...] = weight_base_ref[...]
    for j, (offset, ref) in enumerate(zip(offsets, got)):
        source = lax.rem(me + (n - offset), n)
        here = slice(j * cap, (j + 1) * cap)
        there = pl.ds(pl.multiple_of(source * cap, LANES), cap)
        rows_ref[here, :] = ref[0:cap, :]
        klow_ref[:, here] = low_ref[:, there]
        khigh_ref[:, here] = high_ref[:, there]
        rows = ref.shape[0] - cap
        weight_ref[0:rows, :] += ref[cap:, :].astype(F32)
    blocks = out_ref.shape[0] // LANES
    join = 2 if blocks % 2 == 0 else 1

    def add(group, carry):
        hot = jnp.concatenate(
            [pick_rows(klow_ref[...], khigh_ref[...], (group * join + i).astype(F32).astype(BF)) for i in range(join)], axis=0
        )
        rows = pl.ds(pl.multiple_of(group * join * LANES, LANES), join * LANES)
        sums = dot(hot, rows_ref[...])
        out_ref[rows, :] = sums if first else base_ref[rows, :] + sums
        return carry

    lax.fori_loop(0, blocks // join, add, 0)


def shards(fact_x, dim_owner, dim_slot, fact_owner, fact_slot, dim_table, entity_h, w_msg, w_self, w_neigh, cotangent):
    n, m = lax.axis_size("fact"), lax.axis_size("feat")
    assert m == 4 and n % 2 == 0
    facts = fact_x.shape[0]
    chunks = facts // LANES
    ents = entity_h.shape[0]
    rows_each = ents // m
    width = w_msg.shape[0]
    dims = dim_table.shape[0]
    cap = -(-(3 * facts // n) // LANES) * LANES
    slots = n * cap
    groups = cap // LANES + 1
    own = width // n
    stride = max(16, own)
    step = 512
    tie = lax.optimization_barrier
    ringed = n <= 8
    limit = VMEM_LIMIT if ringed else VMEM_LIMIT_LARGE

    ring = [2 * p if p < n // 2 else 2 * (n - 1 - p) + 1 for p in range(n)]
    to_right = [(ring[p], ring[(p + 1) % n]) for p in range(n)]
    to_left = [(ring[(p + 1) % n], ring[p]) for p in range(n)]

    def pass_on(right, left):
        return lax.ppermute(right, "fact", to_right), lax.ppermute(left, "fact", to_left)

    def swap(block, bit):
        return lax.ppermute(block, "feat", [(i, i ^ bit) for i in range(m)])

    if ringed:
        right, left = pass_on(dim_table, dim_table)
    x_far, x_near = swap(fact_x, 2), swap(fact_x, 1)

    by_lane = (chunks, LANES)
    columns = shape((facts, LANES), BF)
    asks, pos, entity, dlow, dhigh = call(
        functools.partial(route_kernel, n, cap, ents, dims),
        (
            shape((n, groups, LANES), jnp.int32),
            shape(by_lane, jnp.int32),
            shape(by_lane, jnp.int32),
            columns,
            columns,
        ),
        [],
        1 << 28,
        "route",
    )(dim_owner.reshape(by_lane), dim_slot.reshape(by_lane), fact_owner.reshape(by_lane), fact_slot.reshape(by_lane))
    if ringed:
        right, left, x_far, x_near, asks, pos, entity, dlow, dhigh = tie(
            (right, left, x_far, x_near, asks, pos, entity, dlow, dhigh)
        )

    def look(pieces, tables, base):
        rows = sum(t.shape[0] for t in tables)
        return call(
            functools.partial(look_kernel, n, pieces),
            shape((facts, LANES), F32),
            [pltpu.VMEM((step, rows), BF)],
            2 * facts * rows * LANES,
            "look",
            limit,
        )(dlow, dhigh, *tables, base)

    def project(blocks):
        return call(
            functools.partial(project_kernel, m), shape((facts, LANES), F32), [], 2 * facts * width * LANES, "project"
        )(w_msg, *blocks)

    found = jnp.zeros((facts, LANES), F32)
    weights = jnp.concatenate([w_self, w_neigh, entity_h, cotangent], axis=0)
    if ringed:
        half = dims // 2
        near = (right, left)
        after = pass_on(*near)
        x_last = swap(x_far, 1)
        found = look([(0, 0, dims), (-1, 0, dims), (1, 0, dims)], [dim_table, *near], found)
        right, left, x_last, found, weights = tie((*after, x_last, found, weights))
        for k in range(2, n // 2):
            last_round = k == n // 2 - 1
            after = pass_on(right[:half], left[half:]) if last_round else pass_on(right, left)
            if last_round:
                all_last = swap(all_far, 1)
            else:
                all_far, all_near = swap(weights, 2), swap(weights, 1)
                xw = project([fact_x, x_near, x_far, x_last])
            found = look([(-k, 0, dims), (k, 0, dims)], [right, left], found)
            if last_round:
                found, all_last = tie((found, all_last))
            else:
                *after, found, xw, all_far, all_near = tie((*after, found, xw, all_far, all_near))
            right, left = after
        last = [right, left]
        last_pieces = [(-(n // 2), 0, dims), (n // 2, half, dims)]
    else:
        x_last = swap(x_far, 1)
        xw = project([fact_x, x_near, x_far, x_last])
        all_far, all_near = swap(weights, 2), swap(weights, 1)
        all_last = swap(all_far, 1)
        whole = lax.all_gather(dim_table, "fact")
        order = jnp.take(whole, ring_at(ring_place(lax.axis_index("fact"), n) + jnp.arange(n), n), axis=0)
        for k in range(0, n, 8):
            found = look([(k + i, 0, dims) for i in range(8)], [order[k + i] for i in range(8)], found)
        last, last_pieces = [], []
    x_blocks, all_blocks = [fact_x, x_near, x_far, x_last], [weights, all_near, all_far, all_last]
    asked = lax.all_to_all(asks, "fact", 0, 0)
    last_rows = max(LANES, sum(t.shape[0] for t in last))
    slope, part = call(
        functools.partial(message_kernel, n, last_pieces),
        (shape((facts, LANES), F32), shape((n * ents, LANES), BF)),
        [
            pltpu.VMEM((step, last_rows), BF),
            pltpu.VMEM((facts, LANES), BF),
            pltpu.VMEM((LANES, facts), BF),
            pltpu.VMEM((16, facts), BF),
        ],
        2 * facts * (last_rows + n * ents) * LANES,
        "message",
        limit,
    )(dlow, dhigh, *last, found, xw, entity)
    sums = lax.all_to_all(part.reshape(n * m, rows_each, LANES), ("fact", "feat"), 0, 0)
    asked, pos, entity, _ = tie((asked, pos, entity, part))
    hidden, divisor, x_turned = call(
        functools.partial(ready_kernel, m, width, ents),
        (
            shape((m, ents, LANES), BF),
            shape((rows_each, LANES), F32),
            shape((width, facts), BF),
        ),
        [pltpu.VMEM((ents, LANES), F32)],
        1 << 28,
        "ready",
    )(asked, *x_blocks, *all_blocks)
    by_feat = shape((m, rows_each, LANES), BF)
    back, out_parts, pre_parts, agg_parts = call(
        functools.partial(entity_kernel, n, m, width, ents),
        (shape((n * m, rows_each, LANES), BF), by_feat, by_feat, shape((m * rows_each, LANES), BF)),
        [pltpu.VMEM((m, rows_each, LANES), BF)],
        6 * rows_each * width * width,
        "entity",
    )(sums, divisor, *all_blocks)
    scaled = lax.all_to_all(back, ("fact", "feat"), 0, 0).reshape(n * ents, LANES)
    shares = call(
        functools.partial(share_kernel, m),
        tuple(shape(((2 + m) * rows_each, LANES), BF) for _ in range(m)),
        [],
        1 << 20,
        "share",
    )(out_parts, pre_parts, agg_parts)
    got = [shares[0]] + [swap(shares[j], j) for j in range(1, m)]
    pos, entity, asked, _ = tie((pos, entity, asked, back))
    plow, phigh, elow, ehigh = call(
        codes_kernel,
        (shape((LANES, facts), BF), shape((16, facts), BF), columns, columns),
        [],
        1 << 26,
        "codes",
    )(pos, entity)
    rlow, rhigh = call(
        functools.partial(request_kernel, n, cap),
        (shape((LANES, slots), BF), shape((16, slots), BF)),
        [],
        1 << 26,
        "requests",
        limit,
    )(asked)
    pair_shape = (n // 2, 2 * stride, LANES)
    output_h, pair = call(
        functools.partial(weight_kernel, n, m, width, stride),
        (shape((ents, LANES), BF), shape((2, *pair_shape), F32)),
        [pltpu.VMEM((width, LANES), F32), pltpu.VMEM((ents, LANES), BF), pltpu.VMEM((m, ents, LANES), BF)],
        4 * ents * width * LANES,
        "weight",
    )(hidden, *got)
    if ringed:
        keep, give = call(halves_kernel, (shape(pair_shape, F32), shape(pair_shape, BF)), [], 1 << 20, "halves")(pair)
        pairs = [keep, lax.ppermute(give, "fact", [(i, i ^ 1) for i in range(n)])]
        elow, pairs = tie((elow, pairs))
    else:
        pairs = [jnp.stack([pair[0], pair[1]], axis=1).reshape(n, 2 * stride, LANES)]
    d_msg, msg_share = call(
        functools.partial(backward_kernel, n, stride),
        (columns, shape((n, stride, LANES), BF)),
        [pltpu.VMEM((step, n * ents), BF)],
        2 * facts * (n * ents + width) * LANES,
        "backward",
        limit,
    )(scaled, slope, elow, ehigh, x_turned)

    def spread(offsets):
        lengths = [cap + (3 if ringed and k % 2 == 0 else 1) * stride for k in offsets]
        return call(
            functools.partial(spread_kernel, n, cap, stride, offsets),
            tuple(shape((rows, LANES), BF) for rows in lengths),
            [],
            2 * facts * cap * LANES * len(offsets),
            "spread",
            limit,
        )(plow, phigh, d_msg, msg_share, *(pairs if ringed else ()))

    def add_up(offsets, got, base):
        return call(
            functools.partial(table_kernel, n, cap, stride, offsets, base is None),
            (shape((dims, LANES), F32), shape((3 * stride, LANES), F32)),
            [
                pltpu.VMEM((cap * len(got), LANES), BF),
                pltpu.VMEM((LANES, cap * len(got)), BF),
                pltpu.VMEM((16, cap * len(got)), BF),
            ],
            2 * cap * dims * LANES * len(got),
            "table",
            limit,
        )(rlow, rhigh, *got, *(base or ()))

    totals = None
    if ringed:
        messages = {}
        for offsets in [[n // 2], [1, n - 1]] + [[k, n - k] for k in range(n // 2 - 1, 1, -1)]:
            for offset, message in zip(offsets, spread(offsets)):
                messages[offset] = lax.ppermute(message, "fact", [(i, (i + offset) % n) for i in range(n)])
        messages[0] = spread([0])[0]
        for offsets in [[0, 1, n - 1], [n // 2]] + [[k, n - k] for k in range(n // 2 - 1, 1, -1)]:
            totals = add_up(offsets, [messages[k] for k in offsets], totals)
        grad_dim, weight = totals
    else:
        fact_me = lax.axis_index("fact")
        sent = [message for k in range(0, n, 8) for message in spread(list(range(k, k + 8)))]
        by_owner = jnp.take(jnp.stack(sent), lax.rem(jnp.arange(n) - fact_me + n, n), axis=0)
        owned = lax.all_to_all(by_owner, "fact", 0, 0)
        by_offset = jnp.take(owned, lax.rem(fact_me - jnp.arange(n) + n, n), axis=0)
        for k in range(0, n, 8):
            totals = add_up(list(range(k, k + 8)), [by_offset[k + i] for i in range(8)], totals)
        grad_dim, weight = totals
        pair_sum = lax.psum_scatter(pairs[0], "fact", scatter_dimension=0, tiled=True)[0]
        weight = weight + jnp.concatenate([jnp.zeros((stride, LANES), F32), pair_sum], axis=0)
    return (
        output_h,
        weight[0:own],
        weight[stride : stride + own],
        weight[2 * stride : 2 * stride + own],
        grad_dim,
    )


def solution(mesh):
    placed = (
        P("fact", "feat"),
        P("fact", None),
        P("fact"),
        P("fact", None),
        P("fact"),
        P("fact", "feat"),
        P("fact", "feat"),
        P(None, "feat"),
        P(None, "feat"),
        P(None, "feat"),
        P("fact", "feat"),
    )
    return jax.shard_map(
        shards,
        mesh=mesh,
        in_specs=placed,
        out_specs=(P("fact", "feat"),) * 5,
        check_vma=False,
    )
```

profile of v0, /device:TPU:4, one launch (start us, length us, event | category | flops | bytes accessed | tf_op | source)
XLA Modules:
  0.0 115.0 jit_solution(13931827044759311409)
XLA Ops:
  0.7 2.0 %collective-permute-start.1 = (bf16[1024,128]{1,0:T(8,128)(2,1)}, bf16[1024,128]{1,0:T(8,128)(2,1)S(1)}, u32[]{:S(2)}, u32[]{:S(2)}) collective-permute-start(bf16[1024,128]{1,0:T(8,128)(2,1)} %refs_0_.3), channel_id=1, source_target_pairs={{8,0},{16,8},{24,16},{28,24},{20,28},{12,20},{4,12},{0,4},{9,1},{1... | collective-permute-start | bytes 786440 | tf_op jit(solution)/shard_map/ppermute | solution.py:386
  6.3 1.7 %route.1 = (s32[8,4,128]{2,1,0:T(4,128)}, s32[8,128]{1,0:T(8,128)S(1)}, s32[8,128]{1,0:T(8,128)S(1)}, bf16[1024,128]{1,0:T(8,128)(2,1)S(1)}, bf16[1024,128]{1,0:T(8,128)(2,1)S(1)}) custom-call(s32[8,128]{1,0:T(8,128)S(1)} %bitcast.7, s32[8,128]{1,0:T(8,128)S(1)} %bitcast.8, s32[8,128]{1,0:T(8,128)S(1)} %bitcast.9, s32[8,128]{1,0:T(8,128)S(1)} %bitcast.10), custom_call_target="tpu_custom_call" | custom-call | flops 268435456 | bytes 1048576 | tf_op jit(solution)/shard_map/route/pallas_call | solution.py:397
  9.0 2.6 %collective-permute-done.2.refs_2_ = bf16[1024,128]{1,0:T(8,128)(2,1)S(1)} collective-permute-done((bf16[1024,128]{1,0:T(8,128)(2,1)}, bf16[1024,128]{1,0:T(8,128)(2,1)S(1)}, u32[]{:S(2)}, u32[]{:S(2)}) %collective-permute-start.2) | collective-permute-done | bytes 262176 | tf_op jit(solution)/shard_map/ppermute | solution.py:389
  12.0 1.8 %collective-permute-start.5 = (bf16[1024,128]{1,0:T(8,128)(2,1)S(1)}, bf16[1024,128]{1,0:T(8,128)(2,1)S(1)}, u32[]{:S(2)}, u32[]{:S(2)}) collective-permute-start(bf16[1024,128]{1,0:T(8,128)(2,1)S(1)} %collective-permute-done.1.refs_2_), channel_id=1, source_target_pairs={{8,0},{16,8},{24,16},{28,24},{20,28},{12,20},{4,12},{0,4},{9,1},{1... | collective-permute-start | bytes 786440 | tf_op jit(solution)/shard_map/ppermute | solution.py:386
  14.8 2.6 %look.3.refs_2_ = f32[1024,128]{1,0:T(8,128)S(1)} custom-call(bf16[1024,128]{1,0:T(8,128)(2,1)S(1)} %get-tuple-element.88.low_ref, bf16[1024,128]{1,0:T(8,128)(2,1)S(1)} %get-tuple-element.89.high_ref, bf16[1024,128]{1,0:T(8,128)(2,1)S(1)} %copy-done.12, bf16[1024,128]{1,0:T(8,128)(2,1)S(1)} %collective-permute-done.refs_1_, ...), custom_call_target="tpu_custom_call" | custom-call | flops 805306368 | bytes 1048576 | tf_op jit(solution)/shard_map/look/pallas_call | solution.py:417
  17.4 2.3 %collective-permute-done.4.refs_0_ = bf16[1024,128]{1,0:T(8,128)(2,1)S(1)} collective-permute-done((bf16[1024,128]{1,0:T(8,128)(2,1)S(1)}, bf16[1024,128]{1,0:T(8,128)(2,1)S(1)}, u32[]{:S(2)}, u32[]{:S(2)}) %collective-permute-start.4) | collective-permute-done | bytes 262176 | tf_op jit(solution)/shard_map/ppermute | solution.py:386
  19.7 1.6 %collective-permute-start.9 = (bf16[1280,128]{1,0:T(8,128)(2,1)S(1)}, bf16[1280,128]{1,0:T(8,128)(2,1)S(1)}, u32[]{:S(2)}, u32[]{:S(2)}) collective-permute-start(bf16[1280,128]{1,0:T(8,128)(2,1)S(1)} %pad_maximum_fusion.refs_4_.refs_0_), channel_id=1, source_target_pairs={{0,2},{1,3},{2,0},{3,1},{4,6},{5,7},{6,4},{7,5},{8,10},{9,11},{10,... | collective-permute-start | bytes 983048 | tf_op jit(solution)/shard_map/ppermute | solution.py:389
  24.6 1.8 %look.4.refs_2_ = f32[1024,128]{1,0:T(8,128)S(1)} custom-call(bf16[1024,128]{1,0:T(8,128)(2,1)S(1)} %get-tuple-element.88.low_ref, bf16[1024,128]{1,0:T(8,128)(2,1)S(1)} %get-tuple-element.89.high_ref, bf16[1024,128]{1,0:T(8,128)(2,1)S(1)} %collective-permute-done.4.refs_0_, bf16[1024,128]{1,0:T(8,128)(2,1)S(1)} %collective-permute-done.5.refs_1_, ...), custom_call_target="tpu_custom_call" | custom-call | flops 536870912 | bytes 1048576 | tf_op jit(solution)/shard_map/look/pallas_call | solution.py:417
  26.4 3.5 %collective-permute-done.7.refs_0_ = bf16[1024,128]{1,0:T(8,128)(2,1)S(1)} collective-permute-done((bf16[1024,128]{1,0:T(8,128)(2,1)S(1)}, bf16[1024,128]{1,0:T(8,128)(2,1)S(1)}, u32[]{:S(2)}, u32[]{:S(2)}) %collective-permute-start.7) | collective-permute-done | bytes 262176 | tf_op jit(solution)/shard_map/ppermute | solution.py:386
  34.5 5.4 %all-to-all-start = ((s32[8,4,128]{2,1,0:T(4,128)}), s32[8,4,128]{2,1,0:T(4,128)S(1)}, u32[]{:S(2)}, u32[]{:S(2)}) async-start(s32[8,4,128]{2,1,0:T(4,128)} %get-tuple-element.85), calls=%async_computation | async-start | bytes 32768 | tf_op jit(solution)/shard_map/all_to_all | solution.py:467
  39.9 1.8 %look.5.refs_2_ = f32[1024,128]{1,0:T(8,128)S(1)} custom-call(bf16[1024,128]{1,0:T(8,128)(2,1)S(1)} %get-tuple-element.88.low_ref, bf16[1024,128]{1,0:T(8,128)(2,1)S(1)} %get-tuple-element.89.high_ref, bf16[1024,128]{1,0:T(8,128)(2,1)S(1)} %collective-permute-done.7.refs_0_, bf16[1024,128]{1,0:T(8,128)(2,1)S(1)} %collective-permute-done.8.refs_1_, ...), custom_call_target="tpu_custom_call" | custom-call | flops 536870912 | bytes 1048576 | tf_op jit(solution)/shard_map/look/pallas_call | solution.py:417
  41.7 3.8 %message.1 = (f32[1024,128]{1,0:T(8,128)S(1)}, bf16[1024,128]{1,0:T(8,128)(2,1)}) custom-call(bf16[1024,128]{1,0:T(8,128)(2,1)S(1)} %get-tuple-element.88.low_ref, bf16[1024,128]{1,0:T(8,128)(2,1)S(1)} %get-tuple-element.89.high_ref, bf16[512,128]{1,0:T(8,128)(2,1)S(1)} %collective-permute-done.11.refs_0_, bf16[512,128]{1,0:T(8,128)(2,1)} %collective-permute-done.12.refs_1_, ...), custom_call_target="tpu_custom_call" | custom-call | flops 536870912 | bytes 1048576 | tf_op jit(solution)/shard_map/message/pallas_call | solution.py:469
  46.3 5.7 %all-to-all-start.1 = ((bf16[32,32,128]{2,1,0:T(8,128)(2,1)}), bf16[32,32,128]{2,1,0:T(8,128)(2,1)S(1)}, u32[]{:S(2)}, u32[]{:S(2)}) async-start(bf16[32,32,128]{2,1,0:T(8,128)(2,1)} %bitcast.4), calls=%async_computation.1 | async-start | bytes 524288 | tf_op jit(solution)/shard_map/all_to_all | solution.py:482
  53.9 7.8 %all-to-all-done.1.sums_ref = bf16[32,32,128]{2,1,0:T(8,128)(2,1)S(1)} async-done(((bf16[32,32,128]{2,1,0:T(8,128)(2,1)}), bf16[32,32,128]{2,1,0:T(8,128)(2,1)S(1)}, u32[]{:S(2)}, u32[]{:S(2)}) %all-to-all-start.1) | async-done | bytes 262176 | tf_op jit(solution)/shard_map/all_to_all | solution.py:482
  63.9 3.4 %all-to-all-start.2 = ((bf16[32,32,128]{2,1,0:T(8,128)(2,1)}), bf16[32,32,128]{2,1,0:T(8,128)(2,1)S(1)}, u32[]{:S(2)}, u32[]{:S(2)}) async-start(bf16[32,32,128]{2,1,0:T(8,128)(2,1)} %get-tuple-element.121), calls=%async_computation.2 | async-start | bytes 524288 | tf_op jit(solution)/shard_map/all_to_all | solution.py:503
  69.2 4.1 %collective-permute-done.15.refs_2_ = bf16[192,128]{1,0:T(8,128)(2,1)S(1)} collective-permute-done((bf16[192,128]{1,0:T(8,128)(2,1)S(1)}, bf16[192,128]{1,0:T(8,128)(2,1)S(1)}, u32[]{:S(2)}, u32[]{:S(2)}) %collective-permute-start.15) | collective-permute-done | bytes 49184 | tf_op jit(solution)/shard_map/ppermute | solution.py:389
  75.6 4.9 %collective-permute-done.17.refs_1_ = bf16[4,128,128]{2,1,0:T(8,128)(2,1)S(1)} collective-permute-done((bf16[4,128,128]{2,1,0:T(8,128)(2,1)S(1)}, bf16[4,128,128]{2,1,0:T(8,128)(2,1)S(1)}, u32[]{:S(2)}, u32[]{:S(2)}) %collective-permute-start.17) | collective-permute-done | bytes 131104 | tf_op jit(solution)/shard_map/ppermute | solution.py:538
  80.6 1.7 %backward.1 = (bf16[1024,128]{1,0:T(8,128)(2,1)S(1)}, bf16[8,64,128]{2,1,0:T(8,128)(2,1)S(1)}) custom-call(bf16[1024,128]{1,0:T(8,128)(2,1)S(1)} %bitcast.6, f32[1024,128]{1,0:T(8,128)S(1)} %copy-done.8, bf16[1024,128]{1,0:T(8,128)(2,1)S(1)} %get-tuple-element.134.low_ref, bf16[1024,128]{1,0:T(8,128)(2,1)S(1)} %get-tuple-element.135.high_ref, ...), custom_call_target="tpu_custom_call" | custom-call | flops 402653184 | bytes 1048576 | tf_op jit(solution)/shard_map/backward/pallas_call | solution.py:542
  85.3 2.9 %collective-permute-start.22 = (bf16[576,128]{1,0:T(8,128)(2,1)S(1)}, bf16[576,128]{1,0:T(8,128)(2,1)S(1)}, u32[]{:S(2)}, u32[]{:S(2)}) collective-permute-start(bf16[576,128]{1,0:T(8,128)(2,1)S(1)} %spread.7), channel_id=1, source_target_pairs={{0,16},{4,20},{8,24},{12,28},{16,0},{20,4},{24,8},{28,12},{1,17},{... | collective-permute-start | bytes 442376 | tf_op jit(solution)/shard_map/ppermute | solution.py:581
  90.5 2.2 %collective-permute-start.19 = (bf16[576,128]{1,0:T(8,128)(2,1)S(1)}, bf16[576,128]{1,0:T(8,128)(2,1)S(1)}, u32[]{:S(2)}, u32[]{:S(2)}) collective-permute-start(bf16[576,128]{1,0:T(8,128)(2,1)S(1)} %get-tuple-element.142), channel_id=1, source_target_pairs={{0,24},{4,28},{8,0},{12,4},{16,8},{20,12},{24,16},{28,20},{1,25},{... | collective-permute-start | bytes 442376 | tf_op jit(solution)/shard_map/ppermute | solution.py:581
  94.5 3.6 %collective-permute-start.21 = (bf16[448,128]{1,0:T(8,128)(2,1)S(1)}, bf16[448,128]{1,0:T(8,128)(2,1)S(1)}, u32[]{:S(2)}, u32[]{:S(2)}) collective-permute-start(bf16[448,128]{1,0:T(8,128)(2,1)S(1)} %get-tuple-element.144), channel_id=1, source_target_pairs={{0,20},{4,24},{8,28},{12,0},{16,4},{20,8},{24,12},{28,16},{1,21},{... | collective-permute-start | bytes 344072 | tf_op jit(solution)/shard_map/ppermute | solution.py:581
  101.6 3.7 %collective-permute-done.20.refs_0_ = bf16[448,128]{1,0:T(8,128)(2,1)S(1)} collective-permute-done((bf16[448,128]{1,0:T(8,128)(2,1)S(1)}, bf16[448,128]{1,0:T(8,128)(2,1)S(1)}, u32[]{:S(2)}, u32[]{:S(2)}) %collective-permute-start.20) | collective-permute-done | bytes 114720 | tf_op jit(solution)/shard_map/ppermute | solution.py:581
  105.3 6.1 %collective-permute-done.21.refs_1_ = bf16[448,128]{1,0:T(8,128)(2,1)S(1)} collective-permute-done((bf16[448,128]{1,0:T(8,128)(2,1)S(1)}, bf16[448,128]{1,0:T(8,128)(2,1)S(1)}, u32[]{:S(2)}, u32[]{:S(2)}) %collective-permute-start.21) | collective-permute-done | bytes 114720 | tf_op jit(solution)/shard_map/ppermute | solution.py:581
  112.5 1.8 %table.7 = (f32[1024,128]{1,0:T(8,128)}, f32[192,128]{1,0:T(8,128)S(1)}) custom-call(bf16[128,3072]{1,0:T(8,128)(2,1)S(1)} %get-tuple-element.123.low_ref, bf16[16,3072]{1,0:T(8,128)(2,1)S(1)} %get-tuple-element.124.high_ref, bf16[576,128]{1,0:T(8,128)(2,1)S(1)} %collective-permute-done.18.refs_0_, bf16[576,128]{1,0:T(8,128)(2,1)S(1)} %collective-permute-done.19.refs_1_, ...), custom_call_target="tpu_custom_call" | custom-call | flops 201326592 | bytes 1048576 | tf_op jit(solution)/shard_map/table/pallas_call | solution.py:563
  (112 shorter events, 35.1 us)
Async XLA Ops:
  0.6 8.3 %collective-permute-start = (bf16[1024,128]{1,0:T(8,128)(2,1)}, bf16[1024,128]{1,0:T(8,128)(2,1)S(1)}, u32[]{:S(2)}, u32[]{:S(2)}) collective-permute-start(bf16[1024,128]{1,0:T(8,128)(2,1)} %refs_0_.3), channel_id=1, source_target_pairs={{0,8},{8,16},{16,24},{24,28},{28,20},{20,12},{12,4},{4,0},{1,9},{9... | collective-permute-start | bytes 786440 | tf_op jit(solution)/shard_map/ppermute | solution.py:386
  0.7 8.3 %collective-permute-start.1 = (bf16[1024,128]{1,0:T(8,128)(2,1)}, bf16[1024,128]{1,0:T(8,128)(2,1)S(1)}, u32[]{:S(2)}, u32[]{:S(2)}) collective-permute-start(bf16[1024,128]{1,0:T(8,128)(2,1)} %refs_0_.3), channel_id=1, source_target_pairs={{8,0},{16,8},{24,16},{28,24},{20,28},{12,20},{4,12},{0,4},{9,1},{1... | collective-permute-start | bytes 786440 | tf_op jit(solution)/shard_map/ppermute | solution.py:386
  2.7 6.3 %collective-permute-start.3 = (bf16[1024,128]{1,0:T(8,128)(2,1)}, bf16[1024,128]{1,0:T(8,128)(2,1)S(1)}, u32[]{:S(2)}, u32[]{:S(2)}) collective-permute-start(bf16[1024,128]{1,0:T(8,128)(2,1)} %refs_0_.5), channel_id=1, source_target_pairs={{0,1},{1,0},{2,3},{3,2},{4,5},{5,4},{6,7},{7,6},{8,9},{9,8},{10,11... | collective-permute-start | bytes 786440 | tf_op jit(solution)/shard_map/ppermute | solution.py:389
  2.7 8.9 %collective-permute-start.2 = (bf16[1024,128]{1,0:T(8,128)(2,1)}, bf16[1024,128]{1,0:T(8,128)(2,1)S(1)}, u32[]{:S(2)}, u32[]{:S(2)}) collective-permute-start(bf16[1024,128]{1,0:T(8,128)(2,1)} %refs_0_.5), channel_id=1, source_target_pairs={{0,2},{1,3},{2,0},{3,1},{4,6},{5,7},{6,4},{7,5},{8,10},{9,11},{10,... | collective-permute-start | bytes 786440 | tf_op jit(solution)/shard_map/ppermute | solution.py:389
  11.7 8.0 %collective-permute-start.4 = (bf16[1024,128]{1,0:T(8,128)(2,1)S(1)}, bf16[1024,128]{1,0:T(8,128)(2,1)S(1)}, u32[]{:S(2)}, u32[]{:S(2)}) collective-permute-start(bf16[1024,128]{1,0:T(8,128)(2,1)S(1)} %collective-permute-done.refs_1_), channel_id=1, source_target_pairs={{0,8},{8,16},{16,24},{24,28},{28,20},{20,12},{12,4},{4,0},{1,9},{9... | collective-permute-start | bytes 786440 | tf_op jit(solution)/shard_map/ppermute | solution.py:386
  12.0 7.8 %collective-permute-start.5 = (bf16[1024,128]{1,0:T(8,128)(2,1)S(1)}, bf16[1024,128]{1,0:T(8,128)(2,1)S(1)}, u32[]{:S(2)}, u32[]{:S(2)}) collective-permute-start(bf16[1024,128]{1,0:T(8,128)(2,1)S(1)} %collective-permute-done.1.refs_2_), channel_id=1, source_target_pairs={{8,0},{16,8},{24,16},{28,24},{20,28},{12,20},{4,12},{0,4},{9,1},{1... | collective-permute-start | bytes 786440 | tf_op jit(solution)/shard_map/ppermute | solution.py:386
  13.7 6.0 %collective-permute-start.6 = (bf16[1024,128]{1,0:T(8,128)(2,1)S(1)}, bf16[1024,128]{1,0:T(8,128)(2,1)S(1)}, u32[]{:S(2)}, u32[]{:S(2)}) collective-permute-start(bf16[1024,128]{1,0:T(8,128)(2,1)S(1)} %collective-permute-done.2.refs_2_), channel_id=1, source_target_pairs={{0,1},{1,0},{2,3},{3,2},{4,5},{5,4},{6,7},{7,6},{8,9},{9,8},{10,11... | collective-permute-start | bytes 786440 | tf_op jit(solution)/shard_map/ppermute | solution.py:389
  19.7 11.4 %collective-permute-start.10 = (bf16[1280,128]{1,0:T(8,128)(2,1)S(1)}, bf16[1280,128]{1,0:T(8,128)(2,1)S(1)}, u32[]{:S(2)}, u32[]{:S(2)}) collective-permute-start(bf16[1280,128]{1,0:T(8,128)(2,1)S(1)} %pad_maximum_fusion.refs_4_.refs_0_), channel_id=1, source_target_pairs={{0,1},{1,0},{2,3},{3,2},{4,5},{5,4},{6,7},{7,6},{8,9},{9,8},{10,11... | collective-permute-start | bytes 983048 | tf_op jit(solution)/shard_map/ppermute | solution.py:389
  19.7 11.4 %collective-permute-start.9 = (bf16[1280,128]{1,0:T(8,128)(2,1)S(1)}, bf16[1280,128]{1,0:T(8,128)(2,1)S(1)}, u32[]{:S(2)}, u32[]{:S(2)}) collective-permute-start(bf16[1280,128]{1,0:T(8,128)(2,1)S(1)} %pad_maximum_fusion.refs_4_.refs_0_), channel_id=1, source_target_pairs={{0,2},{1,3},{2,0},{3,1},{4,6},{5,7},{6,4},{7,5},{8,10},{9,11},{10,... | collective-permute-start | bytes 983048 | tf_op jit(solution)/shard_map/ppermute | solution.py:389
  21.4 8.4 %collective-permute-start.7 = (bf16[1024,128]{1,0:T(8,128)(2,1)S(1)}, bf16[1024,128]{1,0:T(8,128)(2,1)S(1)}, u32[]{:S(2)}, u32[]{:S(2)}) collective-permute-start(bf16[1024,128]{1,0:T(8,128)(2,1)S(1)} %collective-permute-done.4.refs_0_), channel_id=1, source_target_pairs={{0,8},{8,16},{16,24},{24,28},{28,20},{20,12},{12,4},{4,0},{1,9},{9... | collective-permute-start | bytes 786440 | tf_op jit(solution)/shard_map/ppermute | solution.py:386
  23.0 8.2 %collective-permute-start.8 = (bf16[1024,128]{1,0:T(8,128)(2,1)S(1)}, bf16[1024,128]{1,0:T(8,128)(2,1)S(1)}, u32[]{:S(2)}, u32[]{:S(2)}) collective-permute-start(bf16[1024,128]{1,0:T(8,128)(2,1)S(1)} %collective-permute-done.5.refs_1_), channel_id=1, source_target_pairs={{8,0},{16,8},{24,16},{28,24},{20,28},{12,20},{4,12},{0,4},{9,1},{1... | collective-permute-start | bytes 786440 | tf_op jit(solution)/shard_map/ppermute | solution.py:386
  31.1 10.5 %collective-permute-start.13 = (bf16[1280,128]{1,0:T(8,128)(2,1)S(1)}, bf16[1280,128]{1,0:T(8,128)(2,1)S(1)}, u32[]{:S(2)}, u32[]{:S(2)}) collective-permute-start(bf16[1280,128]{1,0:T(8,128)(2,1)S(1)} %collective-permute-done.9.refs_6_.refs_2_), channel_id=1, source_target_pairs={{0,1},{1,0},{2,3},{3,2},{4,5},{5,4},{6,7},{7,6},{8,9},{9,8},{10,11... | collective-permute-start | bytes 983048 | tf_op jit(solution)/shard_map/ppermute | solution.py:389
  32.4 9.2 %collective-permute-start.11 = (bf16[512,128]{1,0:T(8,128)(2,1)}, bf16[512,128]{1,0:T(8,128)(2,1)S(1)}, u32[]{:S(2)}, u32[]{:S(2)}) collective-permute-start(bf16[512,128]{1,0:T(8,128)(2,1)} %slice.15), channel_id=1, source_target_pairs={{0,8},{8,16},{16,24},{24,28},{28,20},{20,12},{12,4},{4,0},{1,9},{9... | collective-permute-start | bytes 393224 | tf_op jit(solution)/shard_map/ppermute | solution.py:386
  34.0 7.6 %collective-permute-start.12 = (bf16[512,128]{1,0:T(8,128)(2,1)}, bf16[512,128]{1,0:T(8,128)(2,1)}, u32[]{:S(2)}, u32[]{:S(2)}) collective-permute-start(bf16[512,128]{1,0:T(8,128)(2,1)} %slice.16), channel_id=1, source_target_pairs={{8,0},{16,8},{24,16},{28,24},{20,28},{12,20},{4,12},{0,4},{9,1},{1... | collective-permute-start | bytes 393224 | tf_op jit(solution)/shard_map/ppermute | solution.py:386
  34.5 11.8 %all-to-all-start = ((s32[8,4,128]{2,1,0:T(4,128)}), s32[8,4,128]{2,1,0:T(4,128)S(1)}, u32[]{:S(2)}, u32[]{:S(2)}) async-start(s32[8,4,128]{2,1,0:T(4,128)} %get-tuple-element.85), calls=%async_computation | async-start | bytes 32768 | tf_op jit(solution)/shard_map/all_to_all | solution.py:467
  46.3 15.4 %all-to-all-start.1 = ((bf16[32,32,128]{2,1,0:T(8,128)(2,1)}), bf16[32,32,128]{2,1,0:T(8,128)(2,1)S(1)}, u32[]{:S(2)}, u32[]{:S(2)}) async-start(bf16[32,32,128]{2,1,0:T(8,128)(2,1)} %bitcast.4), calls=%async_computation.1 | async-start | bytes 524288 | tf_op jit(solution)/shard_map/all_to_all | solution.py:482
  63.9 16.7 %all-to-all-start.2 = ((bf16[32,32,128]{2,1,0:T(8,128)(2,1)}), bf16[32,32,128]{2,1,0:T(8,128)(2,1)S(1)}, u32[]{:S(2)}, u32[]{:S(2)}) async-start(bf16[32,32,128]{2,1,0:T(8,128)(2,1)} %get-tuple-element.121), calls=%async_computation.2 | async-start | bytes 524288 | tf_op jit(solution)/shard_map/all_to_all | solution.py:503
  82.9 10.4 %collective-permute-start.23 = (bf16[448,128]{1,0:T(8,128)(2,1)S(1)}, bf16[448,128]{1,0:T(8,128)(2,1)S(1)}, u32[]{:S(2)}, u32[]{:S(2)}) collective-permute-start(bf16[448,128]{1,0:T(8,128)(2,1)S(1)} %get-tuple-element.145), channel_id=1, source_target_pairs={{0,4},{4,8},{8,12},{12,16},{16,20},{20,24},{24,28},{28,0},{1,5},{5... | collective-permute-start | bytes 344072 | tf_op jit(solution)/shard_map/ppermute | solution.py:581
  84.3 10.2 %collective-permute-start.24 = (bf16[448,128]{1,0:T(8,128)(2,1)S(1)}, bf16[448,128]{1,0:T(8,128)(2,1)S(1)}, u32[]{:S(2)}, u32[]{:S(2)}) collective-permute-start(bf16[448,128]{1,0:T(8,128)(2,1)S(1)} %get-tuple-element.146), channel_id=1, source_target_pairs={{0,28},{4,0},{8,4},{12,8},{16,12},{20,16},{24,20},{28,24},{1,29},{... | collective-permute-start | bytes 344072 | tf_op jit(solution)/shard_map/ppermute | solution.py:581
  85.3 15.4 %collective-permute-start.22 = (bf16[576,128]{1,0:T(8,128)(2,1)S(1)}, bf16[576,128]{1,0:T(8,128)(2,1)S(1)}, u32[]{:S(2)}, u32[]{:S(2)}) collective-permute-start(bf16[576,128]{1,0:T(8,128)(2,1)S(1)} %spread.7), channel_id=1, source_target_pairs={{0,16},{4,20},{8,24},{12,28},{16,0},{20,4},{24,8},{28,12},{1,17},{... | collective-permute-start | bytes 442376 | tf_op jit(solution)/shard_map/ppermute | solution.py:581
  88.9 23.6 %collective-permute-start.18 = (bf16[576,128]{1,0:T(8,128)(2,1)S(1)}, bf16[576,128]{1,0:T(8,128)(2,1)S(1)}, u32[]{:S(2)}, u32[]{:S(2)}) collective-permute-start(bf16[576,128]{1,0:T(8,128)(2,1)S(1)} %get-tuple-element.141), channel_id=1, source_target_pairs={{0,8},{4,12},{8,16},{12,20},{16,24},{20,28},{24,0},{28,4},{1,9},{5... | collective-permute-start | bytes 442376 | tf_op jit(solution)/shard_map/ppermute | solution.py:581
  90.5 22.0 %collective-permute-start.19 = (bf16[576,128]{1,0:T(8,128)(2,1)S(1)}, bf16[576,128]{1,0:T(8,128)(2,1)S(1)}, u32[]{:S(2)}, u32[]{:S(2)}) collective-permute-start(bf16[576,128]{1,0:T(8,128)(2,1)S(1)} %get-tuple-element.142), channel_id=1, source_target_pairs={{0,24},{4,28},{8,0},{12,4},{16,8},{20,12},{24,16},{28,20},{1,25},{... | collective-permute-start | bytes 442376 | tf_op jit(solution)/shard_map/ppermute | solution.py:581
  93.3 11.9 %collective-permute-start.20 = (bf16[448,128]{1,0:T(8,128)(2,1)S(1)}, bf16[448,128]{1,0:T(8,128)(2,1)S(1)}, u32[]{:S(2)}, u32[]{:S(2)}) collective-permute-start(bf16[448,128]{1,0:T(8,128)(2,1)S(1)} %get-tuple-element.143), channel_id=1, source_target_pairs={{0,12},{4,16},{8,20},{12,24},{16,28},{20,0},{24,4},{28,8},{1,13},{... | collective-permute-start | bytes 344072 | tf_op jit(solution)/shard_map/ppermute | solution.py:581
  94.5 16.9 %collective-permute-start.21 = (bf16[448,128]{1,0:T(8,128)(2,1)S(1)}, bf16[448,128]{1,0:T(8,128)(2,1)S(1)}, u32[]{:S(2)}, u32[]{:S(2)}) collective-permute-start(bf16[448,128]{1,0:T(8,128)(2,1)S(1)} %get-tuple-element.144), channel_id=1, source_target_pairs={{0,20},{4,24},{8,28},{12,0},{16,4},{20,8},{24,12},{28,16},{1,21},{... | collective-permute-start | bytes 344072 | tf_op jit(solution)/shard_map/ppermute | solution.py:581
  (30 other events, 114.3 us)
where the time goes:
time: 116 us; the launch traced here: 115 us
  starting transfers between devices  41.9 us (36%)
  waiting for transfers between devices  38.8 us (33%)
  Pallas kernels  24.4 us (21%)
  local copies, waits for them, and re-layouts  8.83 us (8%)
    ppermute x7, starting transfers between devices, shards(): lax.ppermute(message, 'fact', [(i, (i + offset) % n) for i in range(n)])  13.7 us
    ppermute x7, waiting for transfers between devices, shards(): lax.ppermute(message, 'fact', [(i, (i + offset) % n) for i in range(n)])  10.6 us
    all_to_all x1, waiting for transfers between devices, shards(): lax.all_to_all(part.reshape(n * m, rows_each, LANES), ('fact', 'feat'), 0...  7.78 us
    ppermute x9, waiting for transfers between devices, swap(): return lax.ppermute(block, 'feat', [(i, i ^ bit) for i in range(m)])  7.33 us
    unnamed x52, local copies, waits for them, and re-layouts  6.83 us
    ppermute x4, waiting for transfers between devices, pass_on(): lax.ppermute(right, 'fact', to_right)  6.69 us
    pallas_call x3, Pallas kernels, look(): call(functools.partial(look_kernel, n, pieces), shape((facts, LANES), F32...  6.16 us
    all_to_all x1, starting transfers between devices, shards(): lax.all_to_all(part.reshape(n * m, rows_each, LANES), ('fact', 'feat'), 0...  5.66 us
  transfers between devices with their start and end apart: 28, of which 14 were waited for; matrix products, arithmetic and copies ran while one was open for 1% of the time, Pallas kernels for 16%

commit v1 on v0

--- a/solution.py
+++ b/solution.py
@@ -14,7 +14,7 @@
 VMEM_LIMIT_LARGE = 40 * 1024 * 1024
 
 
-def call(kernel, out_shape, scratch, flops, name, limit=VMEM_LIMIT):
+def call(kernel, out_shape, scratch, flops, name, limit=VMEM_LIMIT, **specs):
     return pl.pallas_call(
         kernel,
         out_shape=out_shape,
@@ -22,6 +22,7 @@
         compiler_params=pltpu.CompilerParams(vmem_limit_bytes=limit),
         cost_estimate=pl.CostEstimate(flops=flops, bytes_accessed=1 << 20, transcendentals=0),
         name=name,
+        **specs,
     )
 
 
@@ -152,7 +153,7 @@
 def message_kernel(n, pieces, low_ref, high_ref, *refs):
     count = len(pieces)
     tables, refs = refs[:count], refs[count:]
-    base_ref, xw_ref, ent_ref, slope_ref, part_ref, hot_ref, msg_ref, erlow_ref, erhigh_ref = refs
+    base_ref, xw_ref, ent_ref, slope_out, part_ref, slope_ref, hot_ref, msg_ref, erlow_ref, erhigh_ref, sem = refs
     facts = low_ref.shape[0]
     step = hot_ref.shape[0]
     place = ring_place(lax.axis_index("fact"), n)
@@ -168,6 +169,8 @@
         gate = jax.nn.sigmoid(pre)
         msg_ref[rows, :] = (pre * gate).astype(BF)
         slope_ref[rows, :] = gate * (1.0 + pre * (1.0 - gate))
+    keep = pltpu.make_async_copy(slope_ref, slope_out, sem)
+    keep.start()
 
     def add(pair, carry):
         hot = jnp.concatenate(
@@ -178,6 +181,7 @@
         return carry
 
     lax.fori_loop(0, part_ref.shape[0] // 256, add, 0)
+    keep.wait()
 
 
 def project_kernel(m, w_ref, *refs):
@@ -191,23 +195,21 @@
     out_ref[...] = total
 
 
-def ready_kernel(m, width, ents, idx_ref, *refs):
-    x_refs, all_refs, (hidden_ref, div_ref, xt_ref, hold_ref) = refs[:m], refs[m : 2 * m], refs[2 * m :]
+def ready_kernel(m, width, ents, *refs):
+    x_refs, all_refs, (hidden_ref, xt_ref) = refs[:m], refs[m : 2 * m], refs[2 * m :]
+    me = lax.axis_index("feat")
+    for j in range(m):
+        hidden_ref[me ^ j] = all_refs[j][2 * width : 2 * width + ents, :]
+        xt_ref[pl.ds(pl.multiple_of((me ^ j) * LANES, LANES), LANES), :] = x_refs[j][...].T
+
+
+def entity_kernel(n, m, width, ents, sums_ref, idx_ref, *refs):
+    all_refs, (back_ref, out_ref, pre_ref, agg_ref, own_ref, hold_ref) = refs[:m], refs[m:]
     rows_each = ents // m
     me = lax.axis_index("feat")
     hits = jnp.sum(idx_ref[:, idx_ref.shape[1] - 1, :], axis=0, keepdims=True).astype(F32)
     hold_ref[...] = jnp.maximum(jnp.broadcast_to(hits, (LANES, ents)).T, 1.0)
-    div_ref[...] = hold_ref[pl.ds(pl.multiple_of(me * rows_each, rows_each), rows_each), :]
-    for j in range(m):
-        hidden_ref[me ^ j] = all_refs[j][2 * width : 2 * width + ents, :]
-        xt_ref[pl.ds(pl.multiple_of((me ^ j) * LANES, LANES), LANES), :] = x_refs[j][...].T
-
-
-def entity_kernel(n, m, width, ents, sums_ref, div_ref, *refs):
-    all_refs, (back_ref, out_ref, pre_ref, agg_ref, own_ref) = refs[:m], refs[m:]
-    rows_each = ents // m
-    me = lax.axis_index("feat")
-    divisor = div_ref[...]
+    divisor = hold_ref[pl.ds(pl.multiple_of(me * rows_each, rows_each), rows_each), :]
     for b in range(m):
         total = sums_ref[b].astype(F32)
         for f in range(1, n):
@@ -290,13 +292,17 @@
             low_ref[:, at : at + LANES], high_ref[:, at : at + LANES] = row_codes(req_ref[s, r : r + 1, :])
 
 
-def backward_kernel(n, stride, scaled_ref, slope_ref, low_ref, high_ref, xt_ref, dmsg_ref, share_ref, hot_ref):
+def backward_kernel(n, stride, slope_in, scaled_ref, low_ref, high_ref, xt_ref, dmsg_ref, share_ref, hot_ref, slope_ref, sem):
+    fetch = pltpu.make_async_copy(slope_in, slope_ref, sem)
+    fetch.start()
     facts = slope_ref.shape[0]
     own = xt_ref.shape[0] // n
     step = hot_ref.shape[0]
     for c in range(facts // step):
         rows = slice(c * step, (c + 1) * step)
         found = gather_rows(low_ref, high_ref, rows, [scaled_ref], [jnp.int32(0)], hot_ref)
+        if c == 0:
+            fetch.wait()
         dmsg_ref[rows, :] = (found * slope_ref[rows, :]).astype(BF)
     total = dot(xt_ref[...], dmsg_ref[...])
     for d in range(n):
@@ -324,12 +330,14 @@
             out_ref[cap + stride :, :] = pair.astype(BF)
 
 
-def table_kernel(n, cap, stride, offsets, first, low_ref, high_ref, *refs):
+def table_kernel(n, cap, stride, offsets, first, final, low_ref, high_ref, *refs):
     count = len(offsets)
     got, refs = refs[:count], refs[count:]
     if not first:
         (base_ref, weight_base_ref), refs = refs[:2], refs[2:]
-    out_ref, weight_ref, rows_ref, klow_ref, khigh_ref = refs
+    out_ref, refs = refs[0], refs[1:]
+    final_refs, refs = (refs[:3], refs[3:]) if final else ((), refs[1:] + refs[:1])
+    rows_ref, klow_ref, khigh_ref, weight_ref = refs
     me = lax.axis_index("fact")
     if first:
         weight_ref[...] = jnp.zeros(weight_ref.shape, F32)
@@ -344,6 +352,8 @@
         khigh_ref[:, here] = high_ref[:, there]
         rows = ref.shape[0] - cap
         weight_ref[0:rows, :] += ref[cap:, :].astype(F32)
+    for which, ref in enumerate(final_refs):
+        ref[...] = weight_ref[which * stride : which * stride + ref.shape[0], :]
     blocks = out_ref.shape[0] // LANES
     join = 2 if blocks % 2 == 0 else 1
 
@@ -390,7 +400,7 @@
 
     if ringed:
         right, left = pass_on(dim_table, dim_table)
-    x_far, x_near = swap(fact_x, 2), swap(fact_x, 1)
+    x_near = swap(fact_x, 1)
 
     by_lane = (chunks, LANES)
     columns = shape((facts, LANES), BF)
@@ -408,8 +418,8 @@
         "route",
     )(dim_owner.reshape(by_lane), dim_slot.reshape(by_lane), fact_owner.reshape(by_lane), fact_slot.reshape(by_lane))
     if ringed:
-        right, left, x_far, x_near, asks, pos, entity, dlow, dhigh = tie(
-            (right, left, x_far, x_near, asks, pos, entity, dlow, dhigh)
+        right, left, x_near, asks, pos, entity, dlow, dhigh = tie(
+            (right, left, x_near, asks, pos, entity, dlow, dhigh)
         )
 
     def look(pieces, tables, base):
@@ -431,38 +441,35 @@
     found = jnp.zeros((facts, LANES), F32)
     weights = jnp.concatenate([w_self, w_neigh, entity_h, cotangent], axis=0)
     if ringed:
-        half = dims // 2
         near = (right, left)
         after = pass_on(*near)
-        x_last = swap(x_far, 1)
+        x_far = swap(fact_x, 2)
         found = look([(0, 0, dims), (-1, 0, dims), (1, 0, dims)], [dim_table, *near], found)
-        right, left, x_last, found, weights = tie((*after, x_last, found, weights))
-        for k in range(2, n // 2):
-            last_round = k == n // 2 - 1
-            after = pass_on(right[:half], left[half:]) if last_round else pass_on(right, left)
-            if last_round:
-                all_last = swap(all_far, 1)
-            else:
-                all_far, all_near = swap(weights, 2), swap(weights, 1)
-                xw = project([fact_x, x_near, x_far, x_last])
+        right, left, x_far, found, weights = tie((*after, x_far, found, weights))
+        for k in range(2, n // 2 - 1):
+            after = pass_on(right, left)
+            x_last = swap(x_far, 1)
             found = look([(-k, 0, dims), (k, 0, dims)], [right, left], found)
-            if last_round:
-                found, all_last = tie((found, all_last))
-            else:
-                *after, found, xw, all_far, all_near = tie((*after, found, xw, all_far, all_near))
-            right, left = after
-        last = [right, left]
-        last_pieces = [(-(n // 2), 0, dims), (n // 2, half, dims)]
+            right, left, found, x_last = tie((*after, found, x_last))
+        all_far = swap(weights, 2)
+        k = n // 2 - 1
+        after = lax.ppermute(right, "fact", to_right)
+        xw = project([fact_x, x_near, x_far, x_last])
+        found = look([(-k, 0, dims), (k, 0, dims)], [right, left], found)
+        all_near = swap(weights, 1)
+        found, all_far, all_near = tie((found, all_far, all_near))
+        last, last_pieces = [after], [(n // 2, 0, dims)]
     else:
+        x_far = swap(fact_x, 2)
         x_last = swap(x_far, 1)
         xw = project([fact_x, x_near, x_far, x_last])
         all_far, all_near = swap(weights, 2), swap(weights, 1)
-        all_last = swap(all_far, 1)
         whole = lax.all_gather(dim_table, "fact")
         order = jnp.take(whole, ring_at(ring_place(lax.axis_index("fact"), n) + jnp.arange(n), n), axis=0)
         for k in range(0, n, 8):
             found = look([(k + i, 0, dims) for i in range(8)], [order[k + i] for i in range(8)], found)
         last, last_pieces = [], []
+    all_last = swap(all_far, 1)
     x_blocks, all_blocks = [fact_x, x_near, x_far, x_last], [weights, all_near, all_far, all_last]
     asked = lax.all_to_all(asks, "fact", 0, 0)
     last_rows = max(LANES, sum(t.shape[0] for t in last))
@@ -470,36 +477,35 @@
         functools.partial(message_kernel, n, last_pieces),
         (shape((facts, LANES), F32), shape((n * ents, LANES), BF)),
         [
+            pltpu.VMEM((facts, LANES), F32),
             pltpu.VMEM((step, last_rows), BF),
             pltpu.VMEM((facts, LANES), BF),
             pltpu.VMEM((LANES, facts), BF),
             pltpu.VMEM((16, facts), BF),
+            pltpu.SemaphoreType.DMA,
         ],
         2 * facts * (last_rows + n * ents) * LANES,
         "message",
         limit,
+        out_specs=(pl.BlockSpec(memory_space=pl.ANY), pl.BlockSpec(memory_space=pltpu.VMEM)),
     )(dlow, dhigh, *last, found, xw, entity)
     sums = lax.all_to_all(part.reshape(n * m, rows_each, LANES), ("fact", "feat"), 0, 0)
-    asked, pos, entity, _ = tie((asked, pos, entity, part))
-    hidden, divisor, x_turned = call(
+    pos, entity, x_blocks, _ = tie((pos, entity, x_blocks, part))
+    hidden, x_turned = call(
         functools.partial(ready_kernel, m, width, ents),
-        (
-            shape((m, ents, LANES), BF),
-            shape((rows_each, LANES), F32),
-            shape((width, facts), BF),
-        ),
-        [pltpu.VMEM((ents, LANES), F32)],
+        (shape((m, ents, LANES), BF), shape((width, facts), BF)),
+        [],
         1 << 28,
         "ready",
-    )(asked, *x_blocks, *all_blocks)
+    )(*x_blocks, *all_blocks)
     by_feat = shape((m, rows_each, LANES), BF)
     back, out_parts, pre_parts, agg_parts = call(
         functools.partial(entity_kernel, n, m, width, ents),
         (shape((n * m, rows_each, LANES), BF), by_feat, by_feat, shape((m * rows_each, LANES), BF)),
-        [pltpu.VMEM((m, rows_each, LANES), BF)],
+        [pltpu.VMEM((m, rows_each, LANES), BF), pltpu.VMEM((ents, LANES), F32)],
         6 * rows_each * width * width,
         "entity",
-    )(sums, divisor, *all_blocks)
+    )(sums, asked, *all_blocks)
     scaled = lax.all_to_all(back, ("fact", "feat"), 0, 0).reshape(n * ents, LANES)
     shares = call(
         functools.partial(share_kernel, m),
@@ -536,17 +542,17 @@
     if ringed:
         keep, give = call(halves_kernel, (shape(pair_shape, F32), shape(pair_shape, BF)), [], 1 << 20, "halves")(pair)
         pairs = [keep, lax.ppermute(give, "fact", [(i, i ^ 1) for i in range(n)])]
-        elow, pairs = tie((elow, pairs))
     else:
         pairs = [jnp.stack([pair[0], pair[1]], axis=1).reshape(n, 2 * stride, LANES)]
     d_msg, msg_share = call(
         functools.partial(backward_kernel, n, stride),
         (columns, shape((n, stride, LANES), BF)),
-        [pltpu.VMEM((step, n * ents), BF)],
+        [pltpu.VMEM((step, n * ents), BF), pltpu.VMEM((facts, LANES), F32), pltpu.SemaphoreType.DMA],
         2 * facts * (n * ents + width) * LANES,
         "backward",
         limit,
-    )(scaled, slope, elow, ehigh, x_turned)
+        in_specs=[pl.BlockSpec(memory_space=pl.ANY)] + [pl.BlockSpec(memory_space=pltpu.VMEM)] * 4,
+    )(slope, scaled, elow, ehigh, x_turned)
 
     def spread(offsets):
         lengths = [cap + (3 if ringed and k % 2 == 0 else 1) * stride for k in offsets]
@@ -559,15 +565,17 @@
             limit,
         )(plow, phigh, d_msg, msg_share, *(pairs if ringed else ()))
 
-    def add_up(offsets, got, base):
+    def add_up(offsets, got, base, final):
+        weight = shape((3 * stride, LANES), F32)
+        scratch = [
+            pltpu.VMEM((cap * len(got), LANES), BF),
+            pltpu.VMEM((LANES, cap * len(got)), BF),
+            pltpu.VMEM((16, cap * len(got)), BF),
+        ]
         return call(
-            functools.partial(table_kernel, n, cap, stride, offsets, base is None),
-            (shape((dims, LANES), F32), shape((3 * stride, LANES), F32)),
-            [
-                pltpu.VMEM((cap * len(got), LANES), BF),
-                pltpu.VMEM((LANES, cap * len(got)), BF),
-                pltpu.VMEM((16, cap * len(got)), BF),
-            ],
+            functools.partial(table_kernel, n, cap, stride, offsets, base is None, final),
+            (shape((dims, LANES), F32),) + ((shape((own, LANES), F32),) * 3 if final else (weight,)),
+            scratch + ([pltpu.VMEM(weight.shape, F32)] if final else []),
             2 * cap * dims * LANES * len(got),
             "table",
             limit,
@@ -576,13 +584,14 @@
     totals = None
     if ringed:
         messages = {}
-        for offsets in [[n // 2], [1, n - 1]] + [[k, n - k] for k in range(n // 2 - 1, 1, -1)]:
+        rest = [[k, n - k] for k in range(n // 2 - 1, 1, -1)]
+        for offsets in [rest[0], [n // 2], [1, n - 1], *rest[1:]]:
             for offset, message in zip(offsets, spread(offsets)):
                 messages[offset] = lax.ppermute(message, "fact", [(i, (i + offset) % n) for i in range(n)])
         messages[0] = spread([0])[0]
-        for offsets in [[0, 1, n - 1], [n // 2]] + [[k, n - k] for k in range(n // 2 - 1, 1, -1)]:
-            totals = add_up(offsets, [messages[k] for k in offsets], totals)
-        grad_dim, weight = totals
+        for offsets in [[0, 1, n - 1], [n // 2], *rest[::-1]]:
+            totals = add_up(offsets, [messages[k] for k in offsets], totals, offsets == rest[0])
+        grad_dim, grad_msg, grad_self, grad_neigh = totals
     else:
         fact_me = lax.axis_index("fact")
         sent = [message for k in range(0, n, 8) for message in spread(list(range(k, k + 8)))]
@@ -590,17 +599,11 @@
         owned = lax.all_to_all(by_owner, "fact", 0, 0)
         by_offset = jnp.take(owned, lax.rem(fact_me - jnp.arange(n) + n, n), axis=0)
         for k in range(0, n, 8):
-            totals = add_up(list(range(k, k + 8)), [by_offset[k + i] for i in range(8)], totals)
-        grad_dim, weight = totals
+            totals = add_up(list(range(k, k + 8)), [by_offset[k + i] for i in range(8)], totals, k + 8 >= n)
+        grad_dim, grad_msg, _, _ = totals
         pair_sum = lax.psum_scatter(pairs[0], "fact", scatter_dimension=0, tiled=True)[0]
-        weight = weight + jnp.concatenate([jnp.zeros((stride, LANES), F32), pair_sum], axis=0)
-    return (
-        output_h,
-        weight[0:own],
-        weight[stride : stride + own],
-        weight[2 * stride : 2 * stride + own],
-        grad_dim,
-    )
+        grad_self, grad_neigh = pair_sum[0:own], pair_sum[stride : stride + own]
+    return output_h, grad_msg, grad_self, grad_neigh, grad_dim
 
 
 def solution(mesh):

time: 116 us -> 105 us (0.905)
  waiting for transfers between devices: 38.8 us -> 30.9 us
  local copies, waits for them, and re-layouts: 8.83 us -> 6.93 us
    ppermute x9, waiting for transfers between devices: 7.33 us -> 3.97 us  [swap(): return lax.ppermute(block, 'feat', [(i, i ^ bit) for i in range(m)])]
    ppermute x1, waiting for transfers between devices: 4.94 us -> 1.82 us  [shards(): pairs = [keep, lax.ppermute(give, 'fact', [(i, i ^ 1) for i in range(n)])]]
    ppermute x4 -> x3, waiting for transfers between devices: 6.69 us -> 3.57 us  [pass_on(): lax.ppermute(right, 'fact', to_right)]
    slice x3 -> x0, local copies, waits for them, and re-layouts: 1.96 us -> none  [the longest x1 0.66 us: shards(): left[half:]]
    ppermute x4 -> x3, starting transfers between devices: 4.68 us -> 2.77 us  [pass_on(): lax.ppermute(left, 'fact', to_left)]
    ppermute x0 -> x1, starting transfers between devices: none -> 1.58 us  [shards(): after = lax.ppermute(right, 'fact', to_right)]
    all_to_all x1, waiting for transfers between devices: 0.01 us -> 1.51 us  [shards(): lax.all_to_all(back, ('fact', 'feat'), 0, 0).reshape(n * ents, LANES)]
    ppermute x4 -> x3, waiting for transfers between devices: 1.48 us -> 2.49 us  [pass_on(): lax.ppermute(left, 'fact', to_left)]
  transfers between devices with their start and end apart: 28 -> 27, of which waited for: 14 -> 16; matrix products, arithmetic and copies ran while one was open for 1% -> 0% of each run, Pallas kernels for 16% -> 20%
where the time goes in v1:
time: 105 us
  starting transfers between devices  41.2 us (39%)
  waiting for transfers between devices  30.9 us (29%)
  Pallas kernels  24.5 us (23%)
  local copies, waits for them, and re-layouts  6.93 us (7%)
    ppermute x7, starting transfers between devices, shards(): lax.ppermute(message, 'fact', [(i, (i + offset) % n) for i in range(n)])  13.7 us
    ppermute x7, waiting for transfers between devices, shards(): lax.ppermute(message, 'fact', [(i, (i + offset) % n) for i in range(n)])  9.5 us
    all_to_all x1, waiting for transfers between devices, shards(): lax.all_to_all(part.reshape(n * m, rows_each, LANES), ('fact', 'feat'), 0...  8.02 us
    unnamed x38, local copies, waits for them, and re-layouts  6.89 us
    pallas_call x3, Pallas kernels, look(): call(functools.partial(look_kernel, n, pieces), shape((facts, LANES), F32...  6.16 us
    all_to_all x1, starting transfers between devices, shards(): lax.all_to_all(part.reshape(n * m, rows_each, LANES), ('fact', 'feat'), 0...  5.8 us
    ppermute x9, starting transfers between devices, swap(): return lax.ppermute(block, 'feat', [(i, i ^ bit) for i in range(m)])  5.35 us
    pallas_call x4, Pallas kernels, add_up(): call(functools.partial(table_kernel, n, cap, stride, offsets, base is Non...  5.03 us
  transfers between devices with their start and end apart: 27, of which 16 were waited for; matrix products, arithmetic and copies ran while one was open for 0% of the time, Pallas kernels for 20%

profile of v1, /device:TPU:4, one launch (start us, length us, event | category | flops | bytes accessed | tf_op | source)
XLA Modules:
  0.0 104.5 jit_solution(11814675421394123176)
XLA Ops:
  0.7 2.0 %collective-permute-start.1 = (bf16[1024,128]{1,0:T(8,128)(2,1)}, bf16[1024,128]{1,0:T(8,128)(2,1)S(1)}, u32[]{:S(2)}, u32[]{:S(2)}) collective-permute-start(bf16[1024,128]{1,0:T(8,128)(2,1)} %refs_0_.2), channel_id=1, source_target_pairs={{8,0},{16,8},{24,16},{28,24},{20,28},{12,20},{4,12},{0,4},{9,1},{1... | collective-permute-start | bytes 786440 | tf_op jit(solution)/shard_map/ppermute | solution.py:396
  6.3 1.7 %route.1 = (s32[8,4,128]{2,1,0:T(4,128)}, s32[8,128]{1,0:T(8,128)S(1)}, s32[8,128]{1,0:T(8,128)S(1)}, bf16[1024,128]{1,0:T(8,128)(2,1)S(1)}, bf16[1024,128]{1,0:T(8,128)(2,1)S(1)}) custom-call(s32[8,128]{1,0:T(8,128)S(1)} %bitcast.7, s32[8,128]{1,0:T(8,128)S(1)} %bitcast.8, s32[8,128]{1,0:T(8,128)S(1)} %bitcast.9, s32[8,128]{1,0:T(8,128)S(1)} %bitcast.10), custom_call_target="tpu_custom_call" | custom-call | flops 268435456 | bytes 1048576 | tf_op jit(solution)/shard_map/route/pallas_call | solution.py:407
  9.0 1.7 %collective-permute-start.3 = (bf16[1024,128]{1,0:T(8,128)(2,1)S(1)}, bf16[1024,128]{1,0:T(8,128)(2,1)S(1)}, u32[]{:S(2)}, u32[]{:S(2)}) collective-permute-start(bf16[1024,128]{1,0:T(8,128)(2,1)S(1)} %collective-permute-done.refs_1_), channel_id=1, source_target_pairs={{0,8},{8,16},{16,24},{24,28},{28,20},{20,12},{12,4},{4,0},{1,9},{9... | collective-permute-start | bytes 786440 | tf_op jit(solution)/shard_map/ppermute | solution.py:396
  12.1 2.6 %look.3.refs_2_ = f32[1024,128]{1,0:T(8,128)S(1)} custom-call(bf16[1024,128]{1,0:T(8,128)(2,1)S(1)} %get-tuple-element.89.low_ref, bf16[1024,128]{1,0:T(8,128)(2,1)S(1)} %get-tuple-element.90.high_ref, bf16[1024,128]{1,0:T(8,128)(2,1)S(1)} %copy-done.10, bf16[1024,128]{1,0:T(8,128)(2,1)S(1)} %collective-permute-done.refs_1_, ...), custom_call_target="tpu_custom_call" | custom-call | flops 805306368 | bytes 1048576 | tf_op jit(solution)/shard_map/look/pallas_call | solution.py:427
  14.7 1.8 %collective-permute-done.3.refs_0_ = bf16[1024,128]{1,0:T(8,128)(2,1)S(1)} collective-permute-done((bf16[1024,128]{1,0:T(8,128)(2,1)S(1)}, bf16[1024,128]{1,0:T(8,128)(2,1)S(1)}, u32[]{:S(2)}, u32[]{:S(2)}) %collective-permute-start.3) | collective-permute-done | bytes 262176 | tf_op jit(solution)/shard_map/ppermute | solution.py:396
  17.3 1.6 %collective-permute-start.6 = (bf16[1024,128]{1,0:T(8,128)(2,1)S(1)}, bf16[1024,128]{1,0:T(8,128)(2,1)S(1)}, u32[]{:S(2)}, u32[]{:S(2)}) collective-permute-start(bf16[1024,128]{1,0:T(8,128)(2,1)S(1)} %collective-permute-done.3.refs_0_), channel_id=1, source_target_pairs={{0,8},{8,16},{16,24},{24,28},{28,20},{20,12},{12,4},{4,0},{1,9},{9... | collective-permute-start | bytes 786440 | tf_op jit(solution)/shard_map/ppermute | solution.py:396
  21.1 1.8 %look.4.refs_2_ = f32[1024,128]{1,0:T(8,128)S(1)} custom-call(bf16[1024,128]{1,0:T(8,128)(2,1)S(1)} %get-tuple-element.89.low_ref, bf16[1024,128]{1,0:T(8,128)(2,1)S(1)} %get-tuple-element.90.high_ref, bf16[1024,128]{1,0:T(8,128)(2,1)S(1)} %collective-permute-done.3.refs_0_, bf16[1024,128]{1,0:T(8,128)(2,1)S(1)} %collective-permute-done.4.refs_1_, ...), custom_call_target="tpu_custom_call" | custom-call | flops 536870912 | bytes 1048576 | tf_op jit(solution)/shard_map/look/pallas_call | solution.py:427
  23.7 1.6 %collective-permute-done.7.refs_1_ = bf16[1024,128]{1,0:T(8,128)(2,1)S(1)} collective-permute-done((bf16[1024,128]{1,0:T(8,128)(2,1)S(1)}, bf16[1024,128]{1,0:T(8,128)(2,1)S(1)}, u32[]{:S(2)}, u32[]{:S(2)}) %collective-permute-start.7) | collective-permute-done | bytes 262176 | tf_op jit(solution)/shard_map/ppermute | solution.py:396
  27.6 4.8 %all-to-all-start.1 = ((s32[8,4,128]{2,1,0:T(4,128)}), s32[8,4,128]{2,1,0:T(4,128)S(1)}, u32[]{:S(2)}, u32[]{:S(2)}) async-start(s32[8,4,128]{2,1,0:T(4,128)} %get-tuple-element.109), calls=%async_computation.1 | async-start | bytes 32768 | tf_op jit(solution)/shard_map/all_to_all | solution.py:474
  33.3 1.8 %look.5.refs_1_ = f32[1024,128]{1,0:T(8,128)S(1)} custom-call(bf16[1024,128]{1,0:T(8,128)(2,1)S(1)} %get-tuple-element.89.low_ref, bf16[1024,128]{1,0:T(8,128)(2,1)S(1)} %get-tuple-element.90.high_ref, bf16[1024,128]{1,0:T(8,128)(2,1)S(1)} %collective-permute-done.6.refs_0_, bf16[1024,128]{1,0:T(8,128)(2,1)S(1)} %copy-done.8, f32[1024,128]{1,0:T(8,128)S(1)} %look.4.refs_2_), custom_call_target="tpu_custom_call" | custom-call | flops 536870912 | bytes 1048576 | tf_op jit(solution)/shard_map/look/pallas_call | solution.py:427
  35.1 3.9 %message.1 = (f32[1024,128]{1,0:T(8,128)S(1)}, bf16[1024,128]{1,0:T(8,128)(2,1)}) custom-call(bf16[1024,128]{1,0:T(8,128)(2,1)S(1)} %get-tuple-element.89.low_ref, bf16[1024,128]{1,0:T(8,128)(2,1)S(1)} %get-tuple-element.90.high_ref, bf16[1024,128]{1,0:T(8,128)(2,1)} %collective-permute-done.9.refs_0_, f32[1024,128]{1,0:T(8,128)S(1)} %look.5.refs_1_, ...), custom_call_target="tpu_custom_call" | custom-call | flops 536870912 | bytes 1048576 | tf_op jit(solution)/shard_map/message/pallas_call | solution.py:476
  39.8 5.8 %all-to-all-start = ((bf16[32,32,128]{2,1,0:T(8,128)(2,1)}), bf16[32,32,128]{2,1,0:T(8,128)(2,1)S(1)}, u32[]{:S(2)}, u32[]{:S(2)}) async-start(bf16[32,32,128]{2,1,0:T(8,128)(2,1)} %bitcast.4), calls=%async_computation | async-start | bytes 524288 | tf_op jit(solution)/shard_map/all_to_all | solution.py:492
  47.3 8.0 %all-to-all-done.sums_ref = bf16[32,32,128]{2,1,0:T(8,128)(2,1)S(1)} async-done(((bf16[32,32,128]{2,1,0:T(8,128)(2,1)}), bf16[32,32,128]{2,1,0:T(8,128)(2,1)S(1)}, u32[]{:S(2)}, u32[]{:S(2)}) %all-to-all-start) | async-done | bytes 262176 | tf_op jit(solution)/shard_map/all_to_all | solution.py:492
  56.9 3.4 %all-to-all-start.2 = ((bf16[32,32,128]{2,1,0:T(8,128)(2,1)}), bf16[32,32,128]{2,1,0:T(8,128)(2,1)S(1)}, u32[]{:S(2)}, u32[]{:S(2)}) async-start(bf16[32,32,128]{2,1,0:T(8,128)(2,1)} %get-tuple-element.120), calls=%async_computation.2 | async-start | bytes 524288 | tf_op jit(solution)/shard_map/all_to_all | solution.py:509
  64.5 1.8 %collective-permute-done.14.refs_2_ = bf16[192,128]{1,0:T(8,128)(2,1)S(1)} collective-permute-done((bf16[192,128]{1,0:T(8,128)(2,1)S(1)}, bf16[192,128]{1,0:T(8,128)(2,1)S(1)}, u32[]{:S(2)}, u32[]{:S(2)}) %collective-permute-start.14) | collective-permute-done | bytes 49184 | tf_op jit(solution)/shard_map/ppermute | solution.py:399
  70.1 1.6 %backward.1 = (bf16[1024,128]{1,0:T(8,128)(2,1)S(1)}, bf16[8,64,128]{2,1,0:T(8,128)(2,1)S(1)}) custom-call(f32[1024,128]{1,0:T(8,128)S(1)} %copy-done.6, bf16[1024,128]{1,0:T(8,128)(2,1)S(1)} %bitcast.6, bf16[1024,128]{1,0:T(8,128)(2,1)S(1)} %get-tuple-element.129.low_ref, bf16[1024,128]{1,0:T(8,128)(2,1)S(1)} %get-tuple-element.130.high_ref, ...), custom_call_target="tpu_custom_call" | custom-call | flops 402653184 | bytes 1048576 | tf_op jit(solution)/shard_map/backward/pallas_call | solution.py:547
  71.8 1.8 %collective-permute-done.16.refs_1_ = bf16[4,128,128]{2,1,0:T(8,128)(2,1)S(1)} collective-permute-done((bf16[4,128,128]{2,1,0:T(8,128)(2,1)S(1)}, bf16[4,128,128]{2,1,0:T(8,128)(2,1)S(1)}, u32[]{:S(2)}, u32[]{:S(2)}) %collective-permute-start.16) | collective-permute-done | bytes 131104 | tf_op jit(solution)/shard_map/ppermute | solution.py:544
  76.6 2.9 %collective-permute-start.21 = (bf16[576,128]{1,0:T(8,128)(2,1)S(1)}, bf16[576,128]{1,0:T(8,128)(2,1)S(1)}, u32[]{:S(2)}, u32[]{:S(2)}) collective-permute-start(bf16[576,128]{1,0:T(8,128)(2,1)S(1)} %spread.7), channel_id=1, source_target_pairs={{0,16},{4,20},{8,24},{12,28},{16,0},{20,4},{24,8},{28,12},{1,17},{... | collective-permute-start | bytes 442376 | tf_op jit(solution)/shard_map/ppermute | solution.py:590
  80.2 1.6 %collective-permute-start.19 = (bf16[576,128]{1,0:T(8,128)(2,1)S(1)}, bf16[576,128]{1,0:T(8,128)(2,1)S(1)}, u32[]{:S(2)}, u32[]{:S(2)}) collective-permute-start(bf16[576,128]{1,0:T(8,128)(2,1)S(1)} %get-tuple-element.139), channel_id=1, source_target_pairs={{0,8},{4,12},{8,16},{12,20},{16,24},{20,28},{24,0},{28,4},{1,9},{5... | collective-permute-start | bytes 442376 | tf_op jit(solution)/shard_map/ppermute | solution.py:590
  81.8 2.2 %collective-permute-start.20 = (bf16[576,128]{1,0:T(8,128)(2,1)S(1)}, bf16[576,128]{1,0:T(8,128)(2,1)S(1)}, u32[]{:S(2)}, u32[]{:S(2)}) collective-permute-start(bf16[576,128]{1,0:T(8,128)(2,1)S(1)} %get-tuple-element.140), channel_id=1, source_target_pairs={{0,24},{4,28},{8,0},{12,4},{16,8},{20,12},{24,16},{28,20},{1,25},{... | collective-permute-start | bytes 442376 | tf_op jit(solution)/shard_map/ppermute | solution.py:590
  85.8 3.6 %collective-permute-start.18 = (bf16[448,128]{1,0:T(8,128)(2,1)S(1)}, bf16[448,128]{1,0:T(8,128)(2,1)S(1)}, u32[]{:S(2)}, u32[]{:S(2)}) collective-permute-start(bf16[448,128]{1,0:T(8,128)(2,1)S(1)} %get-tuple-element.138), channel_id=1, source_target_pairs={{0,20},{4,24},{8,28},{12,0},{16,4},{20,8},{24,12},{28,16},{1,21},{... | collective-permute-start | bytes 344072 | tf_op jit(solution)/shard_map/ppermute | solution.py:590
  94.8 1.8 %collective-permute-done.17.refs_0_ = bf16[448,128]{1,0:T(8,128)(2,1)S(1)} collective-permute-done((bf16[448,128]{1,0:T(8,128)(2,1)S(1)}, bf16[448,128]{1,0:T(8,128)(2,1)S(1)}, u32[]{:S(2)}, u32[]{:S(2)}) %collective-permute-start.17) | collective-permute-done | bytes 114720 | tf_op jit(solution)/shard_map/ppermute | solution.py:590
  96.6 6.1 %collective-permute-done.18.refs_1_ = bf16[448,128]{1,0:T(8,128)(2,1)S(1)} collective-permute-done((bf16[448,128]{1,0:T(8,128)(2,1)S(1)}, bf16[448,128]{1,0:T(8,128)(2,1)S(1)}, u32[]{:S(2)}, u32[]{:S(2)}) %collective-permute-start.18) | collective-permute-done | bytes 114720 | tf_op jit(solution)/shard_map/ppermute | solution.py:590
  102.7 1.8 %table.7 = (f32[1024,128]{1,0:T(8,128)}, f32[64,128]{1,0:T(8,128)}, f32[64,128]{1,0:T(8,128)}, f32[64,128]{1,0:T(8,128)}) custom-call(bf16[128,3072]{1,0:T(8,128)(2,1)S(1)} %get-tuple-element.122.low_ref, bf16[16,3072]{1,0:T(8,128)(2,1)S(1)} %get-tuple-element.123.high_ref, bf16[448,128]{1,0:T(8,128)(2,1)S(1)} %collective-permute-done.17.refs_0_, ...), custom_call_target="tpu_custom_call" | custom-call | flops 201326592 | bytes 1048576 | tf_op jit(solution)/shard_map/table/pallas_call | solution.py:575
  (93 shorter events, 35.7 us)
Async XLA Ops:
  0.6 8.3 %collective-permute-start = (bf16[1024,128]{1,0:T(8,128)(2,1)}, bf16[1024,128]{1,0:T(8,128)(2,1)S(1)}, u32[]{:S(2)}, u32[]{:S(2)}) collective-permute-start(bf16[1024,128]{1,0:T(8,128)(2,1)} %refs_0_.2), channel_id=1, source_target_pairs={{0,8},{8,16},{16,24},{24,28},{28,20},{20,12},{12,4},{4,0},{1,9},{9... | collective-permute-start | bytes 786440 | tf_op jit(solution)/shard_map/ppermute | solution.py:396
  0.7 8.3 %collective-permute-start.1 = (bf16[1024,128]{1,0:T(8,128)(2,1)}, bf16[1024,128]{1,0:T(8,128)(2,1)S(1)}, u32[]{:S(2)}, u32[]{:S(2)}) collective-permute-start(bf16[1024,128]{1,0:T(8,128)(2,1)} %refs_0_.2), channel_id=1, source_target_pairs={{8,0},{16,8},{24,16},{28,24},{20,28},{12,20},{4,12},{0,4},{9,1},{1... | collective-permute-start | bytes 786440 | tf_op jit(solution)/shard_map/ppermute | solution.py:396
  2.7 6.3 %collective-permute-start.2 = (bf16[1024,128]{1,0:T(8,128)(2,1)}, bf16[1024,128]{1,0:T(8,128)(2,1)S(1)}, u32[]{:S(2)}, u32[]{:S(2)}) collective-permute-start(bf16[1024,128]{1,0:T(8,128)(2,1)} %refs_0_.4), channel_id=1, source_target_pairs={{0,1},{1,0},{2,3},{3,2},{4,5},{5,4},{6,7},{7,6},{8,9},{9,8},{10,11... | collective-permute-start | bytes 786440 | tf_op jit(solution)/shard_map/ppermute | solution.py:399
  2.7 12.0 %collective-permute-start.5 = (bf16[1024,128]{1,0:T(8,128)(2,1)}, bf16[1024,128]{1,0:T(8,128)(2,1)S(1)}, u32[]{:S(2)}, u32[]{:S(2)}) collective-permute-start(bf16[1024,128]{1,0:T(8,128)(2,1)} %refs_0_.4), channel_id=1, source_target_pairs={{0,2},{1,3},{2,0},{3,1},{4,6},{5,7},{6,4},{7,5},{8,10},{9,11},{10,... | collective-permute-start | bytes 786440 | tf_op jit(solution)/shard_map/ppermute | solution.py:399
  9.0 7.5 %collective-permute-start.3 = (bf16[1024,128]{1,0:T(8,128)(2,1)S(1)}, bf16[1024,128]{1,0:T(8,128)(2,1)S(1)}, u32[]{:S(2)}, u32[]{:S(2)}) collective-permute-start(bf16[1024,128]{1,0:T(8,128)(2,1)S(1)} %collective-permute-done.refs_1_), channel_id=1, source_target_pairs={{0,8},{8,16},{16,24},{24,28},{28,20},{20,12},{12,4},{4,0},{1,9},{9... | collective-permute-start | bytes 786440 | tf_op jit(solution)/shard_map/ppermute | solution.py:396
  10.8 6.6 %collective-permute-start.4 = (bf16[1024,128]{1,0:T(8,128)(2,1)S(1)}, bf16[1024,128]{1,0:T(8,128)(2,1)S(1)}, u32[]{:S(2)}, u32[]{:S(2)}) collective-permute-start(bf16[1024,128]{1,0:T(8,128)(2,1)S(1)} %collective-permute-done.1.refs_2_), channel_id=1, source_target_pairs={{8,0},{16,8},{24,16},{28,24},{20,28},{12,20},{4,12},{0,4},{9,1},{1... | collective-permute-start | bytes 786440 | tf_op jit(solution)/shard_map/ppermute | solution.py:396
  17.3 6.4 %collective-permute-start.6 = (bf16[1024,128]{1,0:T(8,128)(2,1)S(1)}, bf16[1024,128]{1,0:T(8,128)(2,1)S(1)}, u32[]{:S(2)}, u32[]{:S(2)}) collective-permute-start(bf16[1024,128]{1,0:T(8,128)(2,1)S(1)} %collective-permute-done.3.refs_0_), channel_id=1, source_target_pairs={{0,8},{8,16},{16,24},{24,28},{28,20},{20,12},{12,4},{4,0},{1,9},{9... | collective-permute-start | bytes 786440 | tf_op jit(solution)/shard_map/ppermute | solution.py:396
  18.9 6.4 %collective-permute-start.7 = (bf16[1024,128]{1,0:T(8,128)(2,1)S(1)}, bf16[1024,128]{1,0:T(8,128)(2,1)S(1)}, u32[]{:S(2)}, u32[]{:S(2)}) collective-permute-start(bf16[1024,128]{1,0:T(8,128)(2,1)S(1)} %collective-permute-done.4.refs_1_), channel_id=1, source_target_pairs={{8,0},{16,8},{24,16},{28,24},{20,28},{12,20},{4,12},{0,4},{9,1},{1... | collective-permute-start | bytes 786440 | tf_op jit(solution)/shard_map/ppermute | solution.py:396
  19.4 6.6 %collective-permute-start.8 = (bf16[1024,128]{1,0:T(8,128)(2,1)S(1)}, bf16[1024,128]{1,0:T(8,128)(2,1)S(1)}, u32[]{:S(2)}, u32[]{:S(2)}) collective-permute-start(bf16[1024,128]{1,0:T(8,128)(2,1)S(1)} %collective-permute-done.5.refs_2_), channel_id=1, source_target_pairs={{0,1},{1,0},{2,3},{3,2},{4,5},{5,4},{6,7},{7,6},{8,9},{9,8},{10,11... | collective-permute-start | bytes 786440 | tf_op jit(solution)/shard_map/ppermute | solution.py:399
  19.4 15.7 %collective-permute-start.10 = (bf16[1280,128]{1,0:T(8,128)(2,1)S(1)}, bf16[1280,128]{1,0:T(8,128)(2,1)S(1)}, u32[]{:S(2)}, u32[]{:S(2)}) collective-permute-start(bf16[1280,128]{1,0:T(8,128)(2,1)S(1)} %pad_maximum_fusion.refs_4_.refs_0_), channel_id=1, source_target_pairs={{0,2},{1,3},{2,0},{3,1},{4,6},{5,7},{6,4},{7,5},{8,10},{9,11},{10,... | collective-permute-start | bytes 983048 | tf_op jit(solution)/shard_map/ppermute | solution.py:399
  20.9 14.3 %collective-permute-start.11 = (bf16[1280,128]{1,0:T(8,128)(2,1)S(1)}, bf16[1280,128]{1,0:T(8,128)(2,1)S(1)}, u32[]{:S(2)}, u32[]{:S(2)}) collective-permute-start(bf16[1280,128]{1,0:T(8,128)(2,1)S(1)} %pad_maximum_fusion.refs_4_.refs_0_), channel_id=1, source_target_pairs={{0,1},{1,0},{2,3},{3,2},{4,5},{5,4},{6,7},{7,6},{8,9},{9,8},{10,11... | collective-permute-start | bytes 983048 | tf_op jit(solution)/shard_map/ppermute | solution.py:399
  26.0 9.1 %collective-permute-start.9 = (bf16[1024,128]{1,0:T(8,128)(2,1)S(1)}, bf16[1024,128]{1,0:T(8,128)(2,1)}, u32[]{:S(2)}, u32[]{:S(2)}) collective-permute-start(bf16[1024,128]{1,0:T(8,128)(2,1)S(1)} %collective-permute-done.6.refs_0_), channel_id=1, source_target_pairs={{0,8},{8,16},{16,24},{24,28},{28,20},{20,12},{12,4},{4,0},{1,9},{9... | collective-permute-start | bytes 786440 | tf_op jit(solution)/shard_map/ppermute | solution.py:456
  27.6 12.3 %all-to-all-start.1 = ((s32[8,4,128]{2,1,0:T(4,128)}), s32[8,4,128]{2,1,0:T(4,128)S(1)}, u32[]{:S(2)}, u32[]{:S(2)}) async-start(s32[8,4,128]{2,1,0:T(4,128)} %get-tuple-element.109), calls=%async_computation.1 | async-start | bytes 32768 | tf_op jit(solution)/shard_map/all_to_all | solution.py:474
  39.8 15.5 %all-to-all-start = ((bf16[32,32,128]{2,1,0:T(8,128)(2,1)}), bf16[32,32,128]{2,1,0:T(8,128)(2,1)S(1)}, u32[]{:S(2)}, u32[]{:S(2)}) async-start(bf16[32,32,128]{2,1,0:T(8,128)(2,1)} %bitcast.4), calls=%async_computation | async-start | bytes 524288 | tf_op jit(solution)/shard_map/all_to_all | solution.py:492
  56.9 13.2 %all-to-all-start.2 = ((bf16[32,32,128]{2,1,0:T(8,128)(2,1)}), bf16[32,32,128]{2,1,0:T(8,128)(2,1)S(1)}, u32[]{:S(2)}, u32[]{:S(2)}) async-start(bf16[32,32,128]{2,1,0:T(8,128)(2,1)} %get-tuple-element.120), calls=%async_computation.2 | async-start | bytes 524288 | tf_op jit(solution)/shard_map/all_to_all | solution.py:509
  60.6 5.8 %collective-permute-start.14 = (bf16[192,128]{1,0:T(8,128)(2,1)S(1)}, bf16[192,128]{1,0:T(8,128)(2,1)S(1)}, u32[]{:S(2)}, u32[]{:S(2)}) collective-permute-start(bf16[192,128]{1,0:T(8,128)(2,1)S(1)} %get-tuple-element.115), channel_id=1, source_target_pairs={{0,2},{1,3},{2,0},{3,1},{4,6},{5,7},{6,4},{7,5},{8,10},{9,11},{10,... | collective-permute-start | bytes 147464 | tf_op jit(solution)/shard_map/ppermute | solution.py:399
  67.7 5.9 %collective-permute-start.16 = (bf16[4,128,128]{2,1,0:T(8,128)(2,1)S(1)}, bf16[4,128,128]{2,1,0:T(8,128)(2,1)S(1)}, u32[]{:S(2)}, u32[]{:S(2)}) collective-permute-start(bf16[4,128,128]{2,1,0:T(8,128)(2,1)S(1)} %get-tuple-element.136), channel_id=1, source_target_pairs={{0,4},{4,0},{8,12},{12,8},{16,20},{20,16},{24,28},{28,24},{1,5},{5... | collective-permute-start | bytes 393224 | tf_op jit(solution)/shard_map/ppermute | solution.py:544
  74.2 10.4 %collective-permute-start.22 = (bf16[448,128]{1,0:T(8,128)(2,1)S(1)}, bf16[448,128]{1,0:T(8,128)(2,1)S(1)}, u32[]{:S(2)}, u32[]{:S(2)}) collective-permute-start(bf16[448,128]{1,0:T(8,128)(2,1)S(1)} %get-tuple-element.141), channel_id=1, source_target_pairs={{0,4},{4,8},{8,12},{12,16},{16,20},{20,24},{24,28},{28,0},{1,5},{5... | collective-permute-start | bytes 344072 | tf_op jit(solution)/shard_map/ppermute | solution.py:590
  75.6 10.2 %collective-permute-start.23 = (bf16[448,128]{1,0:T(8,128)(2,1)S(1)}, bf16[448,128]{1,0:T(8,128)(2,1)S(1)}, u32[]{:S(2)}, u32[]{:S(2)}) collective-permute-start(bf16[448,128]{1,0:T(8,128)(2,1)S(1)} %get-tuple-element.142), channel_id=1, source_target_pairs={{0,28},{4,0},{8,4},{12,8},{16,12},{20,16},{24,20},{28,24},{1,29},{... | collective-permute-start | bytes 344072 | tf_op jit(solution)/shard_map/ppermute | solution.py:590
  76.6 15.4 %collective-permute-start.21 = (bf16[576,128]{1,0:T(8,128)(2,1)S(1)}, bf16[576,128]{1,0:T(8,128)(2,1)S(1)}, u32[]{:S(2)}, u32[]{:S(2)}) collective-permute-start(bf16[576,128]{1,0:T(8,128)(2,1)S(1)} %spread.7), channel_id=1, source_target_pairs={{0,16},{4,20},{8,24},{12,28},{16,0},{20,4},{24,8},{28,12},{1,17},{... | collective-permute-start | bytes 442376 | tf_op jit(solution)/shard_map/ppermute | solution.py:590
  80.2 12.7 %collective-permute-start.19 = (bf16[576,128]{1,0:T(8,128)(2,1)S(1)}, bf16[576,128]{1,0:T(8,128)(2,1)S(1)}, u32[]{:S(2)}, u32[]{:S(2)}) collective-permute-start(bf16[576,128]{1,0:T(8,128)(2,1)S(1)} %get-tuple-element.139), channel_id=1, source_target_pairs={{0,8},{4,12},{8,16},{12,20},{16,24},{20,28},{24,0},{28,4},{1,9},{5... | collective-permute-start | bytes 442376 | tf_op jit(solution)/shard_map/ppermute | solution.py:590
  81.8 11.9 %collective-permute-start.20 = (bf16[576,128]{1,0:T(8,128)(2,1)S(1)}, bf16[576,128]{1,0:T(8,128)(2,1)S(1)}, u32[]{:S(2)}, u32[]{:S(2)}) collective-permute-start(bf16[576,128]{1,0:T(8,128)(2,1)S(1)} %get-tuple-element.140), channel_id=1, source_target_pairs={{0,24},{4,28},{8,0},{12,4},{16,8},{20,12},{24,16},{28,20},{1,25},{... | collective-permute-start | bytes 442376 | tf_op jit(solution)/shard_map/ppermute | solution.py:590
  84.6 12.0 %collective-permute-start.17 = (bf16[448,128]{1,0:T(8,128)(2,1)S(1)}, bf16[448,128]{1,0:T(8,128)(2,1)S(1)}, u32[]{:S(2)}, u32[]{:S(2)}) collective-permute-start(bf16[448,128]{1,0:T(8,128)(2,1)S(1)} %get-tuple-element.137), channel_id=1, source_target_pairs={{0,12},{4,16},{8,20},{12,24},{16,28},{20,0},{24,4},{28,8},{1,13},{... | collective-permute-start | bytes 344072 | tf_op jit(solution)/shard_map/ppermute | solution.py:590
  85.8 16.9 %collective-permute-start.18 = (bf16[448,128]{1,0:T(8,128)(2,1)S(1)}, bf16[448,128]{1,0:T(8,128)(2,1)S(1)}, u32[]{:S(2)}, u32[]{:S(2)}) collective-permute-start(bf16[448,128]{1,0:T(8,128)(2,1)S(1)} %get-tuple-element.138), channel_id=1, source_target_pairs={{0,20},{4,24},{8,28},{12,0},{16,4},{20,8},{24,12},{28,16},{1,21},{... | collective-permute-start | bytes 344072 | tf_op jit(solution)/shard_map/ppermute | solution.py:590
  (22 other events, 103.8 us)

commit v2 on v1

--- a/solution.py
+++ b/solution.py
@@ -9,6 +9,8 @@
 
 LANES = 128
 BF = jnp.bfloat16
+IN_HBM = pl.BlockSpec(memory_space=pltpu.HBM)
+IN_VMEM = pl.BlockSpec(memory_space=pltpu.VMEM)
 F32 = jnp.float32
 VMEM_LIMIT = 16 * 1024 * 1024
 VMEM_LIMIT_LARGE = 40 * 1024 * 1024
@@ -70,7 +72,14 @@
     return picked.reshape(low.shape)
 
 
-def route_kernel(n, cap, ents, dims, do_ref, ds_ref, fo_ref, fs_ref, out_ref, pos_ref, ent_ref, dlow_ref, dhigh_ref):
+def route_kernel(n, cap, ents, dims, *refs):
+    given, (out_ref, pos_ref, ent_ref, dlow_ref, dhigh_ref), held_refs, sems = refs[:4], refs[4:9], refs[9:13], refs[13]
+    copies = [pltpu.make_async_copy(src, dst, sems.at[i]) for i, (src, dst) in enumerate(zip(given, held_refs))]
+    for copy in copies:
+        copy.start()
+    for copy in copies:
+        copy.wait()
+    do_ref, ds_ref, fo_ref, fs_ref = held_refs
     chunks = do_ref.shape[0]
     owner = do_ref[...]
     kind = lax.broadcasted_iota(jnp.int32, (n, chunks, LANES), 0)
@@ -152,8 +161,12 @@
 
 def message_kernel(n, pieces, low_ref, high_ref, *refs):
     count = len(pieces)
-    tables, refs = refs[:count], refs[count:]
-    base_ref, xw_ref, ent_ref, slope_out, part_ref, slope_ref, hot_ref, msg_ref, erlow_ref, erhigh_ref, sem = refs
+    sources, refs = refs[:count], refs[count:]
+    base_ref, xw_ref, ent_ref, slope_out, part_ref, slope_ref, hot_ref, msg_ref, erlow_ref, erhigh_ref = refs[:10]
+    tables, (sem, table_sem) = refs[10 : 10 + count], refs[10 + count :]
+    arrivals = [pltpu.make_async_copy(src, dst, table_sem) for src, dst in zip(sources, tables)]
+    for copy in arrivals:
+        copy.start()
     facts = low_ref.shape[0]
     step = hot_ref.shape[0]
     place = ring_place(lax.axis_index("fact"), n)
@@ -161,6 +174,8 @@
     for k in range(ent_ref.shape[0]):
         here = slice(k * LANES, (k + 1) * LANES)
         erlow_ref[:, here], erhigh_ref[:, here] = row_codes(ent_ref[k : k + 1, :])
+    for copy in arrivals:
+        copy.wait()
     for c in range(facts // step):
         rows = slice(c * step, (c + 1) * step)
         pre = xw_ref[rows, :] + base_ref[rows, :]
@@ -204,17 +219,23 @@
 
 
 def entity_kernel(n, m, width, ents, sums_ref, idx_ref, *refs):
-    all_refs, (back_ref, out_ref, pre_ref, agg_ref, own_ref, hold_ref) = refs[:m], refs[m:]
+    all_refs, (back_ref, out_ref, pre_ref, agg_ref, own_ref, hold_ref, words_ref, sem) = refs[:m], refs[m:]
+    fetch = pltpu.make_async_copy(idx_ref, words_ref, sem)
+    fetch.start()
     rows_each = ents // m
     me = lax.axis_index("feat")
-    hits = jnp.sum(idx_ref[:, idx_ref.shape[1] - 1, :], axis=0, keepdims=True).astype(F32)
-    hold_ref[...] = jnp.maximum(jnp.broadcast_to(hits, (LANES, ents)).T, 1.0)
-    divisor = hold_ref[pl.ds(pl.multiple_of(me * rows_each, rows_each), rows_each), :]
+    totals = []
     for b in range(m):
         total = sums_ref[b].astype(F32)
         for f in range(1, n):
             total += sums_ref[f * m + b].astype(F32)
-        agg_ref[b * rows_each : (b + 1) * rows_each, :] = (total / divisor).astype(BF)
+        totals.append(total)
+    fetch.wait()
+    hits = jnp.sum(words_ref[:, words_ref.shape[1] - 1, :], axis=0, keepdims=True).astype(F32)
+    hold_ref[...] = jnp.maximum(jnp.broadcast_to(hits, (LANES, ents)).T, 1.0)
+    divisor = hold_ref[pl.ds(pl.multiple_of(me * rows_each, rows_each), rows_each), :]
+    for b in range(m):
+        agg_ref[b * rows_each : (b + 1) * rows_each, :] = (totals[b] / divisor).astype(BF)
     at = pl.multiple_of(2 * width + me * rows_each, rows_each)
     for j in range(m):
         own_ref[me ^ j] = all_refs[j][pl.ds(at, rows_each), :]
@@ -337,7 +358,7 @@
         (base_ref, weight_base_ref), refs = refs[:2], refs[2:]
     out_ref, refs = refs[0], refs[1:]
     final_refs, refs = (refs[:3], refs[3:]) if final else ((), refs[1:] + refs[:1])
-    rows_ref, klow_ref, khigh_ref, weight_ref = refs
+    rows_ref, klow_ref, khigh_ref, weight_ref = refs[:4]
     me = lax.axis_index("fact")
     if first:
         weight_ref[...] = jnp.zeros(weight_ref.shape, F32)
@@ -357,16 +378,20 @@
     blocks = out_ref.shape[0] // LANES
     join = 2 if blocks % 2 == 0 else 1
 
-    def add(group, carry):
+    target_ref = refs[4] if final else out_ref
+    copies = []
+    for group in range(blocks // join):
         hot = jnp.concatenate(
-            [pick_rows(klow_ref[...], khigh_ref[...], (group * join + i).astype(F32).astype(BF)) for i in range(join)], axis=0
+            [pick_rows(klow_ref[...], khigh_ref[...], jnp.array(group * join + i, BF)) for i in range(join)], axis=0
         )
-        rows = pl.ds(pl.multiple_of(group * join * LANES, LANES), join * LANES)
+        rows = slice(group * join * LANES, (group + 1) * join * LANES)
         sums = dot(hot, rows_ref[...])
-        out_ref[rows, :] = sums if first else base_ref[rows, :] + sums
-        return carry
-
-    lax.fori_loop(0, blocks // join, add, 0)
+        target_ref[rows, :] = sums if first else base_ref[rows, :] + sums
+        if final:
+            copies.append(pltpu.make_async_copy(target_ref.at[rows, :], out_ref.at[rows, :], refs[5].at[group]))
+            copies[-1].start()
+    for copy in copies:
+        copy.wait()
 
 
 def shards(fact_x, dim_owner, dim_slot, fact_owner, fact_slot, dim_table, entity_h, w_msg, w_self, w_neigh, cotangent):
@@ -400,8 +425,6 @@
 
     if ringed:
         right, left = pass_on(dim_table, dim_table)
-    x_near = swap(fact_x, 1)
-
     by_lane = (chunks, LANES)
     columns = shape((facts, LANES), BF)
     asks, pos, entity, dlow, dhigh = call(
@@ -413,14 +436,14 @@
             columns,
             columns,
         ),
-        [],
+        [pltpu.VMEM(by_lane, jnp.int32)] * 4 + [pltpu.SemaphoreType.DMA((4,))],
         1 << 28,
         "route",
+        in_specs=[IN_HBM] * 4,
     )(dim_owner.reshape(by_lane), dim_slot.reshape(by_lane), fact_owner.reshape(by_lane), fact_slot.reshape(by_lane))
     if ringed:
-        right, left, x_near, asks, pos, entity, dlow, dhigh = tie(
-            (right, left, x_near, asks, pos, entity, dlow, dhigh)
-        )
+        asked = lax.all_to_all(asks, "fact", 0, 0)
+        right, left, asked, pos, entity, dlow, dhigh = tie((right, left, asked, pos, entity, dlow, dhigh))
 
     def look(pieces, tables, base):
         rows = sum(t.shape[0] for t in tables)
@@ -443,9 +466,9 @@
     if ringed:
         near = (right, left)
         after = pass_on(*near)
-        x_far = swap(fact_x, 2)
+        x_far, x_near = swap(fact_x, 2), swap(fact_x, 1)
         found = look([(0, 0, dims), (-1, 0, dims), (1, 0, dims)], [dim_table, *near], found)
-        right, left, x_far, found, weights = tie((*after, x_far, found, weights))
+        right, left, x_far, x_near, found, weights = tie((*after, x_far, x_near, found, weights))
         for k in range(2, n // 2 - 1):
             after = pass_on(right, left)
             x_last = swap(x_far, 1)
@@ -460,7 +483,8 @@
         found, all_far, all_near = tie((found, all_far, all_near))
         last, last_pieces = [after], [(n // 2, 0, dims)]
     else:
-        x_far = swap(fact_x, 2)
+        asked = lax.all_to_all(asks, "fact", 0, 0)
+        x_far, x_near = swap(fact_x, 2), swap(fact_x, 1)
         x_last = swap(x_far, 1)
         xw = project([fact_x, x_near, x_far, x_last])
         all_far, all_near = swap(weights, 2), swap(weights, 1)
@@ -471,7 +495,6 @@
         last, last_pieces = [], []
     all_last = swap(all_far, 1)
     x_blocks, all_blocks = [fact_x, x_near, x_far, x_last], [weights, all_near, all_far, all_last]
-    asked = lax.all_to_all(asks, "fact", 0, 0)
     last_rows = max(LANES, sum(t.shape[0] for t in last))
     slope, part = call(
         functools.partial(message_kernel, n, last_pieces),
@@ -482,12 +505,15 @@
             pltpu.VMEM((facts, LANES), BF),
             pltpu.VMEM((LANES, facts), BF),
             pltpu.VMEM((16, facts), BF),
+            *[pltpu.VMEM(t.shape, BF) for t in last],
+            pltpu.SemaphoreType.DMA,
             pltpu.SemaphoreType.DMA,
         ],
         2 * facts * (last_rows + n * ents) * LANES,
         "message",
         limit,
-        out_specs=(pl.BlockSpec(memory_space=pl.ANY), pl.BlockSpec(memory_space=pltpu.VMEM)),
+        in_specs=[IN_VMEM] * 2 + [pl.BlockSpec(memory_space=pl.ANY)] * len(last) + [IN_VMEM] * 3,
+        out_specs=(IN_HBM, IN_VMEM),
     )(dlow, dhigh, *last, found, xw, entity)
     sums = lax.all_to_all(part.reshape(n * m, rows_each, LANES), ("fact", "feat"), 0, 0)
     pos, entity, x_blocks, _ = tie((pos, entity, x_blocks, part))
@@ -502,9 +528,15 @@
     back, out_parts, pre_parts, agg_parts = call(
         functools.partial(entity_kernel, n, m, width, ents),
         (shape((n * m, rows_each, LANES), BF), by_feat, by_feat, shape((m * rows_each, LANES), BF)),
-        [pltpu.VMEM((m, rows_each, LANES), BF), pltpu.VMEM((ents, LANES), F32)],
+        [
+            pltpu.VMEM((m, rows_each, LANES), BF),
+            pltpu.VMEM((ents, LANES), F32),
+            pltpu.VMEM(asked.shape, jnp.int32),
+            pltpu.SemaphoreType.DMA,
+        ],
         6 * rows_each * width * width,
         "entity",
+        in_specs=[IN_VMEM, pl.BlockSpec(memory_space=pl.ANY)] + [IN_VMEM] * m,
     )(sums, asked, *all_blocks)
     scaled = lax.all_to_all(back, ("fact", "feat"), 0, 0).reshape(n * ents, LANES)
     shares = call(
@@ -551,7 +583,7 @@
         2 * facts * (n * ents + width) * LANES,
         "backward",
         limit,
-        in_specs=[pl.BlockSpec(memory_space=pl.ANY)] + [pl.BlockSpec(memory_space=pltpu.VMEM)] * 4,
+        in_specs=[IN_HBM] + [IN_VMEM] * 4,
     )(slope, scaled, elow, ehigh, x_turned)
 
     def spread(offsets):
@@ -563,7 +595,7 @@
             2 * facts * cap * LANES * len(offsets),
             "spread",
             limit,
-        )(plow, phigh, d_msg, msg_share, *(pairs if ringed else ()))
+        )(plow, phigh, d_msg, msg_share, *(pairs if max(lengths) > cap + stride else ()))
 
     def add_up(offsets, got, base, final):
         weight = shape((3 * stride, LANES), F32)
@@ -575,10 +607,20 @@
         return call(
             functools.partial(table_kernel, n, cap, stride, offsets, base is None, final),
             (shape((dims, LANES), F32),) + ((shape((own, LANES), F32),) * 3 if final else (weight,)),
-            scratch + ([pltpu.VMEM(weight.shape, F32)] if final else []),
+            scratch
+            + (
+                [
+                    pltpu.VMEM(weight.shape, F32),
+                    pltpu.VMEM((dims, LANES), F32),
+                    pltpu.SemaphoreType.DMA((dims // LANES,)),
+                ]
+                if final
+                else []
+            ),
             2 * cap * dims * LANES * len(got),
             "table",
             limit,
+            **(dict(out_specs=(IN_HBM, IN_VMEM, IN_VMEM, IN_VMEM)) if final else {}),
         )(rlow, rhigh, *got, *(base or ()))
 
     totals = None

time: 105 us -> 106 us (level)
  waiting for transfers between devices: 30.9 us -> 37.9 us
  starting transfers between devices: 41.2 us -> 38.2 us
  Pallas kernels: 24.5 us -> 22.4 us
  local copies, waits for them, and re-layouts: 6.93 us -> 5.47 us
    all_to_all x1, waiting for transfers between devices: 0.01 us -> 3.58 us  [shards(): asked = lax.all_to_all(asks, 'fact', 0, 0)]
    ppermute x9, waiting for transfers between devices: 3.97 us -> 7.28 us  [swap(): return lax.ppermute(block, 'feat', [(i, i ^ bit) for i in range(m)])]
    all_to_all x1, starting transfers between devices: 5.8 us -> 3.16 us  [shards(): lax.all_to_all(part.reshape(n * m, rows_each, LANES), ('fact', 'feat'), 0...]
    ppermute x7, waiting for transfers between devices: 9.5 us -> 11.8 us  [shards(): lax.ppermute(message, 'fact', [(i, (i + offset) % n) for i in range(n)])]
    ppermute x3, waiting for transfers between devices: 3.57 us -> 1.55 us  [pass_on(): lax.ppermute(right, 'fact', to_right)]
    ppermute x1, waiting for transfers between devices: 0.01 us -> 1.96 us  [shards(): after = lax.ppermute(right, 'fact', to_right)]
    ppermute x1, waiting for transfers between devices: 1.82 us -> 0.01 us  [shards(): pairs = [keep, lax.ppermute(give, 'fact', [(i, i ^ 1) for i in range(n)])]]
    ppermute x3, starting transfers between devices: 2.77 us -> 4.46 us  [pass_on(): lax.ppermute(left, 'fact', to_left)]
  transfers between devices with their start and end apart: 27 -> 27, of which waited for: 16 -> 16; matrix products, arithmetic and copies ran while one was open for 0% -> 0% of each run, Pallas kernels for 20% -> 15%
where the time goes in v2:
time: 106 us; the launch traced here: 105 us
  starting transfers between devices  38.2 us (36%)
  waiting for transfers between devices  37.9 us (36%)
  Pallas kernels  22.4 us (21%)
  local copies, waits for them, and re-layouts  5.47 us (5%)
  between operations  1.11 us (1%)
    ppermute x7, starting transfers between devices, shards(): lax.ppermute(message, 'fact', [(i, (i + offset) % n) for i in range(n)])  12.8 us
    ppermute x7, waiting for transfers between devices, shards(): lax.ppermute(message, 'fact', [(i, (i + offset) % n) for i in range(n)])  11.8 us
    all_to_all x1, waiting for transfers between devices, shards(): lax.all_to_all(part.reshape(n * m, rows_each, LANES), ('fact', 'feat'), 0...  8.02 us
    ppermute x9, waiting for transfers between devices, swap(): return lax.ppermute(block, 'feat', [(i, i ^ bit) for i in range(m)])  7.28 us
    all_to_all x1, starting transfers between devices, shards(): asked = lax.all_to_all(asks, 'fact', 0, 0)  6.35 us
    pallas_call x3, Pallas kernels, look(): call(functools.partial(look_kernel, n, pieces), shape((facts, LANES), F32...  6.16 us
    unnamed x30, local copies, waits for them, and re-layouts  5.44 us
    ppermute x9, starting transfers between devices, swap(): return lax.ppermute(block, 'feat', [(i, i ^ bit) for i in range(m)])  5.35 us
  transfers between devices with their start and end apart: 27, of which 16 were waited for; matrix products, arithmetic and copies ran while one was open for 0% of the time, Pallas kernels for 15%

profile of v2, /device:TPU:4, one launch (start us, length us, event | category | flops | bytes accessed | tf_op | source)
XLA Modules:
  0.0 105.1 jit_solution(17440680463995025382)
XLA Ops:
  0.7 2.0 %collective-permute-start.1 = (bf16[1024,128]{1,0:T(8,128)(2,1)}, bf16[1024,128]{1,0:T(8,128)(2,1)S(1)}, u32[]{:S(2)}, u32[]{:S(2)}) collective-permute-start(bf16[1024,128]{1,0:T(8,128)(2,1)} %refs_0_.2), channel_id=1, source_target_pairs={{8,0},{16,8},{24,16},{28,24},{20,28},{12,20},{4,12},{0,4},{9,1},{1... | collective-permute-start | bytes 786440 | tf_op jit(solution)/shard_map/ppermute | solution.py:421
  4.8 1.8 %route.1 = (s32[8,4,128]{2,1,0:T(4,128)}, s32[8,128]{1,0:T(8,128)S(1)}, s32[8,128]{1,0:T(8,128)S(1)}, bf16[1024,128]{1,0:T(8,128)(2,1)S(1)}, bf16[1024,128]{1,0:T(8,128)(2,1)S(1)}) custom-call(s32[8,128]{1,0:T(8,128)S(1)} %bitcast.7, s32[8,128]{1,0:T(8,128)S(1)} %bitcast.8, s32[8,128]{1,0:T(8,128)S(1)} %bitcast.9, s32[8,128]{1,0:T(8,128)S(1)} %bitcast.10), custom_call_target="tpu_custom_call" | custom-call | flops 268435456 | bytes 1048576 | tf_op jit(solution)/shard_map/route/pallas_call | solution.py:430
  6.6 6.3 %all-to-all-start = ((s32[8,4,128]{2,1,0:T(4,128)}), s32[8,4,128]{2,1,0:T(4,128)S(1)}, u32[]{:S(2)}, u32[]{:S(2)}) async-start(s32[8,4,128]{2,1,0:T(4,128)} %get-tuple-element.79), calls=%async_computation | async-start | bytes 32768 | tf_op jit(solution)/shard_map/all_to_all | solution.py:445
  14.4 3.6 %all-to-all-done.idx_ref.req_ref = s32[8,4,128]{2,1,0:T(4,128)S(1)} async-done(((s32[8,4,128]{2,1,0:T(4,128)}), s32[8,4,128]{2,1,0:T(4,128)S(1)}, u32[]{:S(2)}, u32[]{:S(2)}) %all-to-all-start) | async-done | bytes 16416 | tf_op jit(solution)/shard_map/all_to_all | solution.py:445
  21.1 2.6 %look.3.refs_2_ = f32[1024,128]{1,0:T(8,128)S(1)} custom-call(bf16[1024,128]{1,0:T(8,128)(2,1)S(1)} %get-tuple-element.88.low_ref, bf16[1024,128]{1,0:T(8,128)(2,1)S(1)} %get-tuple-element.89.high_ref, bf16[1024,128]{1,0:T(8,128)(2,1)S(1)} %copy-done.6, bf16[1024,128]{1,0:T(8,128)(2,1)S(1)} %collective-permute-done.refs_1_, ...), custom_call_target="tpu_custom_call" | custom-call | flops 805306368 | bytes 1048576 | tf_op jit(solution)/shard_map/look/pallas_call | solution.py:450
  24.4 2.1 %collective-permute-done.3.refs_1_ = bf16[1024,128]{1,0:T(8,128)(2,1)S(1)} collective-permute-done((bf16[1024,128]{1,0:T(8,128)(2,1)S(1)}, bf16[1024,128]{1,0:T(8,128)(2,1)S(1)}, u32[]{:S(2)}, u32[]{:S(2)}) %collective-permute-start.3) | collective-permute-done | bytes 262176 | tf_op jit(solution)/shard_map/ppermute | solution.py:421
  26.6 1.9 %collective-permute-start.7 = (bf16[1024,128]{1,0:T(8,128)(2,1)S(1)}, bf16[1024,128]{1,0:T(8,128)(2,1)S(1)}, u32[]{:S(2)}, u32[]{:S(2)}) collective-permute-start(bf16[1024,128]{1,0:T(8,128)(2,1)S(1)} %collective-permute-done.3.refs_1_), channel_id=1, source_target_pairs={{8,0},{16,8},{24,16},{28,24},{20,28},{12,20},{4,12},{0,4},{9,1},{1... | collective-permute-start | bytes 786440 | tf_op jit(solution)/shard_map/ppermute | solution.py:421
  30.3 1.8 %look.4.refs_2_ = f32[1024,128]{1,0:T(8,128)S(1)} custom-call(bf16[1024,128]{1,0:T(8,128)(2,1)S(1)} %get-tuple-element.88.low_ref, bf16[1024,128]{1,0:T(8,128)(2,1)S(1)} %get-tuple-element.89.high_ref, bf16[1024,128]{1,0:T(8,128)(2,1)S(1)} %collective-permute-done.2.refs_0_, bf16[1024,128]{1,0:T(8,128)(2,1)S(1)} %collective-permute-done.3.refs_1_, ...), custom_call_target="tpu_custom_call" | custom-call | flops 536870912 | bytes 1048576 | tf_op jit(solution)/shard_map/look/pallas_call | solution.py:450
  34.5 1.8 %look.5.refs_1_ = f32[1024,128]{1,0:T(8,128)S(1)} custom-call(bf16[1024,128]{1,0:T(8,128)(2,1)S(1)} %get-tuple-element.88.low_ref, bf16[1024,128]{1,0:T(8,128)(2,1)S(1)} %get-tuple-element.89.high_ref, bf16[1024,128]{1,0:T(8,128)(2,1)S(1)} %collective-permute-done.6.refs_0_, bf16[1024,128]{1,0:T(8,128)(2,1)S(1)} %collective-permute-done.7.refs_1_, ...), custom_call_target="tpu_custom_call" | custom-call | flops 536870912 | bytes 1048576 | tf_op jit(solution)/shard_map/look/pallas_call | solution.py:450
  36.3 2.4 %collective-permute-done.10.refs_6_.refs_2_ = bf16[1280,128]{1,0:T(8,128)(2,1)S(1)} collective-permute-done((bf16[1280,128]{1,0:T(8,128)(2,1)S(1)}, bf16[1280,128]{1,0:T(8,128)(2,1)S(1)}, u32[]{:S(2)}, u32[]{:S(2)}) %collective-permute-start.10) | collective-permute-done | bytes 327712 | tf_op jit(solution)/shard_map/ppermute | solution.py:424
  38.7 2.0 %collective-permute-done.9.refs_0_ = bf16[1024,128]{1,0:T(8,128)(2,1)S(1)} collective-permute-done((bf16[1024,128]{1,0:T(8,128)(2,1)S(1)}, bf16[1024,128]{1,0:T(8,128)(2,1)S(1)}, u32[]{:S(2)}, u32[]{:S(2)}) %collective-permute-start.9) | collective-permute-done | bytes 262176 | tf_op jit(solution)/shard_map/ppermute | solution.py:479
  40.7 3.0 %message.1 = (f32[1024,128]{1,0:T(8,128)S(1)}, bf16[1024,128]{1,0:T(8,128)(2,1)}) custom-call(bf16[1024,128]{1,0:T(8,128)(2,1)S(1)} %get-tuple-element.88.low_ref, bf16[1024,128]{1,0:T(8,128)(2,1)S(1)} %get-tuple-element.89.high_ref, bf16[1024,128]{1,0:T(8,128)(2,1)S(1)} %collective-permute-done.9.refs_0_, f32[1024,128]{1,0:T(8,128)S(1)} %look.5.refs_1_, ...), custom_call_target="tpu_custom_call" | custom-call | flops 536870912 | bytes 1048576 | tf_op jit(solution)/shard_map/message/pallas_call | solution.py:499
  44.5 3.2 %all-to-all-start.1 = ((bf16[32,32,128]{2,1,0:T(8,128)(2,1)}), bf16[32,32,128]{2,1,0:T(8,128)(2,1)S(1)}, u32[]{:S(2)}, u32[]{:S(2)}) async-start(bf16[32,32,128]{2,1,0:T(8,128)(2,1)} %bitcast.4), calls=%async_computation.1 | async-start | bytes 524288 | tf_op jit(solution)/shard_map/all_to_all | solution.py:518
  49.3 8.0 %all-to-all-done.1.sums_ref = bf16[32,32,128]{2,1,0:T(8,128)(2,1)S(1)} async-done(((bf16[32,32,128]{2,1,0:T(8,128)(2,1)}), bf16[32,32,128]{2,1,0:T(8,128)(2,1)S(1)}, u32[]{:S(2)}, u32[]{:S(2)}) %all-to-all-start.1) | async-done | bytes 262176 | tf_op jit(solution)/shard_map/all_to_all | solution.py:518
  59.0 3.4 %all-to-all-start.2 = ((bf16[32,32,128]{2,1,0:T(8,128)(2,1)}), bf16[32,32,128]{2,1,0:T(8,128)(2,1)S(1)}, u32[]{:S(2)}, u32[]{:S(2)}) async-start(bf16[32,32,128]{2,1,0:T(8,128)(2,1)} %get-tuple-element.120), calls=%async_computation.2 | async-start | bytes 524288 | tf_op jit(solution)/shard_map/all_to_all | solution.py:541
  65.6 2.8 %collective-permute-done.14.refs_2_ = bf16[192,128]{1,0:T(8,128)(2,1)S(1)} collective-permute-done((bf16[192,128]{1,0:T(8,128)(2,1)S(1)}, bf16[192,128]{1,0:T(8,128)(2,1)S(1)}, u32[]{:S(2)}, u32[]{:S(2)}) %collective-permute-start.14) | collective-permute-done | bytes 49184 | tf_op jit(solution)/shard_map/ppermute | solution.py:424
  76.9 2.1 %collective-permute-start.21 = (bf16[576,128]{1,0:T(8,128)(2,1)S(1)}, bf16[576,128]{1,0:T(8,128)(2,1)S(1)}, u32[]{:S(2)}, u32[]{:S(2)}) collective-permute-start(bf16[576,128]{1,0:T(8,128)(2,1)S(1)} %spread.7), channel_id=1, source_target_pairs={{0,16},{4,20},{8,24},{12,28},{16,0},{20,4},{24,8},{28,12},{1,17},{... | collective-permute-start | bytes 442376 | tf_op jit(solution)/shard_map/ppermute | solution.py:632
  81.3 2.1 %collective-permute-start.20 = (bf16[576,128]{1,0:T(8,128)(2,1)S(1)}, bf16[576,128]{1,0:T(8,128)(2,1)S(1)}, u32[]{:S(2)}, u32[]{:S(2)}) collective-permute-start(bf16[576,128]{1,0:T(8,128)(2,1)S(1)} %get-tuple-element.140), channel_id=1, source_target_pairs={{0,24},{4,28},{8,0},{12,4},{16,8},{20,12},{24,16},{28,20},{1,25},{... | collective-permute-start | bytes 442376 | tf_op jit(solution)/shard_map/ppermute | solution.py:632
  84.1 2.4 %collective-permute-start.16 = (bf16[448,128]{1,0:T(8,128)(2,1)S(1)}, bf16[448,128]{1,0:T(8,128)(2,1)S(1)}, u32[]{:S(2)}, u32[]{:S(2)}) collective-permute-start(bf16[448,128]{1,0:T(8,128)(2,1)S(1)} %get-tuple-element.134), channel_id=1, source_target_pairs={{0,12},{4,16},{8,20},{12,24},{16,28},{20,0},{24,4},{28,8},{1,13},{... | collective-permute-start | bytes 344072 | tf_op jit(solution)/shard_map/ppermute | solution.py:632
  86.5 2.4 %collective-permute-start.17 = (bf16[448,128]{1,0:T(8,128)(2,1)S(1)}, bf16[448,128]{1,0:T(8,128)(2,1)S(1)}, u32[]{:S(2)}, u32[]{:S(2)}) collective-permute-start(bf16[448,128]{1,0:T(8,128)(2,1)S(1)} %get-tuple-element.135), channel_id=1, source_target_pairs={{0,20},{4,24},{8,28},{12,0},{16,4},{20,8},{24,12},{28,16},{1,21},{... | collective-permute-start | bytes 344072 | tf_op jit(solution)/shard_map/ppermute | solution.py:632
  90.2 2.3 %collective-permute-done.21.refs_0_ = bf16[576,128]{1,0:T(8,128)(2,1)S(1)} collective-permute-done((bf16[576,128]{1,0:T(8,128)(2,1)S(1)}, bf16[576,128]{1,0:T(8,128)(2,1)S(1)}, u32[]{:S(2)}, u32[]{:S(2)}) %collective-permute-start.21) | collective-permute-done | bytes 147488 | tf_op jit(solution)/shard_map/ppermute | solution.py:632
  94.0 2.6 %collective-permute-done.16.refs_0_ = bf16[448,128]{1,0:T(8,128)(2,1)S(1)} collective-permute-done((bf16[448,128]{1,0:T(8,128)(2,1)S(1)}, bf16[448,128]{1,0:T(8,128)(2,1)S(1)}, u32[]{:S(2)}, u32[]{:S(2)}) %collective-permute-start.16) | collective-permute-done | bytes 114720 | tf_op jit(solution)/shard_map/ppermute | solution.py:632
  96.6 6.4 %collective-permute-done.17.refs_1_ = bf16[448,128]{1,0:T(8,128)(2,1)S(1)} collective-permute-done((bf16[448,128]{1,0:T(8,128)(2,1)S(1)}, bf16[448,128]{1,0:T(8,128)(2,1)S(1)}, u32[]{:S(2)}, u32[]{:S(2)}) %collective-permute-start.17) | collective-permute-done | bytes 114720 | tf_op jit(solution)/shard_map/ppermute | solution.py:632
  103.0 2.0 %table.7 = (f32[1024,128]{1,0:T(8,128)}, f32[64,128]{1,0:T(8,128)}, f32[64,128]{1,0:T(8,128)}, f32[64,128]{1,0:T(8,128)}) custom-call(bf16[128,3072]{1,0:T(8,128)(2,1)S(1)} %get-tuple-element.122.low_ref, bf16[16,3072]{1,0:T(8,128)(2,1)S(1)} %get-tuple-element.123.high_ref, bf16[448,128]{1,0:T(8,128)(2,1)S(1)} %collective-permute-done.16.refs_0_, ...), custom_call_target="tpu_custom_call" | custom-call | flops 201326592 | bytes 1048576 | tf_op jit(solution)/shard_map/table/pallas_call | solution.py:607
  (85 shorter events, 33.2 us)
Async XLA Ops:
  0.6 17.4 %collective-permute-start = (bf16[1024,128]{1,0:T(8,128)(2,1)}, bf16[1024,128]{1,0:T(8,128)(2,1)S(1)}, u32[]{:S(2)}, u32[]{:S(2)}) collective-permute-start(bf16[1024,128]{1,0:T(8,128)(2,1)} %refs_0_.2), channel_id=1, source_target_pairs={{0,8},{8,16},{16,24},{24,28},{28,20},{20,12},{12,4},{4,0},{1,9},{9... | collective-permute-start | bytes 786440 | tf_op jit(solution)/shard_map/ppermute | solution.py:421
  0.7 17.3 %collective-permute-start.1 = (bf16[1024,128]{1,0:T(8,128)(2,1)}, bf16[1024,128]{1,0:T(8,128)(2,1)S(1)}, u32[]{:S(2)}, u32[]{:S(2)}) collective-permute-start(bf16[1024,128]{1,0:T(8,128)(2,1)} %refs_0_.2), channel_id=1, source_target_pairs={{8,0},{16,8},{24,16},{28,24},{20,28},{12,20},{4,12},{0,4},{9,1},{1... | collective-permute-start | bytes 786440 | tf_op jit(solution)/shard_map/ppermute | solution.py:421
  6.6 11.4 %all-to-all-start = ((s32[8,4,128]{2,1,0:T(4,128)}), s32[8,4,128]{2,1,0:T(4,128)S(1)}, u32[]{:S(2)}, u32[]{:S(2)}) async-start(s32[8,4,128]{2,1,0:T(4,128)} %get-tuple-element.79), calls=%async_computation | async-start | bytes 32768 | tf_op jit(solution)/shard_map/all_to_all | solution.py:445
  13.0 10.7 %collective-permute-start.4 = (bf16[1024,128]{1,0:T(8,128)(2,1)S(1)}, bf16[1024,128]{1,0:T(8,128)(2,1)S(1)}, u32[]{:S(2)}, u32[]{:S(2)}) collective-permute-start(bf16[1024,128]{1,0:T(8,128)(2,1)S(1)} %copy-done), channel_id=1, source_target_pairs={{0,2},{1,3},{2,0},{3,1},{4,6},{5,7},{6,4},{7,5},{8,10},{9,11},{10,... | collective-permute-start | bytes 786440 | tf_op jit(solution)/shard_map/ppermute | solution.py:424
  14.4 9.2 %collective-permute-start.5 = (bf16[1024,128]{1,0:T(8,128)(2,1)S(1)}, bf16[1024,128]{1,0:T(8,128)(2,1)S(1)}, u32[]{:S(2)}, u32[]{:S(2)}) collective-permute-start(bf16[1024,128]{1,0:T(8,128)(2,1)S(1)} %copy-done), channel_id=1, source_target_pairs={{0,1},{1,0},{2,3},{3,2},{4,5},{5,4},{6,7},{7,6},{8,9},{9,8},{10,11... | collective-permute-start | bytes 786440 | tf_op jit(solution)/shard_map/ppermute | solution.py:424
  18.0 6.4 %collective-permute-start.2 = (bf16[1024,128]{1,0:T(8,128)(2,1)S(1)}, bf16[1024,128]{1,0:T(8,128)(2,1)S(1)}, u32[]{:S(2)}, u32[]{:S(2)}) collective-permute-start(bf16[1024,128]{1,0:T(8,128)(2,1)S(1)} %collective-permute-done.refs_1_), channel_id=1, source_target_pairs={{0,8},{8,16},{16,24},{24,28},{28,20},{20,12},{12,4},{4,0},{1,9},{9... | collective-permute-start | bytes 786440 | tf_op jit(solution)/shard_map/ppermute | solution.py:421
  19.5 7.0 %collective-permute-start.3 = (bf16[1024,128]{1,0:T(8,128)(2,1)S(1)}, bf16[1024,128]{1,0:T(8,128)(2,1)S(1)}, u32[]{:S(2)}, u32[]{:S(2)}) collective-permute-start(bf16[1024,128]{1,0:T(8,128)(2,1)S(1)} %collective-permute-done.1.refs_2_), channel_id=1, source_target_pairs={{8,0},{16,8},{24,16},{28,24},{20,28},{12,20},{4,12},{0,4},{9,1},{1... | collective-permute-start | bytes 786440 | tf_op jit(solution)/shard_map/ppermute | solution.py:421
  26.5 6.4 %collective-permute-start.6 = (bf16[1024,128]{1,0:T(8,128)(2,1)S(1)}, bf16[1024,128]{1,0:T(8,128)(2,1)S(1)}, u32[]{:S(2)}, u32[]{:S(2)}) collective-permute-start(bf16[1024,128]{1,0:T(8,128)(2,1)S(1)} %collective-permute-done.2.refs_0_), channel_id=1, source_target_pairs={{0,8},{8,16},{16,24},{24,28},{28,20},{20,12},{12,4},{4,0},{1,9},{9... | collective-permute-start | bytes 786440 | tf_op jit(solution)/shard_map/ppermute | solution.py:421
  26.6 6.4 %collective-permute-start.7 = (bf16[1024,128]{1,0:T(8,128)(2,1)S(1)}, bf16[1024,128]{1,0:T(8,128)(2,1)S(1)}, u32[]{:S(2)}, u32[]{:S(2)}) collective-permute-start(bf16[1024,128]{1,0:T(8,128)(2,1)S(1)} %collective-permute-done.3.refs_1_), channel_id=1, source_target_pairs={{8,0},{16,8},{24,16},{28,24},{20,28},{12,20},{4,12},{0,4},{9,1},{1... | collective-permute-start | bytes 786440 | tf_op jit(solution)/shard_map/ppermute | solution.py:421
  28.6 10.1 %collective-permute-start.10 = (bf16[1280,128]{1,0:T(8,128)(2,1)S(1)}, bf16[1280,128]{1,0:T(8,128)(2,1)S(1)}, u32[]{:S(2)}, u32[]{:S(2)}) collective-permute-start(bf16[1280,128]{1,0:T(8,128)(2,1)S(1)} %pad_maximum_fusion.refs_4_.refs_0_), channel_id=1, source_target_pairs={{0,2},{1,3},{2,0},{3,1},{4,6},{5,7},{6,4},{7,5},{8,10},{9,11},{10,... | collective-permute-start | bytes 983048 | tf_op jit(solution)/shard_map/ppermute | solution.py:424
  30.1 8.6 %collective-permute-start.11 = (bf16[1280,128]{1,0:T(8,128)(2,1)S(1)}, bf16[1280,128]{1,0:T(8,128)(2,1)S(1)}, u32[]{:S(2)}, u32[]{:S(2)}) collective-permute-start(bf16[1280,128]{1,0:T(8,128)(2,1)S(1)} %pad_maximum_fusion.refs_4_.refs_0_), channel_id=1, source_target_pairs={{0,1},{1,0},{2,3},{3,2},{4,5},{5,4},{6,7},{7,6},{8,9},{9,8},{10,11... | collective-permute-start | bytes 983048 | tf_op jit(solution)/shard_map/ppermute | solution.py:424
  33.0 7.6 %collective-permute-start.9 = (bf16[1024,128]{1,0:T(8,128)(2,1)S(1)}, bf16[1024,128]{1,0:T(8,128)(2,1)S(1)}, u32[]{:S(2)}, u32[]{:S(2)}) collective-permute-start(bf16[1024,128]{1,0:T(8,128)(2,1)S(1)} %collective-permute-done.6.refs_0_), channel_id=1, source_target_pairs={{0,8},{8,16},{16,24},{24,28},{28,20},{20,12},{12,4},{4,0},{1,9},{9... | collective-permute-start | bytes 786440 | tf_op jit(solution)/shard_map/ppermute | solution.py:479
  44.5 12.9 %all-to-all-start.1 = ((bf16[32,32,128]{2,1,0:T(8,128)(2,1)}), bf16[32,32,128]{2,1,0:T(8,128)(2,1)S(1)}, u32[]{:S(2)}, u32[]{:S(2)}) async-start(bf16[32,32,128]{2,1,0:T(8,128)(2,1)} %bitcast.4), calls=%async_computation.1 | async-start | bytes 524288 | tf_op jit(solution)/shard_map/all_to_all | solution.py:518
  59.0 13.2 %all-to-all-start.2 = ((bf16[32,32,128]{2,1,0:T(8,128)(2,1)}), bf16[32,32,128]{2,1,0:T(8,128)(2,1)S(1)}, u32[]{:S(2)}, u32[]{:S(2)}) async-start(bf16[32,32,128]{2,1,0:T(8,128)(2,1)} %get-tuple-element.120), calls=%async_computation.2 | async-start | bytes 524288 | tf_op jit(solution)/shard_map/all_to_all | solution.py:541
  62.6 5.8 %collective-permute-start.14 = (bf16[192,128]{1,0:T(8,128)(2,1)S(1)}, bf16[192,128]{1,0:T(8,128)(2,1)S(1)}, u32[]{:S(2)}, u32[]{:S(2)}) collective-permute-start(bf16[192,128]{1,0:T(8,128)(2,1)S(1)} %get-tuple-element.115), channel_id=1, source_target_pairs={{0,2},{1,3},{2,0},{3,1},{4,6},{5,7},{6,4},{7,5},{8,10},{9,11},{10,... | collective-permute-start | bytes 147464 | tf_op jit(solution)/shard_map/ppermute | solution.py:424
  64.1 4.9 %collective-permute-start.15 = (bf16[192,128]{1,0:T(8,128)(2,1)S(1)}, bf16[192,128]{1,0:T(8,128)(2,1)S(1)}, u32[]{:S(2)}, u32[]{:S(2)}) collective-permute-start(bf16[192,128]{1,0:T(8,128)(2,1)S(1)} %get-tuple-element.116), channel_id=1, source_target_pairs={{0,3},{1,2},{2,1},{3,0},{4,7},{5,6},{6,5},{7,4},{8,11},{9,10},{10,... | collective-permute-start | bytes 147464 | tf_op jit(solution)/shard_map/ppermute | solution.py:424
  69.8 6.7 %collective-permute-start.18 = (bf16[4,128,128]{2,1,0:T(8,128)(2,1)S(1)}, bf16[4,128,128]{2,1,0:T(8,128)(2,1)S(1)}, u32[]{:S(2)}, u32[]{:S(2)}) collective-permute-start(bf16[4,128,128]{2,1,0:T(8,128)(2,1)S(1)} %get-tuple-element.138), channel_id=1, source_target_pairs={{0,4},{4,0},{8,12},{12,8},{16,20},{20,16},{24,28},{28,24},{1,5},{5... | collective-permute-start | bytes 393224 | tf_op jit(solution)/shard_map/ppermute | solution.py:576
  74.4 9.6 %collective-permute-start.22 = (bf16[448,128]{1,0:T(8,128)(2,1)S(1)}, bf16[448,128]{1,0:T(8,128)(2,1)S(1)}, u32[]{:S(2)}, u32[]{:S(2)}) collective-permute-start(bf16[448,128]{1,0:T(8,128)(2,1)S(1)} %get-tuple-element.141), channel_id=1, source_target_pairs={{0,4},{4,8},{8,12},{12,16},{16,20},{20,24},{24,28},{28,0},{1,5},{5... | collective-permute-start | bytes 344072 | tf_op jit(solution)/shard_map/ppermute | solution.py:632
  76.0 10.5 %collective-permute-start.23 = (bf16[448,128]{1,0:T(8,128)(2,1)S(1)}, bf16[448,128]{1,0:T(8,128)(2,1)S(1)}, u32[]{:S(2)}, u32[]{:S(2)}) collective-permute-start(bf16[448,128]{1,0:T(8,128)(2,1)S(1)} %get-tuple-element.142), channel_id=1, source_target_pairs={{0,28},{4,0},{8,4},{12,8},{16,12},{20,16},{24,20},{28,24},{1,29},{... | collective-permute-start | bytes 344072 | tf_op jit(solution)/shard_map/ppermute | solution.py:632
  76.9 15.6 %collective-permute-start.21 = (bf16[576,128]{1,0:T(8,128)(2,1)S(1)}, bf16[576,128]{1,0:T(8,128)(2,1)S(1)}, u32[]{:S(2)}, u32[]{:S(2)}) collective-permute-start(bf16[576,128]{1,0:T(8,128)(2,1)S(1)} %spread.7), channel_id=1, source_target_pairs={{0,16},{4,20},{8,24},{12,28},{16,0},{20,4},{24,8},{28,12},{1,17},{... | collective-permute-start | bytes 442376 | tf_op jit(solution)/shard_map/ppermute | solution.py:632
  79.6 13.3 %collective-permute-start.19 = (bf16[576,128]{1,0:T(8,128)(2,1)S(1)}, bf16[576,128]{1,0:T(8,128)(2,1)S(1)}, u32[]{:S(2)}, u32[]{:S(2)}) collective-permute-start(bf16[576,128]{1,0:T(8,128)(2,1)S(1)} %get-tuple-element.139), channel_id=1, source_target_pairs={{0,8},{4,12},{8,16},{12,20},{16,24},{20,28},{24,0},{28,4},{1,9},{5... | collective-permute-start | bytes 442376 | tf_op jit(solution)/shard_map/ppermute | solution.py:632
  81.3 12.1 %collective-permute-start.20 = (bf16[576,128]{1,0:T(8,128)(2,1)S(1)}, bf16[576,128]{1,0:T(8,128)(2,1)S(1)}, u32[]{:S(2)}, u32[]{:S(2)}) collective-permute-start(bf16[576,128]{1,0:T(8,128)(2,1)S(1)} %get-tuple-element.140), channel_id=1, source_target_pairs={{0,24},{4,28},{8,0},{12,4},{16,8},{20,12},{24,16},{28,20},{1,25},{... | collective-permute-start | bytes 442376 | tf_op jit(solution)/shard_map/ppermute | solution.py:632
  84.1 12.5 %collective-permute-start.16 = (bf16[448,128]{1,0:T(8,128)(2,1)S(1)}, bf16[448,128]{1,0:T(8,128)(2,1)S(1)}, u32[]{:S(2)}, u32[]{:S(2)}) collective-permute-start(bf16[448,128]{1,0:T(8,128)(2,1)S(1)} %get-tuple-element.134), channel_id=1, source_target_pairs={{0,12},{4,16},{8,20},{12,24},{16,28},{20,0},{24,4},{28,8},{1,13},{... | collective-permute-start | bytes 344072 | tf_op jit(solution)/shard_map/ppermute | solution.py:632
  86.5 16.5 %collective-permute-start.17 = (bf16[448,128]{1,0:T(8,128)(2,1)S(1)}, bf16[448,128]{1,0:T(8,128)(2,1)S(1)}, u32[]{:S(2)}, u32[]{:S(2)}) collective-permute-start(bf16[448,128]{1,0:T(8,128)(2,1)S(1)} %get-tuple-element.135), channel_id=1, source_target_pairs={{0,20},{4,24},{8,28},{12,0},{16,4},{20,8},{24,12},{28,16},{1,21},{... | collective-permute-start | bytes 344072 | tf_op jit(solution)/shard_map/ppermute | solution.py:632
  (18 other events, 97.3 us)

commit v3 on v2

--- a/solution.py
+++ b/solution.py
@@ -373,13 +373,18 @@
         khigh_ref[:, here] = high_ref[:, there]
         rows = ref.shape[0] - cap
         weight_ref[0:rows, :] += ref[cap:, :].astype(F32)
+    copies = []
     for which, ref in enumerate(final_refs):
-        ref[...] = weight_ref[which * stride : which * stride + ref.shape[0], :]
+        copies.append(
+            pltpu.make_async_copy(
+                weight_ref.at[which * stride : which * stride + ref.shape[0], :], ref, refs[6].at[which]
+            )
+        )
+        copies[-1].start()
     blocks = out_ref.shape[0] // LANES
     join = 2 if blocks % 2 == 0 else 1
 
     target_ref = refs[4] if final else out_ref
-    copies = []
     for group in range(blocks // join):
         hot = jnp.concatenate(
             [pick_rows(klow_ref[...], khigh_ref[...], jnp.array(group * join + i, BF)) for i in range(join)], axis=0
@@ -425,6 +430,7 @@
 
     if ringed:
         right, left = pass_on(dim_table, dim_table)
+    x_near = swap(fact_x, 1)
     by_lane = (chunks, LANES)
     columns = shape((facts, LANES), BF)
     asks, pos, entity, dlow, dhigh = call(
@@ -442,8 +448,9 @@
         in_specs=[IN_HBM] * 4,
     )(dim_owner.reshape(by_lane), dim_slot.reshape(by_lane), fact_owner.reshape(by_lane), fact_slot.reshape(by_lane))
     if ringed:
-        asked = lax.all_to_all(asks, "fact", 0, 0)
-        right, left, asked, pos, entity, dlow, dhigh = tie((right, left, asked, pos, entity, dlow, dhigh))
+        right, left, x_near, asks, pos, entity, dlow, dhigh = tie(
+            (right, left, x_near, asks, pos, entity, dlow, dhigh)
+        )
 
     def look(pieces, tables, base):
         rows = sum(t.shape[0] for t in tables)
@@ -466,9 +473,9 @@
     if ringed:
         near = (right, left)
         after = pass_on(*near)
-        x_far, x_near = swap(fact_x, 2), swap(fact_x, 1)
+        x_far = swap(fact_x, 2)
         found = look([(0, 0, dims), (-1, 0, dims), (1, 0, dims)], [dim_table, *near], found)
-        right, left, x_far, x_near, found, weights = tie((*after, x_far, x_near, found, weights))
+        right, left, x_far, found, weights = tie((*after, x_far, found, weights))
         for k in range(2, n // 2 - 1):
             after = pass_on(right, left)
             x_last = swap(x_far, 1)
@@ -478,13 +485,16 @@
         k = n // 2 - 1
         after = lax.ppermute(right, "fact", to_right)
         xw = project([fact_x, x_near, x_far, x_last])
-        found = look([(-k, 0, dims), (k, 0, dims)], [right, left], found)
+        found = look([(k, 0, dims)], [left], found)
+        found, asks = tie((found, asks))
+        asked = lax.all_to_all(asks, "fact", 0, 0)
+        found = look([(-k, 0, dims)], [right], found)
         all_near = swap(weights, 1)
         found, all_far, all_near = tie((found, all_far, all_near))
         last, last_pieces = [after], [(n // 2, 0, dims)]
     else:
         asked = lax.all_to_all(asks, "fact", 0, 0)
-        x_far, x_near = swap(fact_x, 2), swap(fact_x, 1)
+        x_far = swap(fact_x, 2)
         x_last = swap(x_far, 1)
         xw = project([fact_x, x_near, x_far, x_last])
         all_far, all_near = swap(weights, 2), swap(weights, 1)
@@ -498,7 +508,7 @@
     last_rows = max(LANES, sum(t.shape[0] for t in last))
     slope, part = call(
         functools.partial(message_kernel, n, last_pieces),
-        (shape((facts, LANES), F32), shape((n * ents, LANES), BF)),
+        (pltpu.HBM((facts, LANES), F32), shape((n * ents, LANES), BF)),
         [
             pltpu.VMEM((facts, LANES), F32),
             pltpu.VMEM((step, last_rows), BF),
@@ -613,6 +623,7 @@
                     pltpu.VMEM(weight.shape, F32),
                     pltpu.VMEM((dims, LANES), F32),
                     pltpu.SemaphoreType.DMA((dims // LANES,)),
+                    pltpu.SemaphoreType.DMA((3,)),
                 ]
                 if final
                 else []
@@ -620,7 +631,7 @@
             2 * cap * dims * LANES * len(got),
             "table",
             limit,
-            **(dict(out_specs=(IN_HBM, IN_VMEM, IN_VMEM, IN_VMEM)) if final else {}),
+            **(dict(out_specs=(IN_HBM,) * 4) if final else {}),
         )(rlow, rhigh, *got, *(base or ()))
 
     totals = None

time: 106 us -> 101 us (0.953)
  waiting for transfers between devices: 37.9 us -> 31.3 us
  starting transfers between devices: 38.2 us -> 40.6 us
    all_to_all x1, waiting for transfers between devices: 3.58 us -> 0.01 us  [shards(): asked = lax.all_to_all(asks, 'fact', 0, 0)]
    ppermute x9, waiting for transfers between devices: 7.28 us -> 3.97 us  [swap(): return lax.ppermute(block, 'feat', [(i, i ^ bit) for i in range(m)])]
    all_to_all x1, starting transfers between devices: 3.16 us -> 5.8 us  [shards(): lax.all_to_all(part.reshape(n * m, rows_each, LANES), ('fact', 'feat'), 0...]
    ppermute x3, waiting for transfers between devices: 1.55 us -> 3.6 us  [pass_on(): lax.ppermute(right, 'fact', to_right)]
    ppermute x1, waiting for transfers between devices: 1.96 us -> 0.01 us  [shards(): after = lax.ppermute(right, 'fact', to_right)]
    ppermute x3, starting transfers between devices: 4.46 us -> 2.77 us  [pass_on(): lax.ppermute(left, 'fact', to_left)]
    ppermute x3, starting transfers between devices: 1.66 us -> 3.35 us  [pass_on(): lax.ppermute(right, 'fact', to_right)]
    all_to_all x1, starting transfers between devices: 6.35 us -> 4.77 us  [shards(): asked = lax.all_to_all(asks, 'fact', 0, 0)]
  transfers between devices with their start and end apart: 27 -> 27, of which waited for: 16 -> 15; matrix products, arithmetic and copies ran while one was open for 0% -> 0% of each run, Pallas kernels for 15% -> 20%
where the time goes in v3:
time: 101 us
  starting transfers between devices  40.6 us (40%)
  waiting for transfers between devices  31.3 us (31%)
  Pallas kernels  22.7 us (22%)
  local copies, waits for them, and re-layouts  4.95 us (5%)
  between operations  1.16 us (1%)
    ppermute x7, starting transfers between devices, shards(): lax.ppermute(message, 'fact', [(i, (i + offset) % n) for i in range(n)])  12.8 us
    ppermute x7, waiting for transfers between devices, shards(): lax.ppermute(message, 'fact', [(i, (i + offset) % n) for i in range(n)])  11.8 us
    all_to_all x1, waiting for transfers between devices, shards(): lax.all_to_all(part.reshape(n * m, rows_each, LANES), ('fact', 'feat'), 0...  8.02 us
    pallas_call x4, Pallas kernels, look(): call(functools.partial(look_kernel, n, pieces), shape((facts, LANES), F32...  6.27 us
    all_to_all x1, starting transfers between devices, shards(): lax.all_to_all(part.reshape(n * m, rows_each, LANES), ('fact', 'feat'), 0...  5.8 us
    ppermute x9, starting transfers between devices, swap(): return lax.ppermute(block, 'feat', [(i, i ^ bit) for i in range(m)])  5.35 us
    unnamed x36, local copies, waits for them, and re-layouts  4.91 us
    all_to_all x1, starting transfers between devices, shards(): asked = lax.all_to_all(asks, 'fact', 0, 0)  4.77 us
  transfers between devices with their start and end apart: 27, of which 15 were waited for; matrix products, arithmetic and copies ran while one was open for 0% of the time, Pallas kernels for 20%

profile of v3, /device:TPU:4, one launch (start us, length us, event | category | flops | bytes accessed | tf_op | source)
XLA Modules:
  0.0 100.7 jit_solution(11623076397375568439)
XLA Ops:
  0.7 2.0 %collective-permute-start.1 = (bf16[1024,128]{1,0:T(8,128)(2,1)}, bf16[1024,128]{1,0:T(8,128)(2,1)S(1)}, u32[]{:S(2)}, u32[]{:S(2)}) collective-permute-start(bf16[1024,128]{1,0:T(8,128)(2,1)} %refs_0_.2), channel_id=1, source_target_pairs={{8,0},{16,8},{24,16},{28,24},{20,28},{12,20},{4,12},{0,4},{9,1},{1... | collective-permute-start | bytes 786440 | tf_op jit(solution)/shard_map/ppermute | solution.py:426
  6.3 1.8 %route.1 = (s32[8,4,128]{2,1,0:T(4,128)}, s32[8,128]{1,0:T(8,128)S(1)}, s32[8,128]{1,0:T(8,128)S(1)}, bf16[1024,128]{1,0:T(8,128)(2,1)S(1)}, bf16[1024,128]{1,0:T(8,128)(2,1)S(1)}) custom-call(s32[8,128]{1,0:T(8,128)S(1)} %bitcast.7, s32[8,128]{1,0:T(8,128)S(1)} %bitcast.8, s32[8,128]{1,0:T(8,128)S(1)} %bitcast.9, s32[8,128]{1,0:T(8,128)S(1)} %bitcast.10), custom_call_target="tpu_custom_call" | custom-call | flops 268435456 | bytes 1048576 | tf_op jit(solution)/shard_map/route/pallas_call | solution.py:436
  9.1 1.7 %collective-permute-start.3 = (bf16[1024,128]{1,0:T(8,128)(2,1)S(1)}, bf16[1024,128]{1,0:T(8,128)(2,1)S(1)}, u32[]{:S(2)}, u32[]{:S(2)}) collective-permute-start(bf16[1024,128]{1,0:T(8,128)(2,1)S(1)} %collective-permute-done.refs_1_), channel_id=1, source_target_pairs={{0,8},{8,16},{16,24},{24,28},{28,20},{20,12},{12,4},{4,0},{1,9},{9... | collective-permute-start | bytes 786440 | tf_op jit(solution)/shard_map/ppermute | solution.py:426
  12.1 2.6 %look.4.refs_2_ = f32[1024,128]{1,0:T(8,128)S(1)} custom-call(bf16[1024,128]{1,0:T(8,128)(2,1)S(1)} %get-tuple-element.91.low_ref, bf16[1024,128]{1,0:T(8,128)(2,1)S(1)} %get-tuple-element.92.high_ref, bf16[1024,128]{1,0:T(8,128)(2,1)S(1)} %copy-done.9, bf16[1024,128]{1,0:T(8,128)(2,1)S(1)} %collective-permute-done.refs_1_, ...), custom_call_target="tpu_custom_call" | custom-call | flops 805306368 | bytes 1048576 | tf_op jit(solution)/shard_map/look/pallas_call | solution.py:457
  14.7 1.9 %collective-permute-done.3.refs_0_ = bf16[1024,128]{1,0:T(8,128)(2,1)S(1)} collective-permute-done((bf16[1024,128]{1,0:T(8,128)(2,1)S(1)}, bf16[1024,128]{1,0:T(8,128)(2,1)S(1)}, u32[]{:S(2)}, u32[]{:S(2)}) %collective-permute-start.3) | collective-permute-done | bytes 262176 | tf_op jit(solution)/shard_map/ppermute | solution.py:426
  21.1 1.8 %look.5.refs_1_ = f32[1024,128]{1,0:T(8,128)S(1)} custom-call(bf16[1024,128]{1,0:T(8,128)(2,1)S(1)} %get-tuple-element.91.low_ref, bf16[1024,128]{1,0:T(8,128)(2,1)S(1)} %get-tuple-element.92.high_ref, bf16[1024,128]{1,0:T(8,128)(2,1)S(1)} %collective-permute-done.3.refs_0_, bf16[1024,128]{1,0:T(8,128)(2,1)S(1)} %collective-permute-done.4.refs_1_, ...), custom_call_target="tpu_custom_call" | custom-call | flops 536870912 | bytes 1048576 | tf_op jit(solution)/shard_map/look/pallas_call | solution.py:457
  23.7 1.6 %collective-permute-done.7.refs_0_ = bf16[1024,128]{1,0:T(8,128)(2,1)S(1)} collective-permute-done((bf16[1024,128]{1,0:T(8,128)(2,1)S(1)}, bf16[1024,128]{1,0:T(8,128)(2,1)S(1)}, u32[]{:S(2)}, u32[]{:S(2)}) %collective-permute-start.7) | collective-permute-done | bytes 262176 | tf_op jit(solution)/shard_map/ppermute | solution.py:426
  25.3 1.6 %collective-permute-start.9 = (bf16[1024,128]{1,0:T(8,128)(2,1)S(1)}, bf16[1024,128]{1,0:T(8,128)(2,1)}, u32[]{:S(2)}, u32[]{:S(2)}) collective-permute-start(bf16[1024,128]{1,0:T(8,128)(2,1)S(1)} %collective-permute-done.6.refs_0_), channel_id=1, source_target_pairs={{0,8},{8,16},{16,24},{24,28},{28,20},{20,12},{12,4},{4,0},{1,9},{9... | collective-permute-start | bytes 786440 | tf_op jit(solution)/shard_map/ppermute | solution.py:486
  27.8 4.8 %all-to-all-start.1 = ((s32[8,4,128]{2,1,0:T(4,128)}), s32[8,4,128]{2,1,0:T(4,128)S(1)}, u32[]{:S(2)}, u32[]{:S(2)}) async-start(s32[8,4,128]{2,1,0:T(4,128)} %get-tuple-element.113), calls=%async_computation.1 | async-start | bytes 32768 | tf_op jit(solution)/shard_map/all_to_all | solution.py:490
  34.1 3.9 %message.1 = (f32[1024,128]{1,0:T(8,128)}, bf16[1024,128]{1,0:T(8,128)(2,1)}) custom-call(bf16[1024,128]{1,0:T(8,128)(2,1)S(1)} %get-tuple-element.91.low_ref, bf16[1024,128]{1,0:T(8,128)(2,1)S(1)} %get-tuple-element.92.high_ref, bf16[1024,128]{1,0:T(8,128)(2,1)} %collective-permute-done.9.refs_0_, f32[1024,128]{1,0:T(8,128)S(1)} %look.7.refs_1_, ...), custom_call_target="tpu_custom_call" | custom-call | flops 536870912 | bytes 1048576 | tf_op jit(solution)/shard_map/message/pallas_call | solution.py:509
  37.9 5.8 %all-to-all-start = ((bf16[32,32,128]{2,1,0:T(8,128)(2,1)}), bf16[32,32,128]{2,1,0:T(8,128)(2,1)S(1)}, u32[]{:S(2)}, u32[]{:S(2)}) async-start(bf16[32,32,128]{2,1,0:T(8,128)(2,1)} %bitcast.4), calls=%async_computation | async-start | bytes 524288 | tf_op jit(solution)/shard_map/all_to_all | solution.py:528
  45.4 8.0 %all-to-all-done.sums_ref = bf16[32,32,128]{2,1,0:T(8,128)(2,1)S(1)} async-done(((bf16[32,32,128]{2,1,0:T(8,128)(2,1)}), bf16[32,32,128]{2,1,0:T(8,128)(2,1)S(1)}, u32[]{:S(2)}, u32[]{:S(2)}) %all-to-all-start) | async-done | bytes 262176 | tf_op jit(solution)/shard_map/all_to_all | solution.py:528
  53.5 1.6 %entity.1 = (bf16[32,32,128]{2,1,0:T(8,128)(2,1)}, bf16[4,32,128]{2,1,0:T(8,128)(2,1)S(1)}, bf16[4,32,128]{2,1,0:T(8,128)(2,1)S(1)}, bf16[128,128]{1,0:T(8,128)(2,1)S(1)}) custom-call(bf16[32,32,128]{2,1,0:T(8,128)(2,1)S(1)} %all-to-all-done.sums_ref, s32[8,4,128]{2,1,0:T(4,128)S(1)} %all-to-all-done.1.idx_ref.req_ref, ...), custom_call_target="tpu_custom_call" | custom-call | flops 50331648 | bytes 1048576 | tf_op jit(solution)/shard_map/entity/pallas_call | solution.py:538
  55.1 3.5 %all-to-all-start.2 = ((bf16[32,32,128]{2,1,0:T(8,128)(2,1)}), bf16[32,32,128]{2,1,0:T(8,128)(2,1)S(1)}, u32[]{:S(2)}, u32[]{:S(2)}) async-start(bf16[32,32,128]{2,1,0:T(8,128)(2,1)} %get-tuple-element.124), calls=%async_computation.2 | async-start | bytes 524288 | tf_op jit(solution)/shard_map/all_to_all | solution.py:551
  62.8 1.8 %collective-permute-done.14.refs_2_ = bf16[192,128]{1,0:T(8,128)(2,1)S(1)} collective-permute-done((bf16[192,128]{1,0:T(8,128)(2,1)S(1)}, bf16[192,128]{1,0:T(8,128)(2,1)S(1)}, u32[]{:S(2)}, u32[]{:S(2)}) %collective-permute-start.14) | collective-permute-done | bytes 49184 | tf_op jit(solution)/shard_map/ppermute | solution.py:429
  68.4 1.7 %backward.1 = (bf16[1024,128]{1,0:T(8,128)(2,1)S(1)}, bf16[8,64,128]{2,1,0:T(8,128)(2,1)S(1)}) custom-call(f32[1024,128]{1,0:T(8,128)S(1)} %copy-done.7, bf16[1024,128]{1,0:T(8,128)(2,1)S(1)} %bitcast.6, bf16[1024,128]{1,0:T(8,128)(2,1)S(1)} %get-tuple-element.133.low_ref, bf16[1024,128]{1,0:T(8,128)(2,1)S(1)} %get-tuple-element.134.high_ref, ...), custom_call_target="tpu_custom_call" | custom-call | flops 402653184 | bytes 1048576 | tf_op jit(solution)/shard_map/backward/pallas_call | solution.py:589
  73.1 2.1 %collective-permute-start.21 = (bf16[576,128]{1,0:T(8,128)(2,1)S(1)}, bf16[576,128]{1,0:T(8,128)(2,1)S(1)}, u32[]{:S(2)}, u32[]{:S(2)}) collective-permute-start(bf16[576,128]{1,0:T(8,128)(2,1)S(1)} %spread.7), channel_id=1, source_target_pairs={{0,16},{4,20},{8,24},{12,28},{16,0},{20,4},{24,8},{28,12},{1,17},{... | collective-permute-start | bytes 442376 | tf_op jit(solution)/shard_map/ppermute | solution.py:643
  75.8 1.8 %collective-permute-start.19 = (bf16[576,128]{1,0:T(8,128)(2,1)S(1)}, bf16[576,128]{1,0:T(8,128)(2,1)S(1)}, u32[]{:S(2)}, u32[]{:S(2)}) collective-permute-start(bf16[576,128]{1,0:T(8,128)(2,1)S(1)} %get-tuple-element.143), channel_id=1, source_target_pairs={{0,8},{4,12},{8,16},{12,20},{16,24},{20,28},{24,0},{28,4},{1,9},{5... | collective-permute-start | bytes 442376 | tf_op jit(solution)/shard_map/ppermute | solution.py:643
  77.6 2.1 %collective-permute-start.20 = (bf16[576,128]{1,0:T(8,128)(2,1)S(1)}, bf16[576,128]{1,0:T(8,128)(2,1)S(1)}, u32[]{:S(2)}, u32[]{:S(2)}) collective-permute-start(bf16[576,128]{1,0:T(8,128)(2,1)S(1)} %get-tuple-element.144), channel_id=1, source_target_pairs={{0,24},{4,28},{8,0},{12,4},{16,8},{20,12},{24,16},{28,20},{1,25},{... | collective-permute-start | bytes 442376 | tf_op jit(solution)/shard_map/ppermute | solution.py:643
  80.3 2.4 %collective-permute-start.16 = (bf16[448,128]{1,0:T(8,128)(2,1)S(1)}, bf16[448,128]{1,0:T(8,128)(2,1)S(1)}, u32[]{:S(2)}, u32[]{:S(2)}) collective-permute-start(bf16[448,128]{1,0:T(8,128)(2,1)S(1)} %get-tuple-element.138), channel_id=1, source_target_pairs={{0,12},{4,16},{8,20},{12,24},{16,28},{20,0},{24,4},{28,8},{1,13},{... | collective-permute-start | bytes 344072 | tf_op jit(solution)/shard_map/ppermute | solution.py:643
  82.7 2.4 %collective-permute-start.17 = (bf16[448,128]{1,0:T(8,128)(2,1)S(1)}, bf16[448,128]{1,0:T(8,128)(2,1)S(1)}, u32[]{:S(2)}, u32[]{:S(2)}) collective-permute-start(bf16[448,128]{1,0:T(8,128)(2,1)S(1)} %get-tuple-element.139), channel_id=1, source_target_pairs={{0,20},{4,24},{8,28},{12,0},{16,4},{20,8},{24,12},{28,16},{1,21},{... | collective-permute-start | bytes 344072 | tf_op jit(solution)/shard_map/ppermute | solution.py:643
  86.4 2.3 %collective-permute-done.21.refs_0_ = bf16[576,128]{1,0:T(8,128)(2,1)S(1)} collective-permute-done((bf16[576,128]{1,0:T(8,128)(2,1)S(1)}, bf16[576,128]{1,0:T(8,128)(2,1)S(1)}, u32[]{:S(2)}, u32[]{:S(2)}) %collective-permute-start.21) | collective-permute-done | bytes 147488 | tf_op jit(solution)/shard_map/ppermute | solution.py:643
  90.3 2.6 %collective-permute-done.16.refs_0_ = bf16[448,128]{1,0:T(8,128)(2,1)S(1)} collective-permute-done((bf16[448,128]{1,0:T(8,128)(2,1)S(1)}, bf16[448,128]{1,0:T(8,128)(2,1)S(1)}, u32[]{:S(2)}, u32[]{:S(2)}) %collective-permute-start.16) | collective-permute-done | bytes 114720 | tf_op jit(solution)/shard_map/ppermute | solution.py:643
  92.8 6.4 %collective-permute-done.17.refs_1_ = bf16[448,128]{1,0:T(8,128)(2,1)S(1)} collective-permute-done((bf16[448,128]{1,0:T(8,128)(2,1)S(1)}, bf16[448,128]{1,0:T(8,128)(2,1)S(1)}, u32[]{:S(2)}, u32[]{:S(2)}) %collective-permute-start.17) | collective-permute-done | bytes 114720 | tf_op jit(solution)/shard_map/ppermute | solution.py:643
  (92 shorter events, 31.5 us)
Async XLA Ops:
  0.6 8.3 %collective-permute-start = (bf16[1024,128]{1,0:T(8,128)(2,1)}, bf16[1024,128]{1,0:T(8,128)(2,1)S(1)}, u32[]{:S(2)}, u32[]{:S(2)}) collective-permute-start(bf16[1024,128]{1,0:T(8,128)(2,1)} %refs_0_.2), channel_id=1, source_target_pairs={{0,8},{8,16},{16,24},{24,28},{28,20},{20,12},{12,4},{4,0},{1,9},{9... | collective-permute-start | bytes 786440 | tf_op jit(solution)/shard_map/ppermute | solution.py:426
  0.7 8.3 %collective-permute-start.1 = (bf16[1024,128]{1,0:T(8,128)(2,1)}, bf16[1024,128]{1,0:T(8,128)(2,1)S(1)}, u32[]{:S(2)}, u32[]{:S(2)}) collective-permute-start(bf16[1024,128]{1,0:T(8,128)(2,1)} %refs_0_.2), channel_id=1, source_target_pairs={{8,0},{16,8},{24,16},{28,24},{20,28},{12,20},{4,12},{0,4},{9,1},{1... | collective-permute-start | bytes 786440 | tf_op jit(solution)/shard_map/ppermute | solution.py:426
  2.7 6.3 %collective-permute-start.2 = (bf16[1024,128]{1,0:T(8,128)(2,1)}, bf16[1024,128]{1,0:T(8,128)(2,1)S(1)}, u32[]{:S(2)}, u32[]{:S(2)}) collective-permute-start(bf16[1024,128]{1,0:T(8,128)(2,1)} %refs_0_.4), channel_id=1, source_target_pairs={{0,1},{1,0},{2,3},{3,2},{4,5},{5,4},{6,7},{7,6},{8,9},{9,8},{10,11... | collective-permute-start | bytes 786440 | tf_op jit(solution)/shard_map/ppermute | solution.py:429
  2.7 11.9 %collective-permute-start.5 = (bf16[1024,128]{1,0:T(8,128)(2,1)}, bf16[1024,128]{1,0:T(8,128)(2,1)S(1)}, u32[]{:S(2)}, u32[]{:S(2)}) collective-permute-start(bf16[1024,128]{1,0:T(8,128)(2,1)} %refs_0_.4), channel_id=1, source_target_pairs={{0,2},{1,3},{2,0},{3,1},{4,6},{5,7},{6,4},{7,5},{8,10},{9,11},{10,... | collective-permute-start | bytes 786440 | tf_op jit(solution)/shard_map/ppermute | solution.py:429
  9.1 7.6 %collective-permute-start.3 = (bf16[1024,128]{1,0:T(8,128)(2,1)S(1)}, bf16[1024,128]{1,0:T(8,128)(2,1)S(1)}, u32[]{:S(2)}, u32[]{:S(2)}) collective-permute-start(bf16[1024,128]{1,0:T(8,128)(2,1)S(1)} %collective-permute-done.refs_1_), channel_id=1, source_target_pairs={{0,8},{8,16},{16,24},{24,28},{28,20},{20,12},{12,4},{4,0},{1,9},{9... | collective-permute-start | bytes 786440 | tf_op jit(solution)/shard_map/ppermute | solution.py:426
  10.8 6.6 %collective-permute-start.4 = (bf16[1024,128]{1,0:T(8,128)(2,1)S(1)}, bf16[1024,128]{1,0:T(8,128)(2,1)S(1)}, u32[]{:S(2)}, u32[]{:S(2)}) collective-permute-start(bf16[1024,128]{1,0:T(8,128)(2,1)S(1)} %collective-permute-done.1.refs_2_), channel_id=1, source_target_pairs={{8,0},{16,8},{24,16},{28,24},{20,28},{12,20},{4,12},{0,4},{9,1},{1... | collective-permute-start | bytes 786440 | tf_op jit(solution)/shard_map/ppermute | solution.py:426
  17.3 6.4 %collective-permute-start.6 = (bf16[1024,128]{1,0:T(8,128)(2,1)S(1)}, bf16[1024,128]{1,0:T(8,128)(2,1)S(1)}, u32[]{:S(2)}, u32[]{:S(2)}) collective-permute-start(bf16[1024,128]{1,0:T(8,128)(2,1)S(1)} %collective-permute-done.3.refs_0_), channel_id=1, source_target_pairs={{0,8},{8,16},{16,24},{24,28},{28,20},{20,12},{12,4},{4,0},{1,9},{9... | collective-permute-start | bytes 786440 | tf_op jit(solution)/shard_map/ppermute | solution.py:426
  18.9 6.4 %collective-permute-start.7 = (bf16[1024,128]{1,0:T(8,128)(2,1)S(1)}, bf16[1024,128]{1,0:T(8,128)(2,1)S(1)}, u32[]{:S(2)}, u32[]{:S(2)}) collective-permute-start(bf16[1024,128]{1,0:T(8,128)(2,1)S(1)} %collective-permute-done.4.refs_1_), channel_id=1, source_target_pairs={{8,0},{16,8},{24,16},{28,24},{20,28},{12,20},{4,12},{0,4},{9,1},{1... | collective-permute-start | bytes 786440 | tf_op jit(solution)/shard_map/ppermute | solution.py:426
  19.4 5.9 %collective-permute-start.8 = (bf16[1024,128]{1,0:T(8,128)(2,1)S(1)}, bf16[1024,128]{1,0:T(8,128)(2,1)S(1)}, u32[]{:S(2)}, u32[]{:S(2)}) collective-permute-start(bf16[1024,128]{1,0:T(8,128)(2,1)S(1)} %collective-permute-done.5.refs_2_), channel_id=1, source_target_pairs={{0,1},{1,0},{2,3},{3,2},{4,5},{5,4},{6,7},{7,6},{8,9},{9,8},{10,11... | collective-permute-start | bytes 786440 | tf_op jit(solution)/shard_map/ppermute | solution.py:429
  19.4 14.7 %collective-permute-start.10 = (bf16[1280,128]{1,0:T(8,128)(2,1)S(1)}, bf16[1280,128]{1,0:T(8,128)(2,1)S(1)}, u32[]{:S(2)}, u32[]{:S(2)}) collective-permute-start(bf16[1280,128]{1,0:T(8,128)(2,1)S(1)} %pad_maximum_fusion.refs_4_.refs_0_), channel_id=1, source_target_pairs={{0,2},{1,3},{2,0},{3,1},{4,6},{5,7},{6,4},{7,5},{8,10},{9,11},{10,... | collective-permute-start | bytes 983048 | tf_op jit(solution)/shard_map/ppermute | solution.py:429
  20.9 13.2 %collective-permute-start.11 = (bf16[1280,128]{1,0:T(8,128)(2,1)S(1)}, bf16[1280,128]{1,0:T(8,128)(2,1)S(1)}, u32[]{:S(2)}, u32[]{:S(2)}) collective-permute-start(bf16[1280,128]{1,0:T(8,128)(2,1)S(1)} %pad_maximum_fusion.refs_4_.refs_0_), channel_id=1, source_target_pairs={{0,1},{1,0},{2,3},{3,2},{4,5},{5,4},{6,7},{7,6},{8,9},{9,8},{10,11... | collective-permute-start | bytes 983048 | tf_op jit(solution)/shard_map/ppermute | solution.py:429
  25.3 8.7 %collective-permute-start.9 = (bf16[1024,128]{1,0:T(8,128)(2,1)S(1)}, bf16[1024,128]{1,0:T(8,128)(2,1)}, u32[]{:S(2)}, u32[]{:S(2)}) collective-permute-start(bf16[1024,128]{1,0:T(8,128)(2,1)S(1)} %collective-permute-done.6.refs_0_), channel_id=1, source_target_pairs={{0,8},{8,16},{16,24},{24,28},{28,20},{20,12},{12,4},{4,0},{1,9},{9... | collective-permute-start | bytes 786440 | tf_op jit(solution)/shard_map/ppermute | solution.py:486
  27.8 10.1 %all-to-all-start.1 = ((s32[8,4,128]{2,1,0:T(4,128)}), s32[8,4,128]{2,1,0:T(4,128)S(1)}, u32[]{:S(2)}, u32[]{:S(2)}) async-start(s32[8,4,128]{2,1,0:T(4,128)} %get-tuple-element.113), calls=%async_computation.1 | async-start | bytes 32768 | tf_op jit(solution)/shard_map/all_to_all | solution.py:490
  37.9 15.5 %all-to-all-start = ((bf16[32,32,128]{2,1,0:T(8,128)(2,1)}), bf16[32,32,128]{2,1,0:T(8,128)(2,1)S(1)}, u32[]{:S(2)}, u32[]{:S(2)}) async-start(bf16[32,32,128]{2,1,0:T(8,128)(2,1)} %bitcast.4), calls=%async_computation | async-start | bytes 524288 | tf_op jit(solution)/shard_map/all_to_all | solution.py:528
  55.1 13.3 %all-to-all-start.2 = ((bf16[32,32,128]{2,1,0:T(8,128)(2,1)}), bf16[32,32,128]{2,1,0:T(8,128)(2,1)S(1)}, u32[]{:S(2)}, u32[]{:S(2)}) async-start(bf16[32,32,128]{2,1,0:T(8,128)(2,1)} %get-tuple-element.124), calls=%async_computation.2 | async-start | bytes 524288 | tf_op jit(solution)/shard_map/all_to_all | solution.py:551
  58.9 5.8 %collective-permute-start.14 = (bf16[192,128]{1,0:T(8,128)(2,1)S(1)}, bf16[192,128]{1,0:T(8,128)(2,1)S(1)}, u32[]{:S(2)}, u32[]{:S(2)}) collective-permute-start(bf16[192,128]{1,0:T(8,128)(2,1)S(1)} %get-tuple-element.119), channel_id=1, source_target_pairs={{0,2},{1,3},{2,0},{3,1},{4,6},{5,7},{6,4},{7,5},{8,10},{9,11},{10,... | collective-permute-start | bytes 147464 | tf_op jit(solution)/shard_map/ppermute | solution.py:429
  66.0 6.7 %collective-permute-start.18 = (bf16[4,128,128]{2,1,0:T(8,128)(2,1)S(1)}, bf16[4,128,128]{2,1,0:T(8,128)(2,1)S(1)}, u32[]{:S(2)}, u32[]{:S(2)}) collective-permute-start(bf16[4,128,128]{2,1,0:T(8,128)(2,1)S(1)} %get-tuple-element.142), channel_id=1, source_target_pairs={{0,4},{4,0},{8,12},{12,8},{16,20},{20,16},{24,28},{28,24},{1,5},{5... | collective-permute-start | bytes 393224 | tf_op jit(solution)/shard_map/ppermute | solution.py:586
  70.7 9.6 %collective-permute-start.22 = (bf16[448,128]{1,0:T(8,128)(2,1)S(1)}, bf16[448,128]{1,0:T(8,128)(2,1)S(1)}, u32[]{:S(2)}, u32[]{:S(2)}) collective-permute-start(bf16[448,128]{1,0:T(8,128)(2,1)S(1)} %get-tuple-element.145), channel_id=1, source_target_pairs={{0,4},{4,8},{8,12},{12,16},{16,20},{20,24},{24,28},{28,0},{1,5},{5... | collective-permute-start | bytes 344072 | tf_op jit(solution)/shard_map/ppermute | solution.py:643
  72.2 10.5 %collective-permute-start.23 = (bf16[448,128]{1,0:T(8,128)(2,1)S(1)}, bf16[448,128]{1,0:T(8,128)(2,1)S(1)}, u32[]{:S(2)}, u32[]{:S(2)}) collective-permute-start(bf16[448,128]{1,0:T(8,128)(2,1)S(1)} %get-tuple-element.146), channel_id=1, source_target_pairs={{0,28},{4,0},{8,4},{12,8},{16,12},{20,16},{24,20},{28,24},{1,29},{... | collective-permute-start | bytes 344072 | tf_op jit(solution)/shard_map/ppermute | solution.py:643
  73.1 15.6 %collective-permute-start.21 = (bf16[576,128]{1,0:T(8,128)(2,1)S(1)}, bf16[576,128]{1,0:T(8,128)(2,1)S(1)}, u32[]{:S(2)}, u32[]{:S(2)}) collective-permute-start(bf16[576,128]{1,0:T(8,128)(2,1)S(1)} %spread.7), channel_id=1, source_target_pairs={{0,16},{4,20},{8,24},{12,28},{16,0},{20,4},{24,8},{28,12},{1,17},{... | collective-permute-start | bytes 442376 | tf_op jit(solution)/shard_map/ppermute | solution.py:643
  75.8 13.3 %collective-permute-start.19 = (bf16[576,128]{1,0:T(8,128)(2,1)S(1)}, bf16[576,128]{1,0:T(8,128)(2,1)S(1)}, u32[]{:S(2)}, u32[]{:S(2)}) collective-permute-start(bf16[576,128]{1,0:T(8,128)(2,1)S(1)} %get-tuple-element.143), channel_id=1, source_target_pairs={{0,8},{4,12},{8,16},{12,20},{16,24},{20,28},{24,0},{28,4},{1,9},{5... | collective-permute-start | bytes 442376 | tf_op jit(solution)/shard_map/ppermute | solution.py:643
  77.6 12.1 %collective-permute-start.20 = (bf16[576,128]{1,0:T(8,128)(2,1)S(1)}, bf16[576,128]{1,0:T(8,128)(2,1)S(1)}, u32[]{:S(2)}, u32[]{:S(2)}) collective-permute-start(bf16[576,128]{1,0:T(8,128)(2,1)S(1)} %get-tuple-element.144), channel_id=1, source_target_pairs={{0,24},{4,28},{8,0},{12,4},{16,8},{20,12},{24,16},{28,20},{1,25},{... | collective-permute-start | bytes 442376 | tf_op jit(solution)/shard_map/ppermute | solution.py:643
  80.3 12.6 %collective-permute-start.16 = (bf16[448,128]{1,0:T(8,128)(2,1)S(1)}, bf16[448,128]{1,0:T(8,128)(2,1)S(1)}, u32[]{:S(2)}, u32[]{:S(2)}) collective-permute-start(bf16[448,128]{1,0:T(8,128)(2,1)S(1)} %get-tuple-element.138), channel_id=1, source_target_pairs={{0,12},{4,16},{8,20},{12,24},{16,28},{20,0},{24,4},{28,8},{1,13},{... | collective-permute-start | bytes 344072 | tf_op jit(solution)/shard_map/ppermute | solution.py:643
  82.7 16.5 %collective-permute-start.17 = (bf16[448,128]{1,0:T(8,128)(2,1)S(1)}, bf16[448,128]{1,0:T(8,128)(2,1)S(1)}, u32[]{:S(2)}, u32[]{:S(2)}) collective-permute-start(bf16[448,128]{1,0:T(8,128)(2,1)S(1)} %get-tuple-element.139), channel_id=1, source_target_pairs={{0,20},{4,24},{8,28},{12,0},{16,4},{20,8},{24,12},{28,16},{1,21},{... | collective-permute-start | bytes 344072 | tf_op jit(solution)/shard_map/ppermute | solution.py:643
  (21 other events, 115.4 us)

commit v4 on v3

--- a/solution.py
+++ b/solution.py
@@ -176,6 +176,7 @@
         erlow_ref[:, here], erhigh_ref[:, here] = row_codes(ent_ref[k : k + 1, :])
     for copy in arrivals:
         copy.wait()
+    kept = []
     for c in range(facts // step):
         rows = slice(c * step, (c + 1) * step)
         pre = xw_ref[rows, :] + base_ref[rows, :]
@@ -184,8 +185,8 @@
         gate = jax.nn.sigmoid(pre)
         msg_ref[rows, :] = (pre * gate).astype(BF)
         slope_ref[rows, :] = gate * (1.0 + pre * (1.0 - gate))
-    keep = pltpu.make_async_copy(slope_ref, slope_out, sem)
-    keep.start()
+        kept.append(pltpu.make_async_copy(slope_ref.at[rows, :], slope_out.at[rows, :], sem.at[c]))
+        kept[-1].start()
 
     def add(pair, carry):
         hot = jnp.concatenate(
@@ -196,7 +197,8 @@
         return carry
 
     lax.fori_loop(0, part_ref.shape[0] // 256, add, 0)
-    keep.wait()
+    for copy in kept:
+        copy.wait()
 
 
 def project_kernel(m, w_ref, *refs):
@@ -218,10 +220,27 @@
         xt_ref[pl.ds(pl.multiple_of((me ^ j) * LANES, LANES), LANES), :] = x_refs[j][...].T
 
 
-def entity_kernel(n, m, width, ents, sums_ref, idx_ref, *refs):
-    all_refs, (back_ref, out_ref, pre_ref, agg_ref, own_ref, hold_ref, words_ref, sem) = refs[:m], refs[m:]
-    fetch = pltpu.make_async_copy(idx_ref, words_ref, sem)
-    fetch.start()
+def own_kernel(m, width, ents, *refs):
+    all_refs, (self_ref, own_ref) = refs[:m], refs[m:]
+    rows_each = ents // m
+    me = lax.axis_index("feat")
+    at = pl.multiple_of(2 * width + me * rows_each, rows_each)
+    for j in range(m):
+        own_ref[me ^ j] = all_refs[j][pl.ds(at, rows_each), :]
+    hidden = jnp.concatenate([own_ref[b] for b in range(m)], axis=1)
+    for j in range(m):
+        self_ref[j] = dot(hidden, all_refs[j][0:width, :])
+
+
+def entity_kernel(n, m, width, ents, sums_ref, idx_ref, self_in, *refs):
+    all_refs, refs = refs[:m], refs[m:]
+    back_ref, out_ref, pre_ref, agg_ref, self_ref, hold_ref, words_ref, sems = refs
+    fetches = [
+        pltpu.make_async_copy(idx_ref, words_ref, sems.at[0]),
+        pltpu.make_async_copy(self_in, self_ref, sems.at[1]),
+    ]
+    for fetch in fetches:
+        fetch.start()
     rows_each = ents // m
     me = lax.axis_index("feat")
     totals = []
@@ -230,20 +249,18 @@
         for f in range(1, n):
             total += sums_ref[f * m + b].astype(F32)
         totals.append(total)
-    fetch.wait()
+    for fetch in fetches:
+        fetch.wait()
     hits = jnp.sum(words_ref[:, words_ref.shape[1] - 1, :], axis=0, keepdims=True).astype(F32)
     hold_ref[...] = jnp.maximum(jnp.broadcast_to(hits, (LANES, ents)).T, 1.0)
     divisor = hold_ref[pl.ds(pl.multiple_of(me * rows_each, rows_each), rows_each), :]
     for b in range(m):
         agg_ref[b * rows_each : (b + 1) * rows_each, :] = (totals[b] / divisor).astype(BF)
     at = pl.multiple_of(2 * width + me * rows_each, rows_each)
-    for j in range(m):
-        own_ref[me ^ j] = all_refs[j][pl.ds(at, rows_each), :]
     aggregate = jnp.concatenate([agg_ref[b * rows_each : (b + 1) * rows_each, :] for b in range(m)], axis=1)
-    hidden = jnp.concatenate([own_ref[b] for b in range(m)], axis=1)
     d_agg = None
     for j in range(m):
-        pre = dot(hidden, all_refs[j][0:width, :]) + dot(aggregate, all_refs[j][width : 2 * width, :])
+        pre = self_ref[j] + dot(aggregate, all_refs[j][width : 2 * width, :])
         gate = jax.nn.sigmoid(pre)
         cot = all_refs[j][pl.ds(at + ents, rows_each), :].astype(F32)
         d_pre = (cot * (gate * (1.0 + pre * (1.0 - gate)))).astype(BF)
@@ -508,7 +525,7 @@
     last_rows = max(LANES, sum(t.shape[0] for t in last))
     slope, part = call(
         functools.partial(message_kernel, n, last_pieces),
-        (pltpu.HBM((facts, LANES), F32), shape((n * ents, LANES), BF)),
+        (pltpu.HBM((facts, LANES), F32), pltpu.VMEM((n * ents, LANES), BF)),
         [
             pltpu.VMEM((facts, LANES), F32),
             pltpu.VMEM((step, last_rows), BF),
@@ -516,7 +533,7 @@
             pltpu.VMEM((LANES, facts), BF),
             pltpu.VMEM((16, facts), BF),
             *[pltpu.VMEM(t.shape, BF) for t in last],
-            pltpu.SemaphoreType.DMA,
+            pltpu.SemaphoreType.DMA((facts // step,)),
             pltpu.SemaphoreType.DMA,
         ],
         2 * facts * (last_rows + n * ents) * LANES,
@@ -534,20 +551,27 @@
         1 << 28,
         "ready",
     )(*x_blocks, *all_blocks)
+    self_part = call(
+        functools.partial(own_kernel, m, width, ents),
+        shape((m, rows_each, LANES), F32),
+        [pltpu.VMEM((m, rows_each, LANES), BF)],
+        2 * rows_each * width * width,
+        "own",
+    )(*all_blocks)
     by_feat = shape((m, rows_each, LANES), BF)
     back, out_parts, pre_parts, agg_parts = call(
         functools.partial(entity_kernel, n, m, width, ents),
-        (shape((n * m, rows_each, LANES), BF), by_feat, by_feat, shape((m * rows_each, LANES), BF)),
+        (pltpu.VMEM((n * m, rows_each, LANES), BF), by_feat, by_feat, shape((m * rows_each, LANES), BF)),
         [
-            pltpu.VMEM((m, rows_each, LANES), BF),
+            pltpu.VMEM((m, rows_each, LANES), F32),
             pltpu.VMEM((ents, LANES), F32),
             pltpu.VMEM(asked.shape, jnp.int32),
-            pltpu.SemaphoreType.DMA,
+            pltpu.SemaphoreType.DMA((2,)),
         ],
-        6 * rows_each * width * width,
+        4 * rows_each * width * width,
         "entity",
-        in_specs=[IN_VMEM, pl.BlockSpec(memory_space=pl.ANY)] + [IN_VMEM] * m,
-    )(sums, asked, *all_blocks)
+        in_specs=[IN_VMEM] + [pl.BlockSpec(memory_space=pl.ANY)] * 2 + [IN_VMEM] * m,
+    )(sums, asked, self_part, *all_blocks)
     scaled = lax.all_to_all(back, ("fact", "feat"), 0, 0).reshape(n * ents, LANES)
     shares = call(
         functools.partial(share_kernel, m),

time: 101 us -> 102 us (level)
  Pallas kernels: 22.7 us -> 23.9 us
    ppermute x3, waiting for transfers between devices: 2.39 us -> 1.19 us  [pass_on(): lax.ppermute(left, 'fact', to_left)]
    ppermute x3, waiting for transfers between devices: 3.6 us -> 4.79 us  [pass_on(): lax.ppermute(right, 'fact', to_right)]
  transfers between devices with their start and end apart: 27 -> 27, of which waited for: 15 -> 15; matrix products, arithmetic and copies ran while one was open for 0% -> 0% of each run, Pallas kernels for 20% -> 21%
where the time goes in v4:
time: 102 us
  starting transfers between devices  40.4 us (40%)
  waiting for transfers between devices  32 us (31%)
  Pallas kernels  23.9 us (23%)
  local copies, waits for them, and re-layouts  4.06 us (4%)
  between operations  1.16 us (1%)
    ppermute x7, starting transfers between devices, shards(): lax.ppermute(message, 'fact', [(i, (i + offset) % n) for i in range(n)])  12.8 us
    ppermute x7, waiting for transfers between devices, shards(): lax.ppermute(message, 'fact', [(i, (i + offset) % n) for i in range(n)])  11.8 us
    all_to_all x1, waiting for transfers between devices, shards(): lax.all_to_all(part.reshape(n * m, rows_each, LANES), ('fact', 'feat'), 0...  7.82 us
    pallas_call x4, Pallas kernels, look(): call(functools.partial(look_kernel, n, pieces), shape((facts, LANES), F32...  7.21 us
    all_to_all x1, starting transfers between devices, shards(): lax.all_to_all(part.reshape(n * m, rows_each, LANES), ('fact', 'feat'), 0...  5.74 us
    ppermute x9, starting transfers between devices, swap(): return lax.ppermute(block, 'feat', [(i, i ^ bit) for i in range(m)])  5.35 us
    ppermute x9, waiting for transfers between devices, swap(): return lax.ppermute(block, 'feat', [(i, i ^ bit) for i in range(m)])  4.92 us
    all_to_all x1, starting transfers between devices, shards(): asked = lax.all_to_all(asks, 'fact', 0, 0)  4.83 us
  transfers between devices with their start and end apart: 27, of which 15 were waited for; matrix products, arithmetic and copies ran while one was open for 0% of the time, Pallas kernels for 21%

profile of v4, /device:TPU:4, one launch (start us, length us, event | category | flops | bytes accessed | tf_op | source)
XLA Modules:
  0.0 101.5 jit_solution(7654532260151704378)
XLA Ops:
  0.7 2.0 %collective-permute-start.1 = (bf16[1024,128]{1,0:T(8,128)(2,1)}, bf16[1024,128]{1,0:T(8,128)(2,1)S(1)}, u32[]{:S(2)}, u32[]{:S(2)}) collective-permute-start(bf16[1024,128]{1,0:T(8,128)(2,1)} %refs_0_.2), channel_id=1, source_target_pairs={{8,0},{16,8},{24,16},{28,24},{20,28},{12,20},{4,12},{0,4},{9,1},{1... | collective-permute-start | bytes 786440 | tf_op jit(solution)/shard_map/ppermute | solution.py:443
  6.3 1.8 %route.1 = (s32[8,4,128]{2,1,0:T(4,128)}, s32[8,128]{1,0:T(8,128)S(1)}, s32[8,128]{1,0:T(8,128)S(1)}, bf16[1024,128]{1,0:T(8,128)(2,1)S(1)}, bf16[1024,128]{1,0:T(8,128)(2,1)S(1)}) custom-call(s32[8,128]{1,0:T(8,128)S(1)} %bitcast.7, s32[8,128]{1,0:T(8,128)S(1)} %bitcast.8, s32[8,128]{1,0:T(8,128)S(1)} %bitcast.9, s32[8,128]{1,0:T(8,128)S(1)} %bitcast.10), custom_call_target="tpu_custom_call" | custom-call | flops 268435456 | bytes 1048576 | tf_op jit(solution)/shard_map/route/pallas_call | solution.py:453
  9.1 1.7 %collective-permute-start.3 = (bf16[1024,128]{1,0:T(8,128)(2,1)S(1)}, bf16[1024,128]{1,0:T(8,128)(2,1)S(1)}, u32[]{:S(2)}, u32[]{:S(2)}) collective-permute-start(bf16[1024,128]{1,0:T(8,128)(2,1)S(1)} %collective-permute-done.refs_1_), channel_id=1, source_target_pairs={{0,8},{8,16},{16,24},{24,28},{28,20},{20,12},{12,4},{4,0},{1,9},{9... | collective-permute-start | bytes 786440 | tf_op jit(solution)/shard_map/ppermute | solution.py:443
  12.1 2.6 %look.4.refs_2_ = f32[1024,128]{1,0:T(8,128)S(1)} custom-call(bf16[1024,128]{1,0:T(8,128)(2,1)S(1)} %get-tuple-element.91.low_ref, bf16[1024,128]{1,0:T(8,128)(2,1)S(1)} %get-tuple-element.92.high_ref, bf16[1024,128]{1,0:T(8,128)(2,1)S(1)} %copy-done.5, bf16[1024,128]{1,0:T(8,128)(2,1)S(1)} %collective-permute-done.refs_1_, ...), custom_call_target="tpu_custom_call" | custom-call | flops 805306368 | bytes 1048576 | tf_op jit(solution)/shard_map/look/pallas_call | solution.py:474
  14.7 2.4 %collective-permute-done.3.refs_0_ = bf16[1024,128]{1,0:T(8,128)(2,1)S(1)} collective-permute-done((bf16[1024,128]{1,0:T(8,128)(2,1)S(1)}, bf16[1024,128]{1,0:T(8,128)(2,1)S(1)}, u32[]{:S(2)}, u32[]{:S(2)}) %collective-permute-start.3) | collective-permute-done | bytes 262176 | tf_op jit(solution)/shard_map/ppermute | solution.py:443
  21.1 1.8 %look.5.refs_1_ = f32[1024,128]{1,0:T(8,128)S(1)} custom-call(bf16[1024,128]{1,0:T(8,128)(2,1)S(1)} %get-tuple-element.91.low_ref, bf16[1024,128]{1,0:T(8,128)(2,1)S(1)} %get-tuple-element.92.high_ref, bf16[1024,128]{1,0:T(8,128)(2,1)S(1)} %collective-permute-done.3.refs_0_, bf16[1024,128]{1,0:T(8,128)(2,1)S(1)} %collective-permute-done.4.refs_1_, ...), custom_call_target="tpu_custom_call" | custom-call | flops 536870912 | bytes 1048576 | tf_op jit(solution)/shard_map/look/pallas_call | solution.py:474
  25.3 1.6 %collective-permute-start.9 = (bf16[1024,128]{1,0:T(8,128)(2,1)}, bf16[1024,128]{1,0:T(8,128)(2,1)}, u32[]{:S(2)}, u32[]{:S(2)}) collective-permute-start(bf16[1024,128]{1,0:T(8,128)(2,1)} %collective-permute-done.6.refs_0_), channel_id=1, source_target_pairs={{0,8},{8,16},{16,24},{24,28},{28,20},{20,12},{12,4},{4,0},{1,9},{9... | collective-permute-start | bytes 786440 | tf_op jit(solution)/shard_map/ppermute | solution.py:503
  27.8 4.8 %all-to-all-start.1 = ((s32[8,4,128]{2,1,0:T(4,128)}), s32[8,4,128]{2,1,0:T(4,128)S(1)}, u32[]{:S(2)}, u32[]{:S(2)}) async-start(s32[8,4,128]{2,1,0:T(4,128)} %get-tuple-element.113), calls=%async_computation.1 | async-start | bytes 32768 | tf_op jit(solution)/shard_map/all_to_all | solution.py:507
  33.1 1.9 %look.7.refs_1_ = f32[1024,128]{1,0:T(8,128)S(1)} custom-call(bf16[1024,128]{1,0:T(8,128)(2,1)S(1)} %get-tuple-element.91.low_ref, bf16[1024,128]{1,0:T(8,128)(2,1)S(1)} %get-tuple-element.92.high_ref, bf16[1024,128]{1,0:T(8,128)(2,1)} %collective-permute-done.6.refs_0_, f32[1024,128]{1,0:T(8,128)S(1)} %look.6.refs_1_), custom_call_target="tpu_custom_call" | custom-call | flops 268435456 | bytes 1048576 | tf_op jit(solution)/shard_map/look/pallas_call | solution.py:474
  35.0 3.9 %message.1 = (f32[1024,128]{1,0:T(8,128)}, bf16[1024,128]{1,0:T(8,128)(2,1)}) custom-call(bf16[1024,128]{1,0:T(8,128)(2,1)S(1)} %get-tuple-element.91.low_ref, bf16[1024,128]{1,0:T(8,128)(2,1)S(1)} %get-tuple-element.92.high_ref, bf16[1024,128]{1,0:T(8,128)(2,1)} %collective-permute-done.9.refs_0_, f32[1024,128]{1,0:T(8,128)S(1)} %look.7.refs_1_, ...), custom_call_target="tpu_custom_call" | custom-call | flops 536870912 | bytes 1048576 | tf_op jit(solution)/shard_map/message/pallas_call | solution.py:526
  38.9 5.7 %all-to-all-start = ((bf16[32,32,128]{2,1,0:T(8,128)(2,1)}), bf16[32,32,128]{2,1,0:T(8,128)(2,1)S(1)}, u32[]{:S(2)}, u32[]{:S(2)}) async-start(bf16[32,32,128]{2,1,0:T(8,128)(2,1)} %bitcast.4), calls=%async_computation | async-start | bytes 524288 | tf_op jit(solution)/shard_map/all_to_all | solution.py:545
  46.6 7.8 %all-to-all-done.sums_ref = bf16[32,32,128]{2,1,0:T(8,128)(2,1)S(1)} async-done(((bf16[32,32,128]{2,1,0:T(8,128)(2,1)}), bf16[32,32,128]{2,1,0:T(8,128)(2,1)S(1)}, u32[]{:S(2)}, u32[]{:S(2)}) %all-to-all-start) | async-done | bytes 262176 | tf_op jit(solution)/shard_map/all_to_all | solution.py:545
  54.4 1.6 %entity.1 = (bf16[32,32,128]{2,1,0:T(8,128)(2,1)}, bf16[4,32,128]{2,1,0:T(8,128)(2,1)S(1)}, bf16[4,32,128]{2,1,0:T(8,128)(2,1)S(1)}, bf16[128,128]{1,0:T(8,128)(2,1)S(1)}) custom-call(bf16[32,32,128]{2,1,0:T(8,128)(2,1)S(1)} %all-to-all-done.sums_ref, s32[8,4,128]{2,1,0:T(4,128)S(1)} %all-to-all-done.1.idx_ref.req_ref, f32[4,32,128]{2,1,0:T(8,128)S(1)} %own.1.self_in, ...), custom_call_target="tpu_custom_call" | custom-call | flops 33554432 | bytes 1048576 | tf_op jit(solution)/shard_map/entity/pallas_call | solution.py:562
  56.0 3.4 %all-to-all-start.2 = ((bf16[32,32,128]{2,1,0:T(8,128)(2,1)}), bf16[32,32,128]{2,1,0:T(8,128)(2,1)S(1)}, u32[]{:S(2)}, u32[]{:S(2)}) async-start(bf16[32,32,128]{2,1,0:T(8,128)(2,1)} %get-tuple-element.124), calls=%async_computation.2 | async-start | bytes 524288 | tf_op jit(solution)/shard_map/all_to_all | solution.py:575
  62.7 2.8 %collective-permute-done.14.refs_2_ = bf16[192,128]{1,0:T(8,128)(2,1)S(1)} collective-permute-done((bf16[192,128]{1,0:T(8,128)(2,1)S(1)}, bf16[192,128]{1,0:T(8,128)(2,1)S(1)}, u32[]{:S(2)}, u32[]{:S(2)}) %collective-permute-start.14) | collective-permute-done | bytes 49184 | tf_op jit(solution)/shard_map/ppermute | solution.py:446
  69.2 1.7 %backward.1 = (bf16[1024,128]{1,0:T(8,128)(2,1)S(1)}, bf16[8,64,128]{2,1,0:T(8,128)(2,1)S(1)}) custom-call(f32[1024,128]{1,0:T(8,128)S(1)} %copy-done.3, bf16[1024,128]{1,0:T(8,128)(2,1)S(1)} %bitcast.6, bf16[1024,128]{1,0:T(8,128)(2,1)S(1)} %get-tuple-element.133.low_ref, bf16[1024,128]{1,0:T(8,128)(2,1)S(1)} %get-tuple-element.134.high_ref, ...), custom_call_target="tpu_custom_call" | custom-call | flops 402653184 | bytes 1048576 | tf_op jit(solution)/shard_map/backward/pallas_call | solution.py:613
  73.9 2.1 %collective-permute-start.21 = (bf16[576,128]{1,0:T(8,128)(2,1)S(1)}, bf16[576,128]{1,0:T(8,128)(2,1)S(1)}, u32[]{:S(2)}, u32[]{:S(2)}) collective-permute-start(bf16[576,128]{1,0:T(8,128)(2,1)S(1)} %spread.7), channel_id=1, source_target_pairs={{0,16},{4,20},{8,24},{12,28},{16,0},{20,4},{24,8},{28,12},{1,17},{... | collective-permute-start | bytes 442376 | tf_op jit(solution)/shard_map/ppermute | solution.py:667
  76.6 1.6 %collective-permute-start.19 = (bf16[576,128]{1,0:T(8,128)(2,1)S(1)}, bf16[576,128]{1,0:T(8,128)(2,1)S(1)}, u32[]{:S(2)}, u32[]{:S(2)}) collective-permute-start(bf16[576,128]{1,0:T(8,128)(2,1)S(1)} %get-tuple-element.143), channel_id=1, source_target_pairs={{0,8},{4,12},{8,16},{12,20},{16,24},{20,28},{24,0},{28,4},{1,9},{5... | collective-permute-start | bytes 442376 | tf_op jit(solution)/shard_map/ppermute | solution.py:667
  78.3 2.2 %collective-permute-start.20 = (bf16[576,128]{1,0:T(8,128)(2,1)S(1)}, bf16[576,128]{1,0:T(8,128)(2,1)S(1)}, u32[]{:S(2)}, u32[]{:S(2)}) collective-permute-start(bf16[576,128]{1,0:T(8,128)(2,1)S(1)} %get-tuple-element.144), channel_id=1, source_target_pairs={{0,24},{4,28},{8,0},{12,4},{16,8},{20,12},{24,16},{28,20},{1,25},{... | collective-permute-start | bytes 442376 | tf_op jit(solution)/shard_map/ppermute | solution.py:667
  81.1 2.4 %collective-permute-start.16 = (bf16[448,128]{1,0:T(8,128)(2,1)S(1)}, bf16[448,128]{1,0:T(8,128)(2,1)S(1)}, u32[]{:S(2)}, u32[]{:S(2)}) collective-permute-start(bf16[448,128]{1,0:T(8,128)(2,1)S(1)} %get-tuple-element.138), channel_id=1, source_target_pairs={{0,12},{4,16},{8,20},{12,24},{16,28},{20,0},{24,4},{28,8},{1,13},{... | collective-permute-start | bytes 344072 | tf_op jit(solution)/shard_map/ppermute | solution.py:667
  83.5 2.4 %collective-permute-start.17 = (bf16[448,128]{1,0:T(8,128)(2,1)S(1)}, bf16[448,128]{1,0:T(8,128)(2,1)S(1)}, u32[]{:S(2)}, u32[]{:S(2)}) collective-permute-start(bf16[448,128]{1,0:T(8,128)(2,1)S(1)} %get-tuple-element.139), channel_id=1, source_target_pairs={{0,20},{4,24},{8,28},{12,0},{16,4},{20,8},{24,12},{28,16},{1,21},{... | collective-permute-start | bytes 344072 | tf_op jit(solution)/shard_map/ppermute | solution.py:667
  87.3 2.3 %collective-permute-done.21.refs_0_ = bf16[576,128]{1,0:T(8,128)(2,1)S(1)} collective-permute-done((bf16[576,128]{1,0:T(8,128)(2,1)S(1)}, bf16[576,128]{1,0:T(8,128)(2,1)S(1)}, u32[]{:S(2)}, u32[]{:S(2)}) %collective-permute-start.21) | collective-permute-done | bytes 147488 | tf_op jit(solution)/shard_map/ppermute | solution.py:667
  91.1 2.6 %collective-permute-done.16.refs_0_ = bf16[448,128]{1,0:T(8,128)(2,1)S(1)} collective-permute-done((bf16[448,128]{1,0:T(8,128)(2,1)S(1)}, bf16[448,128]{1,0:T(8,128)(2,1)S(1)}, u32[]{:S(2)}, u32[]{:S(2)}) %collective-permute-start.16) | collective-permute-done | bytes 114720 | tf_op jit(solution)/shard_map/ppermute | solution.py:667
  93.6 6.4 %collective-permute-done.17.refs_1_ = bf16[448,128]{1,0:T(8,128)(2,1)S(1)} collective-permute-done((bf16[448,128]{1,0:T(8,128)(2,1)S(1)}, bf16[448,128]{1,0:T(8,128)(2,1)S(1)}, u32[]{:S(2)}, u32[]{:S(2)}) %collective-permute-start.17) | collective-permute-done | bytes 114720 | tf_op jit(solution)/shard_map/ppermute | solution.py:667
  (93 shorter events, 30.9 us)
Async XLA Ops:
  0.6 8.3 %collective-permute-start = (bf16[1024,128]{1,0:T(8,128)(2,1)}, bf16[1024,128]{1,0:T(8,128)(2,1)S(1)}, u32[]{:S(2)}, u32[]{:S(2)}) collective-permute-start(bf16[1024,128]{1,0:T(8,128)(2,1)} %refs_0_.2), channel_id=1, source_target_pairs={{0,8},{8,16},{16,24},{24,28},{28,20},{20,12},{12,4},{4,0},{1,9},{9... | collective-permute-start | bytes 786440 | tf_op jit(solution)/shard_map/ppermute | solution.py:443
  0.7 8.3 %collective-permute-start.1 = (bf16[1024,128]{1,0:T(8,128)(2,1)}, bf16[1024,128]{1,0:T(8,128)(2,1)S(1)}, u32[]{:S(2)}, u32[]{:S(2)}) collective-permute-start(bf16[1024,128]{1,0:T(8,128)(2,1)} %refs_0_.2), channel_id=1, source_target_pairs={{8,0},{16,8},{24,16},{28,24},{20,28},{12,20},{4,12},{0,4},{9,1},{1... | collective-permute-start | bytes 786440 | tf_op jit(solution)/shard_map/ppermute | solution.py:443
  2.7 6.3 %collective-permute-start.2 = (bf16[1024,128]{1,0:T(8,128)(2,1)}, bf16[1024,128]{1,0:T(8,128)(2,1)S(1)}, u32[]{:S(2)}, u32[]{:S(2)}) collective-permute-start(bf16[1024,128]{1,0:T(8,128)(2,1)} %refs_0_.4), channel_id=1, source_target_pairs={{0,1},{1,0},{2,3},{3,2},{4,5},{5,4},{6,7},{7,6},{8,9},{9,8},{10,11... | collective-permute-start | bytes 786440 | tf_op jit(solution)/shard_map/ppermute | solution.py:446
  2.7 11.9 %collective-permute-start.5 = (bf16[1024,128]{1,0:T(8,128)(2,1)}, bf16[1024,128]{1,0:T(8,128)(2,1)S(1)}, u32[]{:S(2)}, u32[]{:S(2)}) collective-permute-start(bf16[1024,128]{1,0:T(8,128)(2,1)} %refs_0_.4), channel_id=1, source_target_pairs={{0,2},{1,3},{2,0},{3,1},{4,6},{5,7},{6,4},{7,5},{8,10},{9,11},{10,... | collective-permute-start | bytes 786440 | tf_op jit(solution)/shard_map/ppermute | solution.py:446
  9.1 8.1 %collective-permute-start.3 = (bf16[1024,128]{1,0:T(8,128)(2,1)S(1)}, bf16[1024,128]{1,0:T(8,128)(2,1)S(1)}, u32[]{:S(2)}, u32[]{:S(2)}) collective-permute-start(bf16[1024,128]{1,0:T(8,128)(2,1)S(1)} %collective-permute-done.refs_1_), channel_id=1, source_target_pairs={{0,8},{8,16},{16,24},{24,28},{28,20},{20,12},{12,4},{4,0},{1,9},{9... | collective-permute-start | bytes 786440 | tf_op jit(solution)/shard_map/ppermute | solution.py:443
  10.8 6.6 %collective-permute-start.4 = (bf16[1024,128]{1,0:T(8,128)(2,1)S(1)}, bf16[1024,128]{1,0:T(8,128)(2,1)S(1)}, u32[]{:S(2)}, u32[]{:S(2)}) collective-permute-start(bf16[1024,128]{1,0:T(8,128)(2,1)S(1)} %collective-permute-done.1.refs_2_), channel_id=1, source_target_pairs={{8,0},{16,8},{24,16},{28,24},{20,28},{12,20},{4,12},{0,4},{9,1},{1... | collective-permute-start | bytes 786440 | tf_op jit(solution)/shard_map/ppermute | solution.py:443
  17.3 7.1 %collective-permute-start.6 = (bf16[1024,128]{1,0:T(8,128)(2,1)S(1)}, bf16[1024,128]{1,0:T(8,128)(2,1)}, u32[]{:S(2)}, u32[]{:S(2)}) collective-permute-start(bf16[1024,128]{1,0:T(8,128)(2,1)S(1)} %collective-permute-done.3.refs_0_), channel_id=1, source_target_pairs={{0,8},{8,16},{16,24},{24,28},{28,20},{20,12},{12,4},{4,0},{1,9},{9... | collective-permute-start | bytes 786440 | tf_op jit(solution)/shard_map/ppermute | solution.py:443
  18.9 6.4 %collective-permute-start.7 = (bf16[1024,128]{1,0:T(8,128)(2,1)S(1)}, bf16[1024,128]{1,0:T(8,128)(2,1)S(1)}, u32[]{:S(2)}, u32[]{:S(2)}) collective-permute-start(bf16[1024,128]{1,0:T(8,128)(2,1)S(1)} %collective-permute-done.4.refs_1_), channel_id=1, source_target_pairs={{8,0},{16,8},{24,16},{28,24},{20,28},{12,20},{4,12},{0,4},{9,1},{1... | collective-permute-start | bytes 786440 | tf_op jit(solution)/shard_map/ppermute | solution.py:443
  19.4 5.9 %collective-permute-start.8 = (bf16[1024,128]{1,0:T(8,128)(2,1)S(1)}, bf16[1024,128]{1,0:T(8,128)(2,1)S(1)}, u32[]{:S(2)}, u32[]{:S(2)}) collective-permute-start(bf16[1024,128]{1,0:T(8,128)(2,1)S(1)} %collective-permute-done.5.refs_2_), channel_id=1, source_target_pairs={{0,1},{1,0},{2,3},{3,2},{4,5},{5,4},{6,7},{7,6},{8,9},{9,8},{10,11... | collective-permute-start | bytes 786440 | tf_op jit(solution)/shard_map/ppermute | solution.py:446
  19.4 15.6 %collective-permute-start.10 = (bf16[1280,128]{1,0:T(8,128)(2,1)S(1)}, bf16[1280,128]{1,0:T(8,128)(2,1)S(1)}, u32[]{:S(2)}, u32[]{:S(2)}) collective-permute-start(bf16[1280,128]{1,0:T(8,128)(2,1)S(1)} %pad_maximum_fusion.refs_4_.refs_0_), channel_id=1, source_target_pairs={{0,2},{1,3},{2,0},{3,1},{4,6},{5,7},{6,4},{7,5},{8,10},{9,11},{10,... | collective-permute-start | bytes 983048 | tf_op jit(solution)/shard_map/ppermute | solution.py:446
  20.9 14.2 %collective-permute-start.11 = (bf16[1280,128]{1,0:T(8,128)(2,1)S(1)}, bf16[1280,128]{1,0:T(8,128)(2,1)S(1)}, u32[]{:S(2)}, u32[]{:S(2)}) collective-permute-start(bf16[1280,128]{1,0:T(8,128)(2,1)S(1)} %pad_maximum_fusion.refs_4_.refs_0_), channel_id=1, source_target_pairs={{0,1},{1,0},{2,3},{3,2},{4,5},{5,4},{6,7},{7,6},{8,9},{9,8},{10,11... | collective-permute-start | bytes 983048 | tf_op jit(solution)/shard_map/ppermute | solution.py:446
  25.3 9.7 %collective-permute-start.9 = (bf16[1024,128]{1,0:T(8,128)(2,1)}, bf16[1024,128]{1,0:T(8,128)(2,1)}, u32[]{:S(2)}, u32[]{:S(2)}) collective-permute-start(bf16[1024,128]{1,0:T(8,128)(2,1)} %collective-permute-done.6.refs_0_), channel_id=1, source_target_pairs={{0,8},{8,16},{16,24},{24,28},{28,20},{20,12},{12,4},{4,0},{1,9},{9... | collective-permute-start | bytes 786440 | tf_op jit(solution)/shard_map/ppermute | solution.py:503
  27.8 11.1 %all-to-all-start.1 = ((s32[8,4,128]{2,1,0:T(4,128)}), s32[8,4,128]{2,1,0:T(4,128)S(1)}, u32[]{:S(2)}, u32[]{:S(2)}) async-start(s32[8,4,128]{2,1,0:T(4,128)} %get-tuple-element.113), calls=%async_computation.1 | async-start | bytes 32768 | tf_op jit(solution)/shard_map/all_to_all | solution.py:507
  38.9 15.5 %all-to-all-start = ((bf16[32,32,128]{2,1,0:T(8,128)(2,1)}), bf16[32,32,128]{2,1,0:T(8,128)(2,1)S(1)}, u32[]{:S(2)}, u32[]{:S(2)}) async-start(bf16[32,32,128]{2,1,0:T(8,128)(2,1)} %bitcast.4), calls=%async_computation | async-start | bytes 524288 | tf_op jit(solution)/shard_map/all_to_all | solution.py:545
  56.0 13.2 %all-to-all-start.2 = ((bf16[32,32,128]{2,1,0:T(8,128)(2,1)}), bf16[32,32,128]{2,1,0:T(8,128)(2,1)S(1)}, u32[]{:S(2)}, u32[]{:S(2)}) async-start(bf16[32,32,128]{2,1,0:T(8,128)(2,1)} %get-tuple-element.124), calls=%async_computation.2 | async-start | bytes 524288 | tf_op jit(solution)/shard_map/all_to_all | solution.py:575
  59.7 5.8 %collective-permute-start.14 = (bf16[192,128]{1,0:T(8,128)(2,1)S(1)}, bf16[192,128]{1,0:T(8,128)(2,1)S(1)}, u32[]{:S(2)}, u32[]{:S(2)}) collective-permute-start(bf16[192,128]{1,0:T(8,128)(2,1)S(1)} %get-tuple-element.119), channel_id=1, source_target_pairs={{0,2},{1,3},{2,0},{3,1},{4,6},{5,7},{6,4},{7,5},{8,10},{9,11},{10,... | collective-permute-start | bytes 147464 | tf_op jit(solution)/shard_map/ppermute | solution.py:446
  66.8 6.7 %collective-permute-start.18 = (bf16[4,128,128]{2,1,0:T(8,128)(2,1)S(1)}, bf16[4,128,128]{2,1,0:T(8,128)(2,1)S(1)}, u32[]{:S(2)}, u32[]{:S(2)}) collective-permute-start(bf16[4,128,128]{2,1,0:T(8,128)(2,1)S(1)} %get-tuple-element.142), channel_id=1, source_target_pairs={{0,4},{4,0},{8,12},{12,8},{16,20},{20,16},{24,28},{28,24},{1,5},{5... | collective-permute-start | bytes 393224 | tf_op jit(solution)/shard_map/ppermute | solution.py:610
  71.5 9.6 %collective-permute-start.22 = (bf16[448,128]{1,0:T(8,128)(2,1)S(1)}, bf16[448,128]{1,0:T(8,128)(2,1)S(1)}, u32[]{:S(2)}, u32[]{:S(2)}) collective-permute-start(bf16[448,128]{1,0:T(8,128)(2,1)S(1)} %get-tuple-element.145), channel_id=1, source_target_pairs={{0,4},{4,8},{8,12},{12,16},{16,20},{20,24},{24,28},{28,0},{1,5},{5... | collective-permute-start | bytes 344072 | tf_op jit(solution)/shard_map/ppermute | solution.py:667
  73.0 10.5 %collective-permute-start.23 = (bf16[448,128]{1,0:T(8,128)(2,1)S(1)}, bf16[448,128]{1,0:T(8,128)(2,1)S(1)}, u32[]{:S(2)}, u32[]{:S(2)}) collective-permute-start(bf16[448,128]{1,0:T(8,128)(2,1)S(1)} %get-tuple-element.146), channel_id=1, source_target_pairs={{0,28},{4,0},{8,4},{12,8},{16,12},{20,16},{24,20},{28,24},{1,29},{... | collective-permute-start | bytes 344072 | tf_op jit(solution)/shard_map/ppermute | solution.py:667
  73.9 15.6 %collective-permute-start.21 = (bf16[576,128]{1,0:T(8,128)(2,1)S(1)}, bf16[576,128]{1,0:T(8,128)(2,1)S(1)}, u32[]{:S(2)}, u32[]{:S(2)}) collective-permute-start(bf16[576,128]{1,0:T(8,128)(2,1)S(1)} %spread.7), channel_id=1, source_target_pairs={{0,16},{4,20},{8,24},{12,28},{16,0},{20,4},{24,8},{28,12},{1,17},{... | collective-permute-start | bytes 442376 | tf_op jit(solution)/shard_map/ppermute | solution.py:667
  76.6 13.3 %collective-permute-start.19 = (bf16[576,128]{1,0:T(8,128)(2,1)S(1)}, bf16[576,128]{1,0:T(8,128)(2,1)S(1)}, u32[]{:S(2)}, u32[]{:S(2)}) collective-permute-start(bf16[576,128]{1,0:T(8,128)(2,1)S(1)} %get-tuple-element.143), channel_id=1, source_target_pairs={{0,8},{4,12},{8,16},{12,20},{16,24},{20,28},{24,0},{28,4},{1,9},{5... | collective-permute-start | bytes 442376 | tf_op jit(solution)/shard_map/ppermute | solution.py:667
  78.3 12.2 %collective-permute-start.20 = (bf16[576,128]{1,0:T(8,128)(2,1)S(1)}, bf16[576,128]{1,0:T(8,128)(2,1)S(1)}, u32[]{:S(2)}, u32[]{:S(2)}) collective-permute-start(bf16[576,128]{1,0:T(8,128)(2,1)S(1)} %get-tuple-element.144), channel_id=1, source_target_pairs={{0,24},{4,28},{8,0},{12,4},{16,8},{20,12},{24,16},{28,20},{1,25},{... | collective-permute-start | bytes 442376 | tf_op jit(solution)/shard_map/ppermute | solution.py:667
  81.1 12.6 %collective-permute-start.16 = (bf16[448,128]{1,0:T(8,128)(2,1)S(1)}, bf16[448,128]{1,0:T(8,128)(2,1)S(1)}, u32[]{:S(2)}, u32[]{:S(2)}) collective-permute-start(bf16[448,128]{1,0:T(8,128)(2,1)S(1)} %get-tuple-element.138), channel_id=1, source_target_pairs={{0,12},{4,16},{8,20},{12,24},{16,28},{20,0},{24,4},{28,8},{1,13},{... | collective-permute-start | bytes 344072 | tf_op jit(solution)/shard_map/ppermute | solution.py:667
  83.5 16.5 %collective-permute-start.17 = (bf16[448,128]{1,0:T(8,128)(2,1)S(1)}, bf16[448,128]{1,0:T(8,128)(2,1)S(1)}, u32[]{:S(2)}, u32[]{:S(2)}) collective-permute-start(bf16[448,128]{1,0:T(8,128)(2,1)S(1)} %get-tuple-element.139), channel_id=1, source_target_pairs={{0,20},{4,24},{8,28},{12,0},{16,4},{20,8},{24,12},{28,16},{1,21},{... | collective-permute-start | bytes 344072 | tf_op jit(solution)/shard_map/ppermute | solution.py:667
  (21 other events, 95.9 us)

commit v5 on v3

--- a/solution.py
+++ b/solution.py
@@ -97,29 +97,31 @@
     entity_owner = fo_ref[...]
     entity_slot = fs_ref[...]
     value = ds_ref[...]
+    entity = entity_owner * ents + entity_slot
     pos_ref[...] = owner * cap + rank
-    ent_ref[...] = entity_owner * ents + entity_slot
+    ent_ref[...] = entity
     fact_dim = owner * dims + value
-    high = (value >> 5).astype(F32)
-    low = (value & 31).astype(F32)
+    words = [(value >> 5).astype(F32), (value & 31).astype(F32), (entity >> 5).astype(F32), (entity & 31).astype(F32)]
     names = lax.broadcasted_iota(jnp.int32, (n, LANES), 0)
     places = lax.broadcasted_iota(jnp.int32, (cap, LANES), 0)
     slots = lax.broadcasted_iota(jnp.int32, (ents, LANES), 0)
-    asked_high = jnp.zeros((n, cap), F32)
-    asked_low = jnp.zeros((n, cap), F32)
+    asked = [jnp.zeros((n, cap), F32) for _ in words]
     hits = jnp.zeros((n, ents), F32)
     for k in range(chunks):
         here = slice(k * LANES, (k + 1) * LANES)
         mine = jnp.where(names == owner[k : k + 1], 1.0, 0.0)
         at = flag(places == rank[k : k + 1])
-        asked_high += nt((mine * high[k : k + 1]).astype(BF), at)
-        asked_low += nt((mine * low[k : k + 1]).astype(BF), at)
+        for w, word in enumerate(words):
+            asked[w] += nt((mine * word[k : k + 1]).astype(BF), at)
         hits += nt(flag(names == entity_owner[k : k + 1]), flag(slots == entity_slot[k : k + 1]))
         dlow_ref[here, :], dhigh_ref[here, :] = column_codes(fact_dim[k : k + 1])
-    asked = (asked_high * 32.0 + asked_low).astype(jnp.int32)
-    for r in range(cap // LANES):
-        out_ref[:, r, :] = asked[:, r * LANES : (r + 1) * LANES]
-    out_ref[:, cap // LANES, :] = hits.astype(jnp.int32)
+    groups = cap // LANES
+    asked_dim = (asked[0] * 32.0 + asked[1]).astype(jnp.int32)
+    asked_ent = (asked[2] * 32.0 + asked[3]).astype(jnp.int32)
+    for r in range(groups):
+        out_ref[:, r, :] = asked_dim[:, r * LANES : (r + 1) * LANES]
+        out_ref[:, groups + r, :] = asked_ent[:, r * LANES : (r + 1) * LANES]
+    out_ref[:, 2 * groups, :] = hits.astype(jnp.int32)
 
 
 def gather_rows(low_ref, high_ref, rows, table_refs, firsts, hot_ref):
@@ -330,25 +332,47 @@
         share_ref[d] = padded(total[d * own : (d + 1) * own, :], stride).astype(BF)
 
 
+def slots_of(d, cap, plow_ref, phigh_ref):
+    return jnp.concatenate(
+        [
+            pick_rows(plow_ref[...], phigh_ref[...], (d * (cap // LANES) + i).astype(F32).astype(BF))
+            for i in range(cap // LANES)
+        ],
+        axis=0,
+    )
+
+
+def early_kernel(n, cap, offset, plow_ref, phigh_ref, slope_ref, out_ref):
+    d = lax.rem(lax.axis_index("fact") + offset, n)
+    out_ref[...] = dot(slots_of(d, cap, plow_ref, phigh_ref), slope_ref[...].astype(BF)).astype(BF)
+
+
+def form_kernel(n, cap, offset, scaled_ref, slopes_ref, idx_ref, rest_ref, out_ref, hot_ref, low_ref, high_ref):
+    groups = cap // LANES
+    source = lax.rem(lax.axis_index("fact") + (n - offset), n)
+    for r in range(groups):
+        here = slice(r * LANES, (r + 1) * LANES)
+        low_ref[here, :], high_ref[here, :] = column_codes(idx_ref[source, groups + r : groups + r + 1, :])
+    found = gather_rows(low_ref, high_ref, slice(0, cap), [scaled_ref], [jnp.int32(0)], hot_ref)
+    out_ref[0:cap, :] = (found * slopes_ref[...].astype(F32)).astype(BF)
+    out_ref[cap:, :] = rest_ref[...]
+
+
 def spread_kernel(n, cap, stride, offsets, plow_ref, phigh_ref, dmsg_ref, share_ref, *refs):
     pair_refs, out_refs = refs[:-len(offsets)], refs[-len(offsets) :]
     me = lax.axis_index("fact")
     for offset, out_ref in zip(offsets, out_refs):
         d = lax.rem(me + offset, n)
-        hot = jnp.concatenate(
-            [
-                pick_rows(plow_ref[...], phigh_ref[...], (d * (cap // LANES) + i).astype(F32).astype(BF))
-                for i in range(cap // LANES)
-            ],
-            axis=0,
-        )
-        out_ref[0:cap, :] = dot(hot, dmsg_ref[...]).astype(BF)
-        out_ref[cap : cap + stride, :] = share_ref[d]
-        if out_ref.shape[0] > cap + stride:
+        at = 0
+        if out_ref.shape[0] >= cap:
+            out_ref[0:cap, :] = dot(slots_of(d, cap, plow_ref, phigh_ref), dmsg_ref[...]).astype(BF)
+            at = cap
+        out_ref[at : at + stride, :] = share_ref[d]
+        if out_ref.shape[0] > at + stride:
             pair = pair_refs[0][lax.div(d, 2)]
             for ref in pair_refs[1:]:
                 pair = pair + ref[lax.div(d, 2)].astype(F32)
-            out_ref[cap + stride :, :] = pair.astype(BF)
+            out_ref[at + stride :, :] = pair.astype(BF)
 
 
 def table_kernel(n, cap, stride, offsets, first, final, low_ref, high_ref, *refs):
@@ -410,7 +434,7 @@
     dims = dim_table.shape[0]
     cap = -(-(3 * facts // n) // LANES) * LANES
     slots = n * cap
-    groups = cap // LANES + 1
+    groups = 2 * (cap // LANES) + 1
     own = width // n
     stride = max(16, own)
     step = 512
@@ -565,6 +589,17 @@
         1 << 26,
         "codes",
     )(pos, entity)
+    if ringed:
+        slope_early, _ = tie((slope, back))
+        slopes = call(
+            functools.partial(early_kernel, n, cap, n // 2),
+            shape((cap, LANES), BF),
+            [],
+            2 * facts * cap * LANES,
+            "early",
+        )(plow, phigh, slope_early)
+        slopes = lax.ppermute(slopes, "fact", [(i, (i + n // 2) % n) for i in range(n)])
+        elow, slopes = tie((elow, slopes))
     rlow, rhigh = call(
         functools.partial(request_kernel, n, cap),
         (shape((LANES, slots), BF), shape((16, slots), BF)),
@@ -598,6 +633,8 @@
 
     def spread(offsets):
         lengths = [cap + (3 if ringed and k % 2 == 0 else 1) * stride for k in offsets]
+        if ringed and offsets == [n // 2]:
+            lengths = [3 * stride]
         return call(
             functools.partial(spread_kernel, n, cap, stride, offsets),
             tuple(shape((rows, LANES), BF) for rows in lengths),
@@ -605,7 +642,7 @@
             2 * facts * cap * LANES * len(offsets),
             "spread",
             limit,
-        )(plow, phigh, d_msg, msg_share, *(pairs if max(lengths) > cap + stride else ()))
+        )(plow, phigh, d_msg, msg_share, *(pairs if ringed and any(k % 2 == 0 for k in offsets) else ()))
 
     def add_up(offsets, got, base, final):
         weight = shape((3 * stride, LANES), F32)
@@ -642,6 +679,13 @@
             for offset, message in zip(offsets, spread(offsets)):
                 messages[offset] = lax.ppermute(message, "fact", [(i, (i + offset) % n) for i in range(n)])
         messages[0] = spread([0])[0]
+        messages[n // 2] = call(
+            functools.partial(form_kernel, n, cap, n // 2),
+            shape((cap + 3 * stride, LANES), BF),
+            [pltpu.VMEM((cap, n * ents), BF), pltpu.VMEM((cap, LANES), BF), pltpu.VMEM((cap, LANES), BF)],
+            2 * cap * n * ents * LANES,
+            "form",
+        )(scaled, slopes, asked, messages[n // 2])
         for offsets in [[0, 1, n - 1], [n // 2], *rest[::-1]]:
             totals = add_up(offsets, [messages[k] for k in offsets], totals, offsets == rest[0])
         grad_dim, grad_msg, grad_self, grad_neigh = totals

time: 101 us -> 105 us (1.040)
  local copies, waits for them, and re-layouts: 4.95 us -> 6.43 us
  waiting for transfers between devices: 31.3 us -> 32.5 us
  Pallas kernels: 22.7 us -> 23.8 us
    ppermute x0 -> x1, waiting for transfers between devices: none -> 2.83 us  [shards(): lax.ppermute(slopes, 'fact', [(i, (i + n // 2) % n) for i in range(n)])]
    ppermute x0 -> x1, starting transfers between devices: none -> 2.5 us  [shards(): lax.ppermute(slopes, 'fact', [(i, (i + n // 2) % n) for i in range(n)])]
    ppermute x7, starting transfers between devices: 12.8 us -> 10.7 us  [shards(): lax.ppermute(message, 'fact', [(i, (i + offset) % n) for i in range(n)])]
    all_to_all x1, waiting for transfers between devices: 1.51 us -> 0.01 us  [shards(): lax.all_to_all(back, ('fact', 'feat'), 0, 0).reshape(n * ents, LANES)]
    unnamed x36 -> x50, local copies, waits for them, and re-layouts: 4.91 us -> 6.4 us
    ppermute x3, waiting for transfers between devices: 2.39 us -> 1.24 us  [pass_on(): lax.ppermute(left, 'fact', to_left)]
  transfers between devices with their start and end apart: 27 -> 28, of which waited for: 15 -> 14; matrix products, arithmetic and copies ran while one was open for 0% -> 0% of each run, Pallas kernels for 20% -> 20%
where the time goes in v5:
time: 105 us
  starting transfers between devices  40.9 us (39%)
  waiting for transfers between devices  32.5 us (31%)
  Pallas kernels  23.8 us (23%)
  local copies, waits for them, and re-layouts  6.43 us (6%)
  between operations  1.27 us (1%)
    ppermute x7, waiting for transfers between devices, shards(): lax.ppermute(message, 'fact', [(i, (i + offset) % n) for i in range(n)])  11.3 us
    ppermute x7, starting transfers between devices, shards(): lax.ppermute(message, 'fact', [(i, (i + offset) % n) for i in range(n)])  10.7 us
    all_to_all x1, waiting for transfers between devices, shards(): lax.all_to_all(part.reshape(n * m, rows_each, LANES), ('fact', 'feat'), 0...  8.02 us
    unnamed x50, local copies, waits for them, and re-layouts  6.4 us
    pallas_call x4, Pallas kernels, look(): call(functools.partial(look_kernel, n, pieces), shape((facts, LANES), F32...  6.27 us
    all_to_all x1, starting transfers between devices, shards(): lax.all_to_all(part.reshape(n * m, rows_each, LANES), ('fact', 'feat'), 0...  5.69 us
    ppermute x9, starting transfers between devices, swap(): return lax.ppermute(block, 'feat', [(i, i ^ bit) for i in range(m)])  5.31 us
    all_to_all x1, starting transfers between devices, shards(): asked = lax.all_to_all(asks, 'fact', 0, 0)  4.83 us
  transfers between devices with their start and end apart: 28, of which 14 were waited for; matrix products, arithmetic and copies ran while one was open for 0% of the time, Pallas kernels for 20%

profile of v5, /device:TPU:4, one launch (start us, length us, event | category | flops | bytes accessed | tf_op | source)
XLA Modules:
  0.0 104.9 jit_solution(7516957341268580932)
XLA Ops:
  0.7 2.0 %collective-permute-start.1 = (bf16[1024,128]{1,0:T(8,128)(2,1)}, bf16[1024,128]{1,0:T(8,128)(2,1)S(1)}, u32[]{:S(2)}, u32[]{:S(2)}) collective-permute-start(bf16[1024,128]{1,0:T(8,128)(2,1)} %refs_0_.2), channel_id=1, source_target_pairs={{8,0},{16,8},{24,16},{28,24},{20,28},{12,20},{4,12},{0,4},{9,1},{1... | collective-permute-start | bytes 786440 | tf_op jit(solution)/shard_map/ppermute | solution.py:450
  6.3 2.3 %route.1 = (s32[8,7,128]{2,1,0:T(8,128)}, s32[8,128]{1,0:T(8,128)S(1)}, s32[8,128]{1,0:T(8,128)S(1)}, bf16[1024,128]{1,0:T(8,128)(2,1)S(1)}, bf16[1024,128]{1,0:T(8,128)(2,1)S(1)}) custom-call(s32[8,128]{1,0:T(8,128)S(1)} %bitcast.8, s32[8,128]{1,0:T(8,128)S(1)} %bitcast.9, s32[8,128]{1,0:T(8,128)S(1)} %bitcast.10, s32[8,128]{1,0:T(8,128)S(1)} %bitcast.11), custom_call_target="tpu_custom_call" | custom-call | flops 268435456 | bytes 1048576 | tf_op jit(solution)/shard_map/route/pallas_call | solution.py:460
  9.1 1.7 %collective-permute-start.3 = (bf16[1024,128]{1,0:T(8,128)(2,1)S(1)}, bf16[1024,128]{1,0:T(8,128)(2,1)S(1)}, u32[]{:S(2)}, u32[]{:S(2)}) collective-permute-start(bf16[1024,128]{1,0:T(8,128)(2,1)S(1)} %collective-permute-done.refs_1_), channel_id=1, source_target_pairs={{0,8},{8,16},{16,24},{24,28},{28,20},{20,12},{12,4},{4,0},{1,9},{9... | collective-permute-start | bytes 786440 | tf_op jit(solution)/shard_map/ppermute | solution.py:450
  12.1 2.6 %look.4.refs_2_ = f32[1024,128]{1,0:T(8,128)S(1)} custom-call(bf16[1024,128]{1,0:T(8,128)(2,1)S(1)} %get-tuple-element.94.low_ref, bf16[1024,128]{1,0:T(8,128)(2,1)S(1)} %get-tuple-element.95.high_ref, bf16[1024,128]{1,0:T(8,128)(2,1)S(1)} %copy-done.16, bf16[1024,128]{1,0:T(8,128)(2,1)S(1)} %collective-permute-done.refs_1_, ...), custom_call_target="tpu_custom_call" | custom-call | flops 805306368 | bytes 1048576 | tf_op jit(solution)/shard_map/look/pallas_call | solution.py:481
  14.7 2.5 %collective-permute-done.3.refs_0_ = bf16[1024,128]{1,0:T(8,128)(2,1)S(1)} collective-permute-done((bf16[1024,128]{1,0:T(8,128)(2,1)S(1)}, bf16[1024,128]{1,0:T(8,128)(2,1)S(1)}, u32[]{:S(2)}, u32[]{:S(2)}) %collective-permute-start.3) | collective-permute-done | bytes 262176 | tf_op jit(solution)/shard_map/ppermute | solution.py:450
  17.4 1.6 %collective-permute-start.6 = (bf16[1024,128]{1,0:T(8,128)(2,1)S(1)}, bf16[1024,128]{1,0:T(8,128)(2,1)S(1)}, u32[]{:S(2)}, u32[]{:S(2)}) collective-permute-start(bf16[1024,128]{1,0:T(8,128)(2,1)S(1)} %collective-permute-done.3.refs_0_), channel_id=1, source_target_pairs={{0,8},{8,16},{16,24},{24,28},{28,20},{20,12},{12,4},{4,0},{1,9},{9... | collective-permute-start | bytes 786440 | tf_op jit(solution)/shard_map/ppermute | solution.py:450
  21.1 1.8 %look.5.refs_1_ = f32[1024,128]{1,0:T(8,128)S(1)} custom-call(bf16[1024,128]{1,0:T(8,128)(2,1)S(1)} %get-tuple-element.94.low_ref, bf16[1024,128]{1,0:T(8,128)(2,1)S(1)} %get-tuple-element.95.high_ref, bf16[1024,128]{1,0:T(8,128)(2,1)S(1)} %collective-permute-done.3.refs_0_, bf16[1024,128]{1,0:T(8,128)(2,1)S(1)} %collective-permute-done.4.refs_1_, ...), custom_call_target="tpu_custom_call" | custom-call | flops 536870912 | bytes 1048576 | tf_op jit(solution)/shard_map/look/pallas_call | solution.py:481
  25.3 1.6 %collective-permute-start.9 = (bf16[1024,128]{1,0:T(8,128)(2,1)S(1)}, bf16[1024,128]{1,0:T(8,128)(2,1)}, u32[]{:S(2)}, u32[]{:S(2)}) collective-permute-start(bf16[1024,128]{1,0:T(8,128)(2,1)S(1)} %collective-permute-done.6.refs_0_), channel_id=1, source_target_pairs={{0,8},{8,16},{16,24},{24,28},{28,20},{20,12},{12,4},{4,0},{1,9},{9... | collective-permute-start | bytes 786440 | tf_op jit(solution)/shard_map/ppermute | solution.py:510
  27.9 4.8 %all-to-all-start.1 = ((s32[8,7,128]{2,1,0:T(8,128)}), s32[8,7,128]{2,1,0:T(8,128)S(1)}, u32[]{:S(2)}, u32[]{:S(2)}) async-start(s32[8,7,128]{2,1,0:T(8,128)} %get-tuple-element.116), calls=%async_computation.1 | async-start | bytes 65536 | tf_op jit(solution)/shard_map/all_to_all | solution.py:514
  35.1 3.8 %message.1 = (f32[1024,128]{1,0:T(8,128)}, bf16[1024,128]{1,0:T(8,128)(2,1)}) custom-call(bf16[1024,128]{1,0:T(8,128)(2,1)S(1)} %get-tuple-element.94.low_ref, bf16[1024,128]{1,0:T(8,128)(2,1)S(1)} %get-tuple-element.95.high_ref, bf16[1024,128]{1,0:T(8,128)(2,1)} %collective-permute-done.9.refs_0_, f32[1024,128]{1,0:T(8,128)S(1)} %look.7.refs_1_, ...), custom_call_target="tpu_custom_call" | custom-call | flops 536870912 | bytes 1048576 | tf_op jit(solution)/shard_map/message/pallas_call | solution.py:533
  38.9 5.7 %all-to-all-start = ((bf16[32,32,128]{2,1,0:T(8,128)(2,1)}), bf16[32,32,128]{2,1,0:T(8,128)(2,1)S(1)}, u32[]{:S(2)}, u32[]{:S(2)}) async-start(bf16[32,32,128]{2,1,0:T(8,128)(2,1)} %bitcast.4), calls=%async_computation | async-start | bytes 524288 | tf_op jit(solution)/shard_map/all_to_all | solution.py:552
  46.3 8.0 %all-to-all-done.sums_ref = bf16[32,32,128]{2,1,0:T(8,128)(2,1)S(1)} async-done(((bf16[32,32,128]{2,1,0:T(8,128)(2,1)}), bf16[32,32,128]{2,1,0:T(8,128)(2,1)S(1)}, u32[]{:S(2)}, u32[]{:S(2)}) %all-to-all-start) | async-done | bytes 262176 | tf_op jit(solution)/shard_map/all_to_all | solution.py:552
  54.3 1.6 %entity.1 = (bf16[32,32,128]{2,1,0:T(8,128)(2,1)}, bf16[4,32,128]{2,1,0:T(8,128)(2,1)S(1)}, bf16[4,32,128]{2,1,0:T(8,128)(2,1)S(1)}, bf16[128,128]{1,0:T(8,128)(2,1)S(1)}) custom-call(bf16[32,32,128]{2,1,0:T(8,128)(2,1)S(1)} %all-to-all-done.sums_ref, s32[8,7,128]{2,1,0:T(8,128)S(1)} %all-to-all-done.1.idx_ref.req_ref, ...), custom_call_target="tpu_custom_call" | custom-call | flops 50331648 | bytes 1048576 | tf_op jit(solution)/shard_map/entity/pallas_call | solution.py:562
  56.0 3.5 %all-to-all-start.2 = ((bf16[32,32,128]{2,1,0:T(8,128)(2,1)}), bf16[32,32,128]{2,1,0:T(8,128)(2,1)S(1)}, u32[]{:S(2)}, u32[]{:S(2)}) async-start(bf16[32,32,128]{2,1,0:T(8,128)(2,1)} %get-tuple-element.127), calls=%async_computation.2 | async-start | bytes 524288 | tf_op jit(solution)/shard_map/all_to_all | solution.py:575
  60.6 2.5 %collective-permute-start.16 = (bf16[384,128]{1,0:T(8,128)(2,1)S(1)}, bf16[384,128]{1,0:T(8,128)(2,1)S(1)}, u32[]{:S(2)}, u32[]{:S(2)}) collective-permute-start(bf16[384,128]{1,0:T(8,128)(2,1)S(1)} %early.1), channel_id=1, source_target_pairs={{0,16},{4,20},{8,24},{12,28},{16,0},{20,4},{24,8},{28,12},{1,17},{... | collective-permute-start | bytes 294920 | tf_op jit(solution)/shard_map/ppermute | solution.py:601
  63.2 1.5 %collective-permute-start.14 = (bf16[192,128]{1,0:T(8,128)(2,1)S(1)}, bf16[192,128]{1,0:T(8,128)(2,1)S(1)}, u32[]{:S(2)}, u32[]{:S(2)}) collective-permute-start(bf16[192,128]{1,0:T(8,128)(2,1)S(1)} %get-tuple-element.122), channel_id=1, source_target_pairs={{0,2},{1,3},{2,0},{3,1},{4,6},{5,7},{6,4},{7,5},{8,10},{9,11},{10,... | collective-permute-start | bytes 147464 | tf_op jit(solution)/shard_map/ppermute | solution.py:453
  65.4 2.1 %collective-permute-done.14.refs_2_ = bf16[192,128]{1,0:T(8,128)(2,1)S(1)} collective-permute-done((bf16[192,128]{1,0:T(8,128)(2,1)S(1)}, bf16[192,128]{1,0:T(8,128)(2,1)S(1)}, u32[]{:S(2)}, u32[]{:S(2)}) %collective-permute-start.14) | collective-permute-done | bytes 49184 | tf_op jit(solution)/shard_map/ppermute | solution.py:453
  70.1 2.8 %collective-permute-done.16.slopes_ref = bf16[384,128]{1,0:T(8,128)(2,1)S(1)} collective-permute-done((bf16[384,128]{1,0:T(8,128)(2,1)S(1)}, bf16[384,128]{1,0:T(8,128)(2,1)S(1)}, u32[]{:S(2)}, u32[]{:S(2)}) %collective-permute-start.16) | collective-permute-done | bytes 98336 | tf_op jit(solution)/shard_map/ppermute | solution.py:601
  74.5 1.6 %backward.1 = (bf16[1024,128]{1,0:T(8,128)(2,1)S(1)}, bf16[8,64,128]{2,1,0:T(8,128)(2,1)S(1)}) custom-call(f32[1024,128]{1,0:T(8,128)S(1)} %copy-done, bf16[1024,128]{1,0:T(8,128)(2,1)S(1)} %bitcast.6, bf16[1024,128]{1,0:T(8,128)(2,1)S(1)} %copy-done.10, bf16[1024,128]{1,0:T(8,128)(2,1)S(1)} %copy-done.12, bf16[512,1024]{1,0:T(8,128)(2,1)S(1)} %get-tuple-element.140.xt_ref), custom_call_target="tpu_custom_call" | custom-call | flops 402653184 | bytes 1048576 | tf_op jit(solution)/shard_map/backward/pallas_call | solution.py:624
  77.5 3.8 %collective-permute-start.21 = (bf16[576,128]{1,0:T(8,128)(2,1)S(1)}, bf16[576,128]{1,0:T(8,128)(2,1)S(1)}, u32[]{:S(2)}, u32[]{:S(2)}) collective-permute-start(bf16[576,128]{1,0:T(8,128)(2,1)S(1)} %get-tuple-element.149), channel_id=1, source_target_pairs={{0,24},{4,28},{8,0},{12,4},{16,8},{20,12},{24,16},{28,20},{1,25},{... | collective-permute-start | bytes 442376 | tf_op jit(solution)/shard_map/ppermute | solution.py:680
  81.3 2.0 %collective-permute-start.24 = (bf16[448,128]{1,0:T(8,128)(2,1)S(1)}, bf16[448,128]{1,0:T(8,128)(2,1)S(1)}, u32[]{:S(2)}, u32[]{:S(2)}) collective-permute-start(bf16[448,128]{1,0:T(8,128)(2,1)S(1)} %get-tuple-element.152), channel_id=1, source_target_pairs={{0,28},{4,0},{8,4},{12,8},{16,12},{20,16},{24,20},{28,24},{1,29},{... | collective-permute-start | bytes 344072 | tf_op jit(solution)/shard_map/ppermute | solution.py:680
  83.9 7.7 %collective-permute-done.22.rest_ref = bf16[192,128]{1,0:T(8,128)(2,1)S(1)} collective-permute-done((bf16[192,128]{1,0:T(8,128)(2,1)S(1)}, bf16[192,128]{1,0:T(8,128)(2,1)S(1)}, u32[]{:S(2)}, u32[]{:S(2)}) %collective-permute-start.22) | collective-permute-done | bytes 49184 | tf_op jit(solution)/shard_map/ppermute | solution.py:680
  92.0 4.3 %collective-permute-start.18 = (bf16[448,128]{1,0:T(8,128)(2,1)S(1)}, bf16[448,128]{1,0:T(8,128)(2,1)S(1)}, u32[]{:S(2)}, u32[]{:S(2)}) collective-permute-start(bf16[448,128]{1,0:T(8,128)(2,1)S(1)} %get-tuple-element.144), channel_id=1, source_target_pairs={{0,20},{4,24},{8,28},{12,0},{16,4},{20,8},{24,12},{28,16},{1,21},{... | collective-permute-start | bytes 344072 | tf_op jit(solution)/shard_map/ppermute | solution.py:680
  100.5 3.0 %collective-permute-done.18.refs_1_ = bf16[448,128]{1,0:T(8,128)(2,1)S(1)} collective-permute-done((bf16[448,128]{1,0:T(8,128)(2,1)S(1)}, bf16[448,128]{1,0:T(8,128)(2,1)S(1)}, u32[]{:S(2)}, u32[]{:S(2)}) %collective-permute-start.18) | collective-permute-done | bytes 114720 | tf_op jit(solution)/shard_map/ppermute | solution.py:680
  (110 shorter events, 28.7 us)
Async XLA Ops:
  0.6 8.3 %collective-permute-start = (bf16[1024,128]{1,0:T(8,128)(2,1)}, bf16[1024,128]{1,0:T(8,128)(2,1)S(1)}, u32[]{:S(2)}, u32[]{:S(2)}) collective-permute-start(bf16[1024,128]{1,0:T(8,128)(2,1)} %refs_0_.2), channel_id=1, source_target_pairs={{0,8},{8,16},{16,24},{24,28},{28,20},{20,12},{12,4},{4,0},{1,9},{9... | collective-permute-start | bytes 786440 | tf_op jit(solution)/shard_map/ppermute | solution.py:450
  0.7 8.3 %collective-permute-start.1 = (bf16[1024,128]{1,0:T(8,128)(2,1)}, bf16[1024,128]{1,0:T(8,128)(2,1)S(1)}, u32[]{:S(2)}, u32[]{:S(2)}) collective-permute-start(bf16[1024,128]{1,0:T(8,128)(2,1)} %refs_0_.2), channel_id=1, source_target_pairs={{8,0},{16,8},{24,16},{28,24},{20,28},{12,20},{4,12},{0,4},{9,1},{1... | collective-permute-start | bytes 786440 | tf_op jit(solution)/shard_map/ppermute | solution.py:450
  2.7 6.3 %collective-permute-start.2 = (bf16[1024,128]{1,0:T(8,128)(2,1)}, bf16[1024,128]{1,0:T(8,128)(2,1)S(1)}, u32[]{:S(2)}, u32[]{:S(2)}) collective-permute-start(bf16[1024,128]{1,0:T(8,128)(2,1)} %refs_0_.4), channel_id=1, source_target_pairs={{0,1},{1,0},{2,3},{3,2},{4,5},{5,4},{6,7},{7,6},{8,9},{9,8},{10,11... | collective-permute-start | bytes 786440 | tf_op jit(solution)/shard_map/ppermute | solution.py:453
  2.7 11.9 %collective-permute-start.5 = (bf16[1024,128]{1,0:T(8,128)(2,1)}, bf16[1024,128]{1,0:T(8,128)(2,1)S(1)}, u32[]{:S(2)}, u32[]{:S(2)}) collective-permute-start(bf16[1024,128]{1,0:T(8,128)(2,1)} %refs_0_.4), channel_id=1, source_target_pairs={{0,2},{1,3},{2,0},{3,1},{4,6},{5,7},{6,4},{7,5},{8,10},{9,11},{10,... | collective-permute-start | bytes 786440 | tf_op jit(solution)/shard_map/ppermute | solution.py:453
  9.1 8.1 %collective-permute-start.3 = (bf16[1024,128]{1,0:T(8,128)(2,1)S(1)}, bf16[1024,128]{1,0:T(8,128)(2,1)S(1)}, u32[]{:S(2)}, u32[]{:S(2)}) collective-permute-start(bf16[1024,128]{1,0:T(8,128)(2,1)S(1)} %collective-permute-done.refs_1_), channel_id=1, source_target_pairs={{0,8},{8,16},{16,24},{24,28},{28,20},{20,12},{12,4},{4,0},{1,9},{9... | collective-permute-start | bytes 786440 | tf_op jit(solution)/shard_map/ppermute | solution.py:450
  10.8 6.6 %collective-permute-start.4 = (bf16[1024,128]{1,0:T(8,128)(2,1)S(1)}, bf16[1024,128]{1,0:T(8,128)(2,1)S(1)}, u32[]{:S(2)}, u32[]{:S(2)}) collective-permute-start(bf16[1024,128]{1,0:T(8,128)(2,1)S(1)} %collective-permute-done.1.refs_2_), channel_id=1, source_target_pairs={{8,0},{16,8},{24,16},{28,24},{20,28},{12,20},{4,12},{0,4},{9,1},{1... | collective-permute-start | bytes 786440 | tf_op jit(solution)/shard_map/ppermute | solution.py:450
  17.4 7.0 %collective-permute-start.6 = (bf16[1024,128]{1,0:T(8,128)(2,1)S(1)}, bf16[1024,128]{1,0:T(8,128)(2,1)S(1)}, u32[]{:S(2)}, u32[]{:S(2)}) collective-permute-start(bf16[1024,128]{1,0:T(8,128)(2,1)S(1)} %collective-permute-done.3.refs_0_), channel_id=1, source_target_pairs={{0,8},{8,16},{16,24},{24,28},{28,20},{20,12},{12,4},{4,0},{1,9},{9... | collective-permute-start | bytes 786440 | tf_op jit(solution)/shard_map/ppermute | solution.py:450
  19.0 6.4 %collective-permute-start.7 = (bf16[1024,128]{1,0:T(8,128)(2,1)S(1)}, bf16[1024,128]{1,0:T(8,128)(2,1)S(1)}, u32[]{:S(2)}, u32[]{:S(2)}) collective-permute-start(bf16[1024,128]{1,0:T(8,128)(2,1)S(1)} %collective-permute-done.4.refs_1_), channel_id=1, source_target_pairs={{8,0},{16,8},{24,16},{28,24},{20,28},{12,20},{4,12},{0,4},{9,1},{1... | collective-permute-start | bytes 786440 | tf_op jit(solution)/shard_map/ppermute | solution.py:450
  19.4 5.9 %collective-permute-start.8 = (bf16[1024,128]{1,0:T(8,128)(2,1)S(1)}, bf16[1024,128]{1,0:T(8,128)(2,1)S(1)}, u32[]{:S(2)}, u32[]{:S(2)}) collective-permute-start(bf16[1024,128]{1,0:T(8,128)(2,1)S(1)} %collective-permute-done.5.refs_2_), channel_id=1, source_target_pairs={{0,1},{1,0},{2,3},{3,2},{4,5},{5,4},{6,7},{7,6},{8,9},{9,8},{10,11... | collective-permute-start | bytes 786440 | tf_op jit(solution)/shard_map/ppermute | solution.py:453
  19.4 15.6 %collective-permute-start.10 = (bf16[1280,128]{1,0:T(8,128)(2,1)S(1)}, bf16[1280,128]{1,0:T(8,128)(2,1)S(1)}, u32[]{:S(2)}, u32[]{:S(2)}) collective-permute-start(bf16[1280,128]{1,0:T(8,128)(2,1)S(1)} %pad_maximum_fusion.refs_4_.refs_0_), channel_id=1, source_target_pairs={{0,2},{1,3},{2,0},{3,1},{4,6},{5,7},{6,4},{7,5},{8,10},{9,11},{10,... | collective-permute-start | bytes 983048 | tf_op jit(solution)/shard_map/ppermute | solution.py:453
  20.9 14.2 %collective-permute-start.11 = (bf16[1280,128]{1,0:T(8,128)(2,1)S(1)}, bf16[1280,128]{1,0:T(8,128)(2,1)S(1)}, u32[]{:S(2)}, u32[]{:S(2)}) collective-permute-start(bf16[1280,128]{1,0:T(8,128)(2,1)S(1)} %pad_maximum_fusion.refs_4_.refs_0_), channel_id=1, source_target_pairs={{0,1},{1,0},{2,3},{3,2},{4,5},{5,4},{6,7},{7,6},{8,9},{9,8},{10,11... | collective-permute-start | bytes 983048 | tf_op jit(solution)/shard_map/ppermute | solution.py:453
  25.3 9.7 %collective-permute-start.9 = (bf16[1024,128]{1,0:T(8,128)(2,1)S(1)}, bf16[1024,128]{1,0:T(8,128)(2,1)}, u32[]{:S(2)}, u32[]{:S(2)}) collective-permute-start(bf16[1024,128]{1,0:T(8,128)(2,1)S(1)} %collective-permute-done.6.refs_0_), channel_id=1, source_target_pairs={{0,8},{8,16},{16,24},{24,28},{28,20},{20,12},{12,4},{4,0},{1,9},{9... | collective-permute-start | bytes 786440 | tf_op jit(solution)/shard_map/ppermute | solution.py:510
  27.9 11.0 %all-to-all-start.1 = ((s32[8,7,128]{2,1,0:T(8,128)}), s32[8,7,128]{2,1,0:T(8,128)S(1)}, u32[]{:S(2)}, u32[]{:S(2)}) async-start(s32[8,7,128]{2,1,0:T(8,128)} %get-tuple-element.116), calls=%async_computation.1 | async-start | bytes 65536 | tf_op jit(solution)/shard_map/all_to_all | solution.py:514
  38.9 15.4 %all-to-all-start = ((bf16[32,32,128]{2,1,0:T(8,128)(2,1)}), bf16[32,32,128]{2,1,0:T(8,128)(2,1)S(1)}, u32[]{:S(2)}, u32[]{:S(2)}) async-start(bf16[32,32,128]{2,1,0:T(8,128)(2,1)} %bitcast.4), calls=%async_computation | async-start | bytes 524288 | tf_op jit(solution)/shard_map/all_to_all | solution.py:552
  56.0 17.6 %all-to-all-start.2 = ((bf16[32,32,128]{2,1,0:T(8,128)(2,1)}), bf16[32,32,128]{2,1,0:T(8,128)(2,1)S(1)}, u32[]{:S(2)}, u32[]{:S(2)}) async-start(bf16[32,32,128]{2,1,0:T(8,128)(2,1)} %get-tuple-element.127), calls=%async_computation.2 | async-start | bytes 524288 | tf_op jit(solution)/shard_map/all_to_all | solution.py:575
  60.6 12.3 %collective-permute-start.16 = (bf16[384,128]{1,0:T(8,128)(2,1)S(1)}, bf16[384,128]{1,0:T(8,128)(2,1)S(1)}, u32[]{:S(2)}, u32[]{:S(2)}) collective-permute-start(bf16[384,128]{1,0:T(8,128)(2,1)S(1)} %early.1), channel_id=1, source_target_pairs={{0,16},{4,20},{8,24},{12,28},{16,0},{20,4},{24,8},{28,12},{1,17},{... | collective-permute-start | bytes 294920 | tf_op jit(solution)/shard_map/ppermute | solution.py:601
  69.4 7.4 %collective-permute-start.19 = (bf16[4,128,128]{2,1,0:T(8,128)(2,1)S(1)}, bf16[4,128,128]{2,1,0:T(8,128)(2,1)S(1)}, u32[]{:S(2)}, u32[]{:S(2)}) collective-permute-start(bf16[4,128,128]{2,1,0:T(8,128)(2,1)S(1)} %get-tuple-element.147), channel_id=1, source_target_pairs={{0,4},{4,0},{8,12},{12,8},{16,20},{20,16},{24,28},{28,24},{1,5},{5... | collective-permute-start | bytes 393224 | tf_op jit(solution)/shard_map/ppermute | solution.py:621
  76.7 15.3 %collective-permute-start.23 = (bf16[448,128]{1,0:T(8,128)(2,1)S(1)}, bf16[448,128]{1,0:T(8,128)(2,1)S(1)}, u32[]{:S(2)}, u32[]{:S(2)}) collective-permute-start(bf16[448,128]{1,0:T(8,128)(2,1)S(1)} %get-tuple-element.151), channel_id=1, source_target_pairs={{0,4},{4,8},{8,12},{12,16},{16,20},{20,24},{24,28},{28,0},{1,5},{5... | collective-permute-start | bytes 344072 | tf_op jit(solution)/shard_map/ppermute | solution.py:680
  77.4 21.8 %collective-permute-start.20 = (bf16[576,128]{1,0:T(8,128)(2,1)S(1)}, bf16[576,128]{1,0:T(8,128)(2,1)S(1)}, u32[]{:S(2)}, u32[]{:S(2)}) collective-permute-start(bf16[576,128]{1,0:T(8,128)(2,1)S(1)} %get-tuple-element.148), channel_id=1, source_target_pairs={{0,8},{4,12},{8,16},{12,20},{16,24},{20,28},{24,0},{28,4},{1,9},{5... | collective-permute-start | bytes 442376 | tf_op jit(solution)/shard_map/ppermute | solution.py:680
  77.5 21.7 %collective-permute-start.21 = (bf16[576,128]{1,0:T(8,128)(2,1)S(1)}, bf16[576,128]{1,0:T(8,128)(2,1)S(1)}, u32[]{:S(2)}, u32[]{:S(2)}) collective-permute-start(bf16[576,128]{1,0:T(8,128)(2,1)S(1)} %get-tuple-element.149), channel_id=1, source_target_pairs={{0,24},{4,28},{8,0},{12,4},{16,8},{20,12},{24,16},{28,20},{1,25},{... | collective-permute-start | bytes 442376 | tf_op jit(solution)/shard_map/ppermute | solution.py:680
  81.3 16.7 %collective-permute-start.24 = (bf16[448,128]{1,0:T(8,128)(2,1)S(1)}, bf16[448,128]{1,0:T(8,128)(2,1)S(1)}, u32[]{:S(2)}, u32[]{:S(2)}) collective-permute-start(bf16[448,128]{1,0:T(8,128)(2,1)S(1)} %get-tuple-element.152), channel_id=1, source_target_pairs={{0,28},{4,0},{8,4},{12,8},{16,12},{20,16},{24,20},{28,24},{1,29},{... | collective-permute-start | bytes 344072 | tf_op jit(solution)/shard_map/ppermute | solution.py:680
  83.3 8.4 %collective-permute-start.22 = (bf16[192,128]{1,0:T(8,128)(2,1)S(1)}, bf16[192,128]{1,0:T(8,128)(2,1)S(1)}, u32[]{:S(2)}, u32[]{:S(2)}) collective-permute-start(bf16[192,128]{1,0:T(8,128)(2,1)S(1)} %spread.7), channel_id=1, source_target_pairs={{0,16},{4,20},{8,24},{12,28},{16,0},{20,4},{24,8},{28,12},{1,17},{... | collective-permute-start | bytes 147464 | tf_op jit(solution)/shard_map/ppermute | solution.py:680
  91.7 8.8 %collective-permute-start.17 = (bf16[448,128]{1,0:T(8,128)(2,1)S(1)}, bf16[448,128]{1,0:T(8,128)(2,1)S(1)}, u32[]{:S(2)}, u32[]{:S(2)}) collective-permute-start(bf16[448,128]{1,0:T(8,128)(2,1)S(1)} %get-tuple-element.143), channel_id=1, source_target_pairs={{0,12},{4,16},{8,20},{12,24},{16,28},{20,0},{24,4},{28,8},{1,13},{... | collective-permute-start | bytes 344072 | tf_op jit(solution)/shard_map/ppermute | solution.py:680
  92.0 11.4 %collective-permute-start.18 = (bf16[448,128]{1,0:T(8,128)(2,1)S(1)}, bf16[448,128]{1,0:T(8,128)(2,1)S(1)}, u32[]{:S(2)}, u32[]{:S(2)}) collective-permute-start(bf16[448,128]{1,0:T(8,128)(2,1)S(1)} %get-tuple-element.144), channel_id=1, source_target_pairs={{0,20},{4,24},{8,28},{12,0},{16,4},{20,8},{24,12},{28,16},{1,21},{... | collective-permute-start | bytes 344072 | tf_op jit(solution)/shard_map/ppermute | solution.py:680
  (29 other events, 131.1 us)

commit v6 on v3

--- a/solution.py
+++ b/solution.py
@@ -122,19 +122,27 @@
     out_ref[:, cap // LANES, :] = hits.astype(jnp.int32)
 
 
-def gather_rows(low_ref, high_ref, rows, table_refs, firsts, hot_ref):
+def fill_rows(low_ref, high_ref, rows, blocks, firsts, hot_ref):
     at = 0
     low, high = low_ref[rows, :], high_ref[rows, :]
-    for table, first in zip(table_refs, firsts):
-        for k in range(table.shape[0] // LANES):
+    for count, first in zip(blocks, firsts):
+        for k in range(count):
             hot_ref[:, at : at + LANES] = pick_block(low, high, (first + k).astype(F32).astype(BF))
             at += LANES
+
+
+def multiply_rows(table_refs, hot_ref):
     total, at = None, 0
     for table in table_refs:
         part = dot(hot_ref[:, at : at + table.shape[0]], table[...])
         total = part if total is None else total + part
         at += table.shape[0]
     return total
+
+
+def gather_rows(low_ref, high_ref, rows, table_refs, firsts, hot_ref):
+    fill_rows(low_ref, high_ref, rows, [table.shape[0] // LANES for table in table_refs], firsts, hot_ref)
+    return multiply_rows(table_refs, hot_ref)
 
 
 def ring_at(place, n):
@@ -162,15 +170,19 @@
 def message_kernel(n, pieces, low_ref, high_ref, *refs):
     count = len(pieces)
     sources, refs = refs[:count], refs[count:]
-    base_ref, xw_ref, ent_ref, slope_out, part_ref, slope_ref, hot_ref, msg_ref, erlow_ref, erhigh_ref = refs[:10]
-    tables, (sem, table_sem) = refs[10 : 10 + count], refs[10 + count :]
+    base_ref, xw_ref, ent_ref, slope_out, part_out, slope_ref, hot_ref, msg_ref, erlow_ref, erhigh_ref = refs[:10]
+    part_ref, tables, (sem, table_sem, part_sem) = refs[10], refs[11 : 11 + count], refs[11 + count :]
     arrivals = [pltpu.make_async_copy(src, dst, table_sem) for src, dst in zip(sources, tables)]
     for copy in arrivals:
         copy.start()
     facts = low_ref.shape[0]
-    step = hot_ref.shape[0]
+    step = hot_ref.shape[1]
     place = ring_place(lax.axis_index("fact"), n)
     firsts = [lax.div(ring_at(place + hops, n) * dims + row, LANES) for hops, row, dims in pieces]
+    if count:
+        for c in range(facts // step):
+            rows = slice(c * step, (c + 1) * step)
+            fill_rows(low_ref, high_ref, rows, [table.shape[0] // LANES for table in tables], firsts, hot_ref.at[c])
     for k in range(ent_ref.shape[0]):
         here = slice(k * LANES, (k + 1) * LANES)
         erlow_ref[:, here], erhigh_ref[:, here] = row_codes(ent_ref[k : k + 1, :])
@@ -180,7 +192,7 @@
         rows = slice(c * step, (c + 1) * step)
         pre = xw_ref[rows, :] + base_ref[rows, :]
         if count:
-            pre = pre + gather_rows(low_ref, high_ref, rows, tables, firsts, hot_ref)
+            pre = pre + multiply_rows(tables, hot_ref.at[c])
         gate = jax.nn.sigmoid(pre)
         msg_ref[rows, :] = (pre * gate).astype(BF)
         slope_ref[rows, :] = gate * (1.0 + pre * (1.0 - gate))
@@ -195,8 +207,20 @@
         part_ref[rows, :] = dot(hot, msg_ref[...]).astype(BF)
         return carry
 
-    lax.fori_loop(0, part_ref.shape[0] // 256, add, 0)
-    keep.wait()
+    groups = part_ref.shape[0] // 256
+    copies = [keep]
+    if groups <= 8:
+        for pair in range(groups):
+            add(jnp.int32(pair), 0)
+            rows = slice(pair * 256, (pair + 1) * 256)
+            copies.append(pltpu.make_async_copy(part_ref.at[rows, :], part_out.at[rows, :], part_sem.at[pair]))
+            copies[-1].start()
+    else:
+        lax.fori_loop(0, groups, add, 0)
+        copies.append(pltpu.make_async_copy(part_ref, part_out, part_sem.at[0]))
+        copies[-1].start()
+    for copy in copies:
+        copy.wait()
 
 
 def project_kernel(m, w_ref, *refs):
@@ -219,7 +243,8 @@
 
 
 def entity_kernel(n, m, width, ents, sums_ref, idx_ref, *refs):
-    all_refs, (back_ref, out_ref, pre_ref, agg_ref, own_ref, hold_ref, words_ref, sem) = refs[:m], refs[m:]
+    all_refs, refs = refs[:m], refs[m:]
+    back_ref, out_ref, pre_ref, agg_ref, own_ref, hold_ref, words_ref, scaled_ref, sem, back_sem = refs
     fetch = pltpu.make_async_copy(idx_ref, words_ref, sem)
     fetch.start()
     rows_each = ents // m
@@ -252,9 +277,14 @@
         term = nt(d_pre, all_refs[j][width : 2 * width, :])
         d_agg = term if d_agg is None else d_agg + term
     for b in range(m):
-        scaled = (d_agg[:, b * LANES : (b + 1) * LANES] / divisor).astype(BF)
-        for f in range(n):
-            back_ref[f * m + b] = scaled
+        scaled_ref[b] = (d_agg[:, b * LANES : (b + 1) * LANES] / divisor).astype(BF)
+    copies = [
+        pltpu.make_async_copy(scaled_ref, back_ref.at[f * m : (f + 1) * m], back_sem.at[f]) for f in range(n)
+    ]
+    for copy in copies:
+        copy.start()
+    for copy in copies:
+        copy.wait()
 
 
 def share_kernel(m, out_ref, pre_ref, agg_ref, *share_refs):
@@ -511,19 +541,21 @@
         (pltpu.HBM((facts, LANES), F32), shape((n * ents, LANES), BF)),
         [
             pltpu.VMEM((facts, LANES), F32),
-            pltpu.VMEM((step, last_rows), BF),
+            pltpu.VMEM((facts // step, step, last_rows), BF),
             pltpu.VMEM((facts, LANES), BF),
             pltpu.VMEM((LANES, facts), BF),
             pltpu.VMEM((16, facts), BF),
+            pltpu.VMEM((n * ents, LANES), BF),
             *[pltpu.VMEM(t.shape, BF) for t in last],
             pltpu.SemaphoreType.DMA,
             pltpu.SemaphoreType.DMA,
+            pltpu.SemaphoreType.DMA((8,)),
         ],
         2 * facts * (last_rows + n * ents) * LANES,
         "message",
         limit,
         in_specs=[IN_VMEM] * 2 + [pl.BlockSpec(memory_space=pl.ANY)] * len(last) + [IN_VMEM] * 3,
-        out_specs=(IN_HBM, IN_VMEM),
+        out_specs=(IN_HBM, IN_HBM),
     )(dlow, dhigh, *last, found, xw, entity)
     sums = lax.all_to_all(part.reshape(n * m, rows_each, LANES), ("fact", "feat"), 0, 0)
     pos, entity, x_blocks, _ = tie((pos, entity, x_blocks, part))
@@ -542,11 +574,14 @@
             pltpu.VMEM((m, rows_each, LANES), BF),
             pltpu.VMEM((ents, LANES), F32),
             pltpu.VMEM(asked.shape, jnp.int32),
+            pltpu.VMEM((m, rows_each, LANES), BF),
             pltpu.SemaphoreType.DMA,
+            pltpu.SemaphoreType.DMA((n,)),
         ],
         6 * rows_each * width * width,
         "entity",
         in_specs=[IN_VMEM, pl.BlockSpec(memory_space=pl.ANY)] + [IN_VMEM] * m,
+        out_specs=(IN_HBM, IN_VMEM, IN_VMEM, IN_VMEM),
     )(sums, asked, *all_blocks)
     scaled = lax.all_to_all(back, ("fact", "feat"), 0, 0).reshape(n * ents, LANES)
     shares = call(

time: 101 us -> 100 us (0.990)
  transfers between devices with their start and end apart: 27 -> 27, of which waited for: 15 -> 16; matrix products, arithmetic and copies ran while one was open for 0% -> 0% of each run, Pallas kernels for 20% -> 19%
where the time goes in v6:
time: 100 us
  starting transfers between devices  40 us (40%)
  waiting for transfers between devices  31.9 us (32%)
  Pallas kernels  22 us (22%)
  local copies, waits for them, and re-layouts  4.95 us (5%)
  between operations  1.16 us (1%)
    ppermute x7, starting transfers between devices, shards(): lax.ppermute(message, 'fact', [(i, (i + offset) % n) for i in range(n)])  12.8 us
    ppermute x7, waiting for transfers between devices, shards(): lax.ppermute(message, 'fact', [(i, (i + offset) % n) for i in range(n)])  11.8 us
    all_to_all x1, waiting for transfers between devices, shards(): lax.all_to_all(part.reshape(n * m, rows_each, LANES), ('fact', 'feat'), 0...  8.02 us
    pallas_call x4, Pallas kernels, look(): call(functools.partial(look_kernel, n, pieces), shape((facts, LANES), F32...  6.27 us
    ppermute x9, starting transfers between devices, swap(): return lax.ppermute(block, 'feat', [(i, i ^ bit) for i in range(m)])  5.35 us
    all_to_all x1, starting transfers between devices, shards(): lax.all_to_all(part.reshape(n * m, rows_each, LANES), ('fact', 'feat'), 0...  5.21 us
    unnamed x36, local copies, waits for them, and re-layouts  4.91 us
    all_to_all x1, starting transfers between devices, shards(): asked = lax.all_to_all(asks, 'fact', 0, 0)  4.77 us
  transfers between devices with their start and end apart: 27, of which 16 were waited for; matrix products, arithmetic and copies ran while one was open for 0% of the time, Pallas kernels for 19%

profile of v6, /device:TPU:4, one launch (start us, length us, event | category | flops | bytes accessed | tf_op | source)
XLA Modules:
  0.0 100.0 jit_solution(4428049309101255302)
XLA Ops:
  0.7 2.0 %collective-permute-start.1 = (bf16[1024,128]{1,0:T(8,128)(2,1)}, bf16[1024,128]{1,0:T(8,128)(2,1)S(1)}, u32[]{:S(2)}, u32[]{:S(2)}) collective-permute-start(bf16[1024,128]{1,0:T(8,128)(2,1)} %refs_0_.2), channel_id=1, source_target_pairs={{8,0},{16,8},{24,16},{28,24},{20,28},{12,20},{4,12},{0,4},{9,1},{1... | collective-permute-start | bytes 786440 | tf_op jit(solution)/shard_map/ppermute | solution.py:456
  6.3 1.8 %route.1 = (s32[8,4,128]{2,1,0:T(4,128)}, s32[8,128]{1,0:T(8,128)S(1)}, s32[8,128]{1,0:T(8,128)S(1)}, bf16[1024,128]{1,0:T(8,128)(2,1)S(1)}, bf16[1024,128]{1,0:T(8,128)(2,1)S(1)}) custom-call(s32[8,128]{1,0:T(8,128)S(1)} %bitcast.7, s32[8,128]{1,0:T(8,128)S(1)} %bitcast.8, s32[8,128]{1,0:T(8,128)S(1)} %bitcast.9, s32[8,128]{1,0:T(8,128)S(1)} %bitcast.10), custom_call_target="tpu_custom_call" | custom-call | flops 268435456 | bytes 1048576 | tf_op jit(solution)/shard_map/route/pallas_call | solution.py:466
  9.1 1.7 %collective-permute-start.3 = (bf16[1024,128]{1,0:T(8,128)(2,1)S(1)}, bf16[1024,128]{1,0:T(8,128)(2,1)S(1)}, u32[]{:S(2)}, u32[]{:S(2)}) collective-permute-start(bf16[1024,128]{1,0:T(8,128)(2,1)S(1)} %collective-permute-done.refs_1_), channel_id=1, source_target_pairs={{0,8},{8,16},{16,24},{24,28},{28,20},{20,12},{12,4},{4,0},{1,9},{9... | collective-permute-start | bytes 786440 | tf_op jit(solution)/shard_map/ppermute | solution.py:456
  12.1 2.6 %look.4.refs_2_ = f32[1024,128]{1,0:T(8,128)S(1)} custom-call(bf16[1024,128]{1,0:T(8,128)(2,1)S(1)} %get-tuple-element.91.low_ref, bf16[1024,128]{1,0:T(8,128)(2,1)S(1)} %get-tuple-element.92.high_ref, bf16[1024,128]{1,0:T(8,128)(2,1)S(1)} %copy-done.9, bf16[1024,128]{1,0:T(8,128)(2,1)S(1)} %collective-permute-done.refs_1_, ...), custom_call_target="tpu_custom_call" | custom-call | flops 805306368 | bytes 1048576 | tf_op jit(solution)/shard_map/look/pallas_call | solution.py:487
  14.7 1.9 %collective-permute-done.3.refs_0_ = bf16[1024,128]{1,0:T(8,128)(2,1)S(1)} collective-permute-done((bf16[1024,128]{1,0:T(8,128)(2,1)S(1)}, bf16[1024,128]{1,0:T(8,128)(2,1)S(1)}, u32[]{:S(2)}, u32[]{:S(2)}) %collective-permute-start.3) | collective-permute-done | bytes 262176 | tf_op jit(solution)/shard_map/ppermute | solution.py:456
  21.1 1.8 %look.5.refs_1_ = f32[1024,128]{1,0:T(8,128)S(1)} custom-call(bf16[1024,128]{1,0:T(8,128)(2,1)S(1)} %get-tuple-element.91.low_ref, bf16[1024,128]{1,0:T(8,128)(2,1)S(1)} %get-tuple-element.92.high_ref, bf16[1024,128]{1,0:T(8,128)(2,1)S(1)} %collective-permute-done.3.refs_0_, bf16[1024,128]{1,0:T(8,128)(2,1)S(1)} %collective-permute-done.4.refs_1_, ...), custom_call_target="tpu_custom_call" | custom-call | flops 536870912 | bytes 1048576 | tf_op jit(solution)/shard_map/look/pallas_call | solution.py:487
  23.7 1.6 %collective-permute-done.7.refs_0_ = bf16[1024,128]{1,0:T(8,128)(2,1)S(1)} collective-permute-done((bf16[1024,128]{1,0:T(8,128)(2,1)S(1)}, bf16[1024,128]{1,0:T(8,128)(2,1)S(1)}, u32[]{:S(2)}, u32[]{:S(2)}) %collective-permute-start.7) | collective-permute-done | bytes 262176 | tf_op jit(solution)/shard_map/ppermute | solution.py:456
  25.3 1.6 %collective-permute-start.9 = (bf16[1024,128]{1,0:T(8,128)(2,1)S(1)}, bf16[1024,128]{1,0:T(8,128)(2,1)}, u32[]{:S(2)}, u32[]{:S(2)}) collective-permute-start(bf16[1024,128]{1,0:T(8,128)(2,1)S(1)} %collective-permute-done.6.refs_0_), channel_id=1, source_target_pairs={{0,8},{8,16},{16,24},{24,28},{28,20},{20,12},{12,4},{4,0},{1,9},{9... | collective-permute-start | bytes 786440 | tf_op jit(solution)/shard_map/ppermute | solution.py:516
  27.8 4.8 %all-to-all-start.1 = ((s32[8,4,128]{2,1,0:T(4,128)}), s32[8,4,128]{2,1,0:T(4,128)S(1)}, u32[]{:S(2)}, u32[]{:S(2)}) async-start(s32[8,4,128]{2,1,0:T(4,128)} %get-tuple-element.113), calls=%async_computation.1 | async-start | bytes 32768 | tf_op jit(solution)/shard_map/all_to_all | solution.py:520
  34.1 3.0 %message.1 = (f32[1024,128]{1,0:T(8,128)}, bf16[1024,128]{1,0:T(8,128)(2,1)}) custom-call(bf16[1024,128]{1,0:T(8,128)(2,1)S(1)} %get-tuple-element.91.low_ref, bf16[1024,128]{1,0:T(8,128)(2,1)S(1)} %get-tuple-element.92.high_ref, bf16[1024,128]{1,0:T(8,128)(2,1)} %collective-permute-done.9.refs_0_, f32[1024,128]{1,0:T(8,128)S(1)} %look.7.refs_1_, ...), custom_call_target="tpu_custom_call" | custom-call | flops 536870912 | bytes 1048576 | tf_op jit(solution)/shard_map/message/pallas_call | solution.py:539
  37.7 5.2 %all-to-all-start = ((bf16[32,32,128]{2,1,0:T(8,128)(2,1)}), bf16[32,32,128]{2,1,0:T(8,128)(2,1)S(1)}, u32[]{:S(2)}, u32[]{:S(2)}) async-start(bf16[32,32,128]{2,1,0:T(8,128)(2,1)} %bitcast.4), calls=%async_computation | async-start | bytes 524288 | tf_op jit(solution)/shard_map/all_to_all | solution.py:560
  44.6 8.0 %all-to-all-done.sums_ref = bf16[32,32,128]{2,1,0:T(8,128)(2,1)S(1)} async-done(((bf16[32,32,128]{2,1,0:T(8,128)(2,1)}), bf16[32,32,128]{2,1,0:T(8,128)(2,1)S(1)}, u32[]{:S(2)}, u32[]{:S(2)}) %all-to-all-start) | async-done | bytes 262176 | tf_op jit(solution)/shard_map/all_to_all | solution.py:560
  52.6 1.7 %entity.1 = (bf16[32,32,128]{2,1,0:T(8,128)(2,1)}, bf16[4,32,128]{2,1,0:T(8,128)(2,1)S(1)}, bf16[4,32,128]{2,1,0:T(8,128)(2,1)S(1)}, bf16[128,128]{1,0:T(8,128)(2,1)S(1)}) custom-call(bf16[32,32,128]{2,1,0:T(8,128)(2,1)S(1)} %all-to-all-done.sums_ref, s32[8,4,128]{2,1,0:T(4,128)S(1)} %all-to-all-done.1.idx_ref.req_ref, ...), custom_call_target="tpu_custom_call" | custom-call | flops 50331648 | bytes 1048576 | tf_op jit(solution)/shard_map/entity/pallas_call | solution.py:570
  54.3 3.5 %all-to-all-start.2 = ((bf16[32,32,128]{2,1,0:T(8,128)(2,1)}), bf16[32,32,128]{2,1,0:T(8,128)(2,1)S(1)}, u32[]{:S(2)}, u32[]{:S(2)}) async-start(bf16[32,32,128]{2,1,0:T(8,128)(2,1)} %get-tuple-element.124), calls=%async_computation.2 | async-start | bytes 524288 | tf_op jit(solution)/shard_map/all_to_all | solution.py:586
  62.1 1.8 %collective-permute-done.14.refs_2_ = bf16[192,128]{1,0:T(8,128)(2,1)S(1)} collective-permute-done((bf16[192,128]{1,0:T(8,128)(2,1)S(1)}, bf16[192,128]{1,0:T(8,128)(2,1)S(1)}, u32[]{:S(2)}, u32[]{:S(2)}) %collective-permute-start.14) | collective-permute-done | bytes 49184 | tf_op jit(solution)/shard_map/ppermute | solution.py:459
  67.7 1.6 %backward.1 = (bf16[1024,128]{1,0:T(8,128)(2,1)S(1)}, bf16[8,64,128]{2,1,0:T(8,128)(2,1)S(1)}) custom-call(f32[1024,128]{1,0:T(8,128)S(1)} %copy-done.7, bf16[1024,128]{1,0:T(8,128)(2,1)S(1)} %bitcast.6, bf16[1024,128]{1,0:T(8,128)(2,1)S(1)} %get-tuple-element.133.low_ref, bf16[1024,128]{1,0:T(8,128)(2,1)S(1)} %get-tuple-element.134.high_ref, ...), custom_call_target="tpu_custom_call" | custom-call | flops 402653184 | bytes 1048576 | tf_op jit(solution)/shard_map/backward/pallas_call | solution.py:624
  72.4 2.1 %collective-permute-start.21 = (bf16[576,128]{1,0:T(8,128)(2,1)S(1)}, bf16[576,128]{1,0:T(8,128)(2,1)S(1)}, u32[]{:S(2)}, u32[]{:S(2)}) collective-permute-start(bf16[576,128]{1,0:T(8,128)(2,1)S(1)} %spread.7), channel_id=1, source_target_pairs={{0,16},{4,20},{8,24},{12,28},{16,0},{20,4},{24,8},{28,12},{1,17},{... | collective-permute-start | bytes 442376 | tf_op jit(solution)/shard_map/ppermute | solution.py:678
  75.1 1.8 %collective-permute-start.19 = (bf16[576,128]{1,0:T(8,128)(2,1)S(1)}, bf16[576,128]{1,0:T(8,128)(2,1)S(1)}, u32[]{:S(2)}, u32[]{:S(2)}) collective-permute-start(bf16[576,128]{1,0:T(8,128)(2,1)S(1)} %get-tuple-element.143), channel_id=1, source_target_pairs={{0,8},{4,12},{8,16},{12,20},{16,24},{20,28},{24,0},{28,4},{1,9},{5... | collective-permute-start | bytes 442376 | tf_op jit(solution)/shard_map/ppermute | solution.py:678
  76.8 2.1 %collective-permute-start.20 = (bf16[576,128]{1,0:T(8,128)(2,1)S(1)}, bf16[576,128]{1,0:T(8,128)(2,1)S(1)}, u32[]{:S(2)}, u32[]{:S(2)}) collective-permute-start(bf16[576,128]{1,0:T(8,128)(2,1)S(1)} %get-tuple-element.144), channel_id=1, source_target_pairs={{0,24},{4,28},{8,0},{12,4},{16,8},{20,12},{24,16},{28,20},{1,25},{... | collective-permute-start | bytes 442376 | tf_op jit(solution)/shard_map/ppermute | solution.py:678
  79.5 2.4 %collective-permute-start.16 = (bf16[448,128]{1,0:T(8,128)(2,1)S(1)}, bf16[448,128]{1,0:T(8,128)(2,1)S(1)}, u32[]{:S(2)}, u32[]{:S(2)}) collective-permute-start(bf16[448,128]{1,0:T(8,128)(2,1)S(1)} %get-tuple-element.138), channel_id=1, source_target_pairs={{0,12},{4,16},{8,20},{12,24},{16,28},{20,0},{24,4},{28,8},{1,13},{... | collective-permute-start | bytes 344072 | tf_op jit(solution)/shard_map/ppermute | solution.py:678
  81.9 2.3 %collective-permute-start.17 = (bf16[448,128]{1,0:T(8,128)(2,1)S(1)}, bf16[448,128]{1,0:T(8,128)(2,1)S(1)}, u32[]{:S(2)}, u32[]{:S(2)}) collective-permute-start(bf16[448,128]{1,0:T(8,128)(2,1)S(1)} %get-tuple-element.139), channel_id=1, source_target_pairs={{0,20},{4,24},{8,28},{12,0},{16,4},{20,8},{24,12},{28,16},{1,21},{... | collective-permute-start | bytes 344072 | tf_op jit(solution)/shard_map/ppermute | solution.py:678
  85.7 2.3 %collective-permute-done.21.refs_0_ = bf16[576,128]{1,0:T(8,128)(2,1)S(1)} collective-permute-done((bf16[576,128]{1,0:T(8,128)(2,1)S(1)}, bf16[576,128]{1,0:T(8,128)(2,1)S(1)}, u32[]{:S(2)}, u32[]{:S(2)}) %collective-permute-start.21) | collective-permute-done | bytes 147488 | tf_op jit(solution)/shard_map/ppermute | solution.py:678
  89.5 2.6 %collective-permute-done.16.refs_0_ = bf16[448,128]{1,0:T(8,128)(2,1)S(1)} collective-permute-done((bf16[448,128]{1,0:T(8,128)(2,1)S(1)}, bf16[448,128]{1,0:T(8,128)(2,1)S(1)}, u32[]{:S(2)}, u32[]{:S(2)}) %collective-permute-start.16) | collective-permute-done | bytes 114720 | tf_op jit(solution)/shard_map/ppermute | solution.py:678
  92.1 6.4 %collective-permute-done.17.refs_1_ = bf16[448,128]{1,0:T(8,128)(2,1)S(1)} collective-permute-done((bf16[448,128]{1,0:T(8,128)(2,1)S(1)}, bf16[448,128]{1,0:T(8,128)(2,1)S(1)}, u32[]{:S(2)}, u32[]{:S(2)}) %collective-permute-start.17) | collective-permute-done | bytes 114720 | tf_op jit(solution)/shard_map/ppermute | solution.py:678
  (92 shorter events, 32.2 us)
Async XLA Ops:
  0.6 8.3 %collective-permute-start = (bf16[1024,128]{1,0:T(8,128)(2,1)}, bf16[1024,128]{1,0:T(8,128)(2,1)S(1)}, u32[]{:S(2)}, u32[]{:S(2)}) collective-permute-start(bf16[1024,128]{1,0:T(8,128)(2,1)} %refs_0_.2), channel_id=1, source_target_pairs={{0,8},{8,16},{16,24},{24,28},{28,20},{20,12},{12,4},{4,0},{1,9},{9... | collective-permute-start | bytes 786440 | tf_op jit(solution)/shard_map/ppermute | solution.py:456
  0.7 8.3 %collective-permute-start.1 = (bf16[1024,128]{1,0:T(8,128)(2,1)}, bf16[1024,128]{1,0:T(8,128)(2,1)S(1)}, u32[]{:S(2)}, u32[]{:S(2)}) collective-permute-start(bf16[1024,128]{1,0:T(8,128)(2,1)} %refs_0_.2), channel_id=1, source_target_pairs={{8,0},{16,8},{24,16},{28,24},{20,28},{12,20},{4,12},{0,4},{9,1},{1... | collective-permute-start | bytes 786440 | tf_op jit(solution)/shard_map/ppermute | solution.py:456
  2.7 6.3 %collective-permute-start.2 = (bf16[1024,128]{1,0:T(8,128)(2,1)}, bf16[1024,128]{1,0:T(8,128)(2,1)S(1)}, u32[]{:S(2)}, u32[]{:S(2)}) collective-permute-start(bf16[1024,128]{1,0:T(8,128)(2,1)} %refs_0_.4), channel_id=1, source_target_pairs={{0,1},{1,0},{2,3},{3,2},{4,5},{5,4},{6,7},{7,6},{8,9},{9,8},{10,11... | collective-permute-start | bytes 786440 | tf_op jit(solution)/shard_map/ppermute | solution.py:459
  2.7 11.9 %collective-permute-start.5 = (bf16[1024,128]{1,0:T(8,128)(2,1)}, bf16[1024,128]{1,0:T(8,128)(2,1)S(1)}, u32[]{:S(2)}, u32[]{:S(2)}) collective-permute-start(bf16[1024,128]{1,0:T(8,128)(2,1)} %refs_0_.4), channel_id=1, source_target_pairs={{0,2},{1,3},{2,0},{3,1},{4,6},{5,7},{6,4},{7,5},{8,10},{9,11},{10,... | collective-permute-start | bytes 786440 | tf_op jit(solution)/shard_map/ppermute | solution.py:459
  9.1 7.6 %collective-permute-start.3 = (bf16[1024,128]{1,0:T(8,128)(2,1)S(1)}, bf16[1024,128]{1,0:T(8,128)(2,1)S(1)}, u32[]{:S(2)}, u32[]{:S(2)}) collective-permute-start(bf16[1024,128]{1,0:T(8,128)(2,1)S(1)} %collective-permute-done.refs_1_), channel_id=1, source_target_pairs={{0,8},{8,16},{16,24},{24,28},{28,20},{20,12},{12,4},{4,0},{1,9},{9... | collective-permute-start | bytes 786440 | tf_op jit(solution)/shard_map/ppermute | solution.py:456
  10.8 6.6 %collective-permute-start.4 = (bf16[1024,128]{1,0:T(8,128)(2,1)S(1)}, bf16[1024,128]{1,0:T(8,128)(2,1)S(1)}, u32[]{:S(2)}, u32[]{:S(2)}) collective-permute-start(bf16[1024,128]{1,0:T(8,128)(2,1)S(1)} %collective-permute-done.1.refs_2_), channel_id=1, source_target_pairs={{8,0},{16,8},{24,16},{28,24},{20,28},{12,20},{4,12},{0,4},{9,1},{1... | collective-permute-start | bytes 786440 | tf_op jit(solution)/shard_map/ppermute | solution.py:456
  17.3 6.4 %collective-permute-start.6 = (bf16[1024,128]{1,0:T(8,128)(2,1)S(1)}, bf16[1024,128]{1,0:T(8,128)(2,1)S(1)}, u32[]{:S(2)}, u32[]{:S(2)}) collective-permute-start(bf16[1024,128]{1,0:T(8,128)(2,1)S(1)} %collective-permute-done.3.refs_0_), channel_id=1, source_target_pairs={{0,8},{8,16},{16,24},{24,28},{28,20},{20,12},{12,4},{4,0},{1,9},{9... | collective-permute-start | bytes 786440 | tf_op jit(solution)/shard_map/ppermute | solution.py:456
  18.9 6.4 %collective-permute-start.7 = (bf16[1024,128]{1,0:T(8,128)(2,1)S(1)}, bf16[1024,128]{1,0:T(8,128)(2,1)S(1)}, u32[]{:S(2)}, u32[]{:S(2)}) collective-permute-start(bf16[1024,128]{1,0:T(8,128)(2,1)S(1)} %collective-permute-done.4.refs_1_), channel_id=1, source_target_pairs={{8,0},{16,8},{24,16},{28,24},{20,28},{12,20},{4,12},{0,4},{9,1},{1... | collective-permute-start | bytes 786440 | tf_op jit(solution)/shard_map/ppermute | solution.py:456
  19.4 5.9 %collective-permute-start.8 = (bf16[1024,128]{1,0:T(8,128)(2,1)S(1)}, bf16[1024,128]{1,0:T(8,128)(2,1)S(1)}, u32[]{:S(2)}, u32[]{:S(2)}) collective-permute-start(bf16[1024,128]{1,0:T(8,128)(2,1)S(1)} %collective-permute-done.5.refs_2_), channel_id=1, source_target_pairs={{0,1},{1,0},{2,3},{3,2},{4,5},{5,4},{6,7},{7,6},{8,9},{9,8},{10,11... | collective-permute-start | bytes 786440 | tf_op jit(solution)/shard_map/ppermute | solution.py:459
  19.4 14.7 %collective-permute-start.10 = (bf16[1280,128]{1,0:T(8,128)(2,1)S(1)}, bf16[1280,128]{1,0:T(8,128)(2,1)S(1)}, u32[]{:S(2)}, u32[]{:S(2)}) collective-permute-start(bf16[1280,128]{1,0:T(8,128)(2,1)S(1)} %pad_maximum_fusion.refs_4_.refs_0_), channel_id=1, source_target_pairs={{0,2},{1,3},{2,0},{3,1},{4,6},{5,7},{6,4},{7,5},{8,10},{9,11},{10,... | collective-permute-start | bytes 983048 | tf_op jit(solution)/shard_map/ppermute | solution.py:459
  20.9 13.2 %collective-permute-start.11 = (bf16[1280,128]{1,0:T(8,128)(2,1)S(1)}, bf16[1280,128]{1,0:T(8,128)(2,1)S(1)}, u32[]{:S(2)}, u32[]{:S(2)}) collective-permute-start(bf16[1280,128]{1,0:T(8,128)(2,1)S(1)} %pad_maximum_fusion.refs_4_.refs_0_), channel_id=1, source_target_pairs={{0,1},{1,0},{2,3},{3,2},{4,5},{5,4},{6,7},{7,6},{8,9},{9,8},{10,11... | collective-permute-start | bytes 983048 | tf_op jit(solution)/shard_map/ppermute | solution.py:459
  25.3 8.7 %collective-permute-start.9 = (bf16[1024,128]{1,0:T(8,128)(2,1)S(1)}, bf16[1024,128]{1,0:T(8,128)(2,1)}, u32[]{:S(2)}, u32[]{:S(2)}) collective-permute-start(bf16[1024,128]{1,0:T(8,128)(2,1)S(1)} %collective-permute-done.6.refs_0_), channel_id=1, source_target_pairs={{0,8},{8,16},{16,24},{24,28},{28,20},{20,12},{12,4},{4,0},{1,9},{9... | collective-permute-start | bytes 786440 | tf_op jit(solution)/shard_map/ppermute | solution.py:516
  27.8 9.9 %all-to-all-start.1 = ((s32[8,4,128]{2,1,0:T(4,128)}), s32[8,4,128]{2,1,0:T(4,128)S(1)}, u32[]{:S(2)}, u32[]{:S(2)}) async-start(s32[8,4,128]{2,1,0:T(4,128)} %get-tuple-element.113), calls=%async_computation.1 | async-start | bytes 32768 | tf_op jit(solution)/shard_map/all_to_all | solution.py:520
  37.7 14.9 %all-to-all-start = ((bf16[32,32,128]{2,1,0:T(8,128)(2,1)}), bf16[32,32,128]{2,1,0:T(8,128)(2,1)S(1)}, u32[]{:S(2)}, u32[]{:S(2)}) async-start(bf16[32,32,128]{2,1,0:T(8,128)(2,1)} %bitcast.4), calls=%async_computation | async-start | bytes 524288 | tf_op jit(solution)/shard_map/all_to_all | solution.py:560
  54.3 13.3 %all-to-all-start.2 = ((bf16[32,32,128]{2,1,0:T(8,128)(2,1)}), bf16[32,32,128]{2,1,0:T(8,128)(2,1)S(1)}, u32[]{:S(2)}, u32[]{:S(2)}) async-start(bf16[32,32,128]{2,1,0:T(8,128)(2,1)} %get-tuple-element.124), calls=%async_computation.2 | async-start | bytes 524288 | tf_op jit(solution)/shard_map/all_to_all | solution.py:586
  58.1 5.8 %collective-permute-start.14 = (bf16[192,128]{1,0:T(8,128)(2,1)S(1)}, bf16[192,128]{1,0:T(8,128)(2,1)S(1)}, u32[]{:S(2)}, u32[]{:S(2)}) collective-permute-start(bf16[192,128]{1,0:T(8,128)(2,1)S(1)} %get-tuple-element.119), channel_id=1, source_target_pairs={{0,2},{1,3},{2,0},{3,1},{4,6},{5,7},{6,4},{7,5},{8,10},{9,11},{10,... | collective-permute-start | bytes 147464 | tf_op jit(solution)/shard_map/ppermute | solution.py:459
  65.3 6.7 %collective-permute-start.18 = (bf16[4,128,128]{2,1,0:T(8,128)(2,1)S(1)}, bf16[4,128,128]{2,1,0:T(8,128)(2,1)S(1)}, u32[]{:S(2)}, u32[]{:S(2)}) collective-permute-start(bf16[4,128,128]{2,1,0:T(8,128)(2,1)S(1)} %get-tuple-element.142), channel_id=1, source_target_pairs={{0,4},{4,0},{8,12},{12,8},{16,20},{20,16},{24,28},{28,24},{1,5},{5... | collective-permute-start | bytes 393224 | tf_op jit(solution)/shard_map/ppermute | solution.py:621
  69.9 9.6 %collective-permute-start.22 = (bf16[448,128]{1,0:T(8,128)(2,1)S(1)}, bf16[448,128]{1,0:T(8,128)(2,1)S(1)}, u32[]{:S(2)}, u32[]{:S(2)}) collective-permute-start(bf16[448,128]{1,0:T(8,128)(2,1)S(1)} %get-tuple-element.145), channel_id=1, source_target_pairs={{0,4},{4,8},{8,12},{12,16},{16,20},{20,24},{24,28},{28,0},{1,5},{5... | collective-permute-start | bytes 344072 | tf_op jit(solution)/shard_map/ppermute | solution.py:678
  71.5 10.5 %collective-permute-start.23 = (bf16[448,128]{1,0:T(8,128)(2,1)S(1)}, bf16[448,128]{1,0:T(8,128)(2,1)S(1)}, u32[]{:S(2)}, u32[]{:S(2)}) collective-permute-start(bf16[448,128]{1,0:T(8,128)(2,1)S(1)} %get-tuple-element.146), channel_id=1, source_target_pairs={{0,28},{4,0},{8,4},{12,8},{16,12},{20,16},{24,20},{28,24},{1,29},{... | collective-permute-start | bytes 344072 | tf_op jit(solution)/shard_map/ppermute | solution.py:678
  72.4 15.6 %collective-permute-start.21 = (bf16[576,128]{1,0:T(8,128)(2,1)S(1)}, bf16[576,128]{1,0:T(8,128)(2,1)S(1)}, u32[]{:S(2)}, u32[]{:S(2)}) collective-permute-start(bf16[576,128]{1,0:T(8,128)(2,1)S(1)} %spread.7), channel_id=1, source_target_pairs={{0,16},{4,20},{8,24},{12,28},{16,0},{20,4},{24,8},{28,12},{1,17},{... | collective-permute-start | bytes 442376 | tf_op jit(solution)/shard_map/ppermute | solution.py:678
  75.1 13.3 %collective-permute-start.19 = (bf16[576,128]{1,0:T(8,128)(2,1)S(1)}, bf16[576,128]{1,0:T(8,128)(2,1)S(1)}, u32[]{:S(2)}, u32[]{:S(2)}) collective-permute-start(bf16[576,128]{1,0:T(8,128)(2,1)S(1)} %get-tuple-element.143), channel_id=1, source_target_pairs={{0,8},{4,12},{8,16},{12,20},{16,24},{20,28},{24,0},{28,4},{1,9},{5... | collective-permute-start | bytes 442376 | tf_op jit(solution)/shard_map/ppermute | solution.py:678
  76.8 12.1 %collective-permute-start.20 = (bf16[576,128]{1,0:T(8,128)(2,1)S(1)}, bf16[576,128]{1,0:T(8,128)(2,1)S(1)}, u32[]{:S(2)}, u32[]{:S(2)}) collective-permute-start(bf16[576,128]{1,0:T(8,128)(2,1)S(1)} %get-tuple-element.144), channel_id=1, source_target_pairs={{0,24},{4,28},{8,0},{12,4},{16,8},{20,12},{24,16},{28,20},{1,25},{... | collective-permute-start | bytes 442376 | tf_op jit(solution)/shard_map/ppermute | solution.py:678
  79.5 12.6 %collective-permute-start.16 = (bf16[448,128]{1,0:T(8,128)(2,1)S(1)}, bf16[448,128]{1,0:T(8,128)(2,1)S(1)}, u32[]{:S(2)}, u32[]{:S(2)}) collective-permute-start(bf16[448,128]{1,0:T(8,128)(2,1)S(1)} %get-tuple-element.138), channel_id=1, source_target_pairs={{0,12},{4,16},{8,20},{12,24},{16,28},{20,0},{24,4},{28,8},{1,13},{... | collective-permute-start | bytes 344072 | tf_op jit(solution)/shard_map/ppermute | solution.py:678
  81.9 16.5 %collective-permute-start.17 = (bf16[448,128]{1,0:T(8,128)(2,1)S(1)}, bf16[448,128]{1,0:T(8,128)(2,1)S(1)}, u32[]{:S(2)}, u32[]{:S(2)}) collective-permute-start(bf16[448,128]{1,0:T(8,128)(2,1)S(1)} %get-tuple-element.139), channel_id=1, source_target_pairs={{0,20},{4,24},{8,28},{12,0},{16,4},{20,8},{24,12},{28,16},{1,21},{... | collective-permute-start | bytes 344072 | tf_op jit(solution)/shard_map/ppermute | solution.py:678
  (21 other events, 115.4 us)

commit v7 on v6

--- a/solution.py
+++ b/solution.py
@@ -12,7 +12,7 @@
 IN_HBM = pl.BlockSpec(memory_space=pltpu.HBM)
 IN_VMEM = pl.BlockSpec(memory_space=pltpu.VMEM)
 F32 = jnp.float32
-VMEM_LIMIT = 16 * 1024 * 1024
+VMEM_LIMIT = 10 * 1024 * 1024
 VMEM_LIMIT_LARGE = 40 * 1024 * 1024
 
 

time: 100 us -> 100 us (level)
  no operation moved by 1% of the time
where the time goes in v7:
time: 100 us
  starting transfers between devices  40 us (40%)
  waiting for transfers between devices  31.9 us (32%)
  Pallas kernels  22 us (22%)
  local copies, waits for them, and re-layouts  4.95 us (5%)
  between operations  1.16 us (1%)
    ppermute x7, starting transfers between devices, shards(): lax.ppermute(message, 'fact', [(i, (i + offset) % n) for i in range(n)])  12.8 us
    ppermute x7, waiting for transfers between devices, shards(): lax.ppermute(message, 'fact', [(i, (i + offset) % n) for i in range(n)])  11.8 us
    all_to_all x1, waiting for transfers between devices, shards(): lax.all_to_all(part.reshape(n * m, rows_each, LANES), ('fact', 'feat'), 0...  8.02 us
    pallas_call x4, Pallas kernels, look(): call(functools.partial(look_kernel, n, pieces), shape((facts, LANES), F32...  6.26 us
    ppermute x9, starting transfers between devices, swap(): return lax.ppermute(block, 'feat', [(i, i ^ bit) for i in range(m)])  5.35 us
    all_to_all x1, starting transfers between devices, shards(): lax.all_to_all(part.reshape(n * m, rows_each, LANES), ('fact', 'feat'), 0...  5.21 us
    unnamed x36, local copies, waits for them, and re-layouts  4.91 us
    all_to_all x1, starting transfers between devices, shards(): asked = lax.all_to_all(asks, 'fact', 0, 0)  4.77 us
  transfers between devices with their start and end apart: 27, of which 16 were waited for; matrix products, arithmetic and copies ran while one was open for 0% of the time, Pallas kernels for 19%

profile of v7, /device:TPU:4, one launch (start us, length us, event | category | flops | bytes accessed | tf_op | source)
XLA Modules:
  0.0 100.0 jit_solution(8226137731684618404)
XLA Ops:
  0.7 2.0 %collective-permute-start.1 = (bf16[1024,128]{1,0:T(8,128)(2,1)}, bf16[1024,128]{1,0:T(8,128)(2,1)S(1)}, u32[]{:S(2)}, u32[]{:S(2)}) collective-permute-start(bf16[1024,128]{1,0:T(8,128)(2,1)} %refs_0_.2), channel_id=1, source_target_pairs={{8,0},{16,8},{24,16},{28,24},{20,28},{12,20},{4,12},{0,4},{9,1},{1... | collective-permute-start | bytes 786440 | tf_op jit(solution)/shard_map/ppermute | solution.py:456
  6.3 1.8 %route.1 = (s32[8,4,128]{2,1,0:T(4,128)}, s32[8,128]{1,0:T(8,128)S(1)}, s32[8,128]{1,0:T(8,128)S(1)}, bf16[1024,128]{1,0:T(8,128)(2,1)S(1)}, bf16[1024,128]{1,0:T(8,128)(2,1)S(1)}) custom-call(s32[8,128]{1,0:T(8,128)S(1)} %bitcast.7, s32[8,128]{1,0:T(8,128)S(1)} %bitcast.8, s32[8,128]{1,0:T(8,128)S(1)} %bitcast.9, s32[8,128]{1,0:T(8,128)S(1)} %bitcast.10), custom_call_target="tpu_custom_call" | custom-call | flops 268435456 | bytes 1048576 | tf_op jit(solution)/shard_map/route/pallas_call | solution.py:466
  9.1 1.7 %collective-permute-start.3 = (bf16[1024,128]{1,0:T(8,128)(2,1)S(1)}, bf16[1024,128]{1,0:T(8,128)(2,1)S(1)}, u32[]{:S(2)}, u32[]{:S(2)}) collective-permute-start(bf16[1024,128]{1,0:T(8,128)(2,1)S(1)} %collective-permute-done.refs_1_), channel_id=1, source_target_pairs={{0,8},{8,16},{16,24},{24,28},{28,20},{20,12},{12,4},{4,0},{1,9},{9... | collective-permute-start | bytes 786440 | tf_op jit(solution)/shard_map/ppermute | solution.py:456
  12.1 2.6 %look.4.refs_2_ = f32[1024,128]{1,0:T(8,128)S(1)} custom-call(bf16[1024,128]{1,0:T(8,128)(2,1)S(1)} %get-tuple-element.91.low_ref, bf16[1024,128]{1,0:T(8,128)(2,1)S(1)} %get-tuple-element.92.high_ref, bf16[1024,128]{1,0:T(8,128)(2,1)S(1)} %copy-done.9, bf16[1024,128]{1,0:T(8,128)(2,1)S(1)} %collective-permute-done.refs_1_, ...), custom_call_target="tpu_custom_call" | custom-call | flops 805306368 | bytes 1048576 | tf_op jit(solution)/shard_map/look/pallas_call | solution.py:487
  14.7 1.9 %collective-permute-done.3.refs_0_ = bf16[1024,128]{1,0:T(8,128)(2,1)S(1)} collective-permute-done((bf16[1024,128]{1,0:T(8,128)(2,1)S(1)}, bf16[1024,128]{1,0:T(8,128)(2,1)S(1)}, u32[]{:S(2)}, u32[]{:S(2)}) %collective-permute-start.3) | collective-permute-done | bytes 262176 | tf_op jit(solution)/shard_map/ppermute | solution.py:456
  21.1 1.8 %look.5.refs_1_ = f32[1024,128]{1,0:T(8,128)S(1)} custom-call(bf16[1024,128]{1,0:T(8,128)(2,1)S(1)} %get-tuple-element.91.low_ref, bf16[1024,128]{1,0:T(8,128)(2,1)S(1)} %get-tuple-element.92.high_ref, bf16[1024,128]{1,0:T(8,128)(2,1)S(1)} %collective-permute-done.3.refs_0_, bf16[1024,128]{1,0:T(8,128)(2,1)S(1)} %collective-permute-done.4.refs_1_, ...), custom_call_target="tpu_custom_call" | custom-call | flops 536870912 | bytes 1048576 | tf_op jit(solution)/shard_map/look/pallas_call | solution.py:487
  23.7 1.6 %collective-permute-done.7.refs_0_ = bf16[1024,128]{1,0:T(8,128)(2,1)S(1)} collective-permute-done((bf16[1024,128]{1,0:T(8,128)(2,1)S(1)}, bf16[1024,128]{1,0:T(8,128)(2,1)S(1)}, u32[]{:S(2)}, u32[]{:S(2)}) %collective-permute-start.7) | collective-permute-done | bytes 262176 | tf_op jit(solution)/shard_map/ppermute | solution.py:456
  25.3 1.6 %collective-permute-start.9 = (bf16[1024,128]{1,0:T(8,128)(2,1)S(1)}, bf16[1024,128]{1,0:T(8,128)(2,1)}, u32[]{:S(2)}, u32[]{:S(2)}) collective-permute-start(bf16[1024,128]{1,0:T(8,128)(2,1)S(1)} %collective-permute-done.6.refs_0_), channel_id=1, source_target_pairs={{0,8},{8,16},{16,24},{24,28},{28,20},{20,12},{12,4},{4,0},{1,9},{9... | collective-permute-start | bytes 786440 | tf_op jit(solution)/shard_map/ppermute | solution.py:516
  27.8 4.8 %all-to-all-start.1 = ((s32[8,4,128]{2,1,0:T(4,128)}), s32[8,4,128]{2,1,0:T(4,128)S(1)}, u32[]{:S(2)}, u32[]{:S(2)}) async-start(s32[8,4,128]{2,1,0:T(4,128)} %get-tuple-element.113), calls=%async_computation.1 | async-start | bytes 32768 | tf_op jit(solution)/shard_map/all_to_all | solution.py:520
  34.1 3.0 %message.1 = (f32[1024,128]{1,0:T(8,128)}, bf16[1024,128]{1,0:T(8,128)(2,1)}) custom-call(bf16[1024,128]{1,0:T(8,128)(2,1)S(1)} %get-tuple-element.91.low_ref, bf16[1024,128]{1,0:T(8,128)(2,1)S(1)} %get-tuple-element.92.high_ref, bf16[1024,128]{1,0:T(8,128)(2,1)} %collective-permute-done.9.refs_0_, f32[1024,128]{1,0:T(8,128)S(1)} %look.7.refs_1_, ...), custom_call_target="tpu_custom_call" | custom-call | flops 536870912 | bytes 1048576 | tf_op jit(solution)/shard_map/message/pallas_call | solution.py:539
  37.7 5.2 %all-to-all-start = ((bf16[32,32,128]{2,1,0:T(8,128)(2,1)}), bf16[32,32,128]{2,1,0:T(8,128)(2,1)S(1)}, u32[]{:S(2)}, u32[]{:S(2)}) async-start(bf16[32,32,128]{2,1,0:T(8,128)(2,1)} %bitcast.4), calls=%async_computation | async-start | bytes 524288 | tf_op jit(solution)/shard_map/all_to_all | solution.py:560
  44.6 8.0 %all-to-all-done.sums_ref = bf16[32,32,128]{2,1,0:T(8,128)(2,1)S(1)} async-done(((bf16[32,32,128]{2,1,0:T(8,128)(2,1)}), bf16[32,32,128]{2,1,0:T(8,128)(2,1)S(1)}, u32[]{:S(2)}, u32[]{:S(2)}) %all-to-all-start) | async-done | bytes 262176 | tf_op jit(solution)/shard_map/all_to_all | solution.py:560
  52.6 1.7 %entity.1 = (bf16[32,32,128]{2,1,0:T(8,128)(2,1)}, bf16[4,32,128]{2,1,0:T(8,128)(2,1)S(1)}, bf16[4,32,128]{2,1,0:T(8,128)(2,1)S(1)}, bf16[128,128]{1,0:T(8,128)(2,1)S(1)}) custom-call(bf16[32,32,128]{2,1,0:T(8,128)(2,1)S(1)} %all-to-all-done.sums_ref, s32[8,4,128]{2,1,0:T(4,128)S(1)} %all-to-all-done.1.idx_ref.req_ref, ...), custom_call_target="tpu_custom_call" | custom-call | flops 50331648 | bytes 1048576 | tf_op jit(solution)/shard_map/entity/pallas_call | solution.py:570
  54.3 3.5 %all-to-all-start.2 = ((bf16[32,32,128]{2,1,0:T(8,128)(2,1)}), bf16[32,32,128]{2,1,0:T(8,128)(2,1)S(1)}, u32[]{:S(2)}, u32[]{:S(2)}) async-start(bf16[32,32,128]{2,1,0:T(8,128)(2,1)} %get-tuple-element.124), calls=%async_computation.2 | async-start | bytes 524288 | tf_op jit(solution)/shard_map/all_to_all | solution.py:586
  62.1 1.8 %collective-permute-done.14.refs_2_ = bf16[192,128]{1,0:T(8,128)(2,1)S(1)} collective-permute-done((bf16[192,128]{1,0:T(8,128)(2,1)S(1)}, bf16[192,128]{1,0:T(8,128)(2,1)S(1)}, u32[]{:S(2)}, u32[]{:S(2)}) %collective-permute-start.14) | collective-permute-done | bytes 49184 | tf_op jit(solution)/shard_map/ppermute | solution.py:459
  67.7 1.6 %backward.1 = (bf16[1024,128]{1,0:T(8,128)(2,1)S(1)}, bf16[8,64,128]{2,1,0:T(8,128)(2,1)S(1)}) custom-call(f32[1024,128]{1,0:T(8,128)S(1)} %copy-done.7, bf16[1024,128]{1,0:T(8,128)(2,1)S(1)} %bitcast.6, bf16[1024,128]{1,0:T(8,128)(2,1)S(1)} %get-tuple-element.133.low_ref, bf16[1024,128]{1,0:T(8,128)(2,1)S(1)} %get-tuple-element.134.high_ref, ...), custom_call_target="tpu_custom_call" | custom-call | flops 402653184 | bytes 1048576 | tf_op jit(solution)/shard_map/backward/pallas_call | solution.py:624
  72.4 2.1 %collective-permute-start.21 = (bf16[576,128]{1,0:T(8,128)(2,1)S(1)}, bf16[576,128]{1,0:T(8,128)(2,1)S(1)}, u32[]{:S(2)}, u32[]{:S(2)}) collective-permute-start(bf16[576,128]{1,0:T(8,128)(2,1)S(1)} %spread.7), channel_id=1, source_target_pairs={{0,16},{4,20},{8,24},{12,28},{16,0},{20,4},{24,8},{28,12},{1,17},{... | collective-permute-start | bytes 442376 | tf_op jit(solution)/shard_map/ppermute | solution.py:678
  75.1 1.8 %collective-permute-start.19 = (bf16[576,128]{1,0:T(8,128)(2,1)S(1)}, bf16[576,128]{1,0:T(8,128)(2,1)S(1)}, u32[]{:S(2)}, u32[]{:S(2)}) collective-permute-start(bf16[576,128]{1,0:T(8,128)(2,1)S(1)} %get-tuple-element.143), channel_id=1, source_target_pairs={{0,8},{4,12},{8,16},{12,20},{16,24},{20,28},{24,0},{28,4},{1,9},{5... | collective-permute-start | bytes 442376 | tf_op jit(solution)/shard_map/ppermute | solution.py:678
  76.8 2.1 %collective-permute-start.20 = (bf16[576,128]{1,0:T(8,128)(2,1)S(1)}, bf16[576,128]{1,0:T(8,128)(2,1)S(1)}, u32[]{:S(2)}, u32[]{:S(2)}) collective-permute-start(bf16[576,128]{1,0:T(8,128)(2,1)S(1)} %get-tuple-element.144), channel_id=1, source_target_pairs={{0,24},{4,28},{8,0},{12,4},{16,8},{20,12},{24,16},{28,20},{1,25},{... | collective-permute-start | bytes 442376 | tf_op jit(solution)/shard_map/ppermute | solution.py:678
  79.5 2.4 %collective-permute-start.16 = (bf16[448,128]{1,0:T(8,128)(2,1)S(1)}, bf16[448,128]{1,0:T(8,128)(2,1)S(1)}, u32[]{:S(2)}, u32[]{:S(2)}) collective-permute-start(bf16[448,128]{1,0:T(8,128)(2,1)S(1)} %get-tuple-element.138), channel_id=1, source_target_pairs={{0,12},{4,16},{8,20},{12,24},{16,28},{20,0},{24,4},{28,8},{1,13},{... | collective-permute-start | bytes 344072 | tf_op jit(solution)/shard_map/ppermute | solution.py:678
  81.9 2.3 %collective-permute-start.17 = (bf16[448,128]{1,0:T(8,128)(2,1)S(1)}, bf16[448,128]{1,0:T(8,128)(2,1)S(1)}, u32[]{:S(2)}, u32[]{:S(2)}) collective-permute-start(bf16[448,128]{1,0:T(8,128)(2,1)S(1)} %get-tuple-element.139), channel_id=1, source_target_pairs={{0,20},{4,24},{8,28},{12,0},{16,4},{20,8},{24,12},{28,16},{1,21},{... | collective-permute-start | bytes 344072 | tf_op jit(solution)/shard_map/ppermute | solution.py:678
  85.7 2.3 %collective-permute-done.21.refs_0_ = bf16[576,128]{1,0:T(8,128)(2,1)S(1)} collective-permute-done((bf16[576,128]{1,0:T(8,128)(2,1)S(1)}, bf16[576,128]{1,0:T(8,128)(2,1)S(1)}, u32[]{:S(2)}, u32[]{:S(2)}) %collective-permute-start.21) | collective-permute-done | bytes 147488 | tf_op jit(solution)/shard_map/ppermute | solution.py:678
  89.5 2.6 %collective-permute-done.16.refs_0_ = bf16[448,128]{1,0:T(8,128)(2,1)S(1)} collective-permute-done((bf16[448,128]{1,0:T(8,128)(2,1)S(1)}, bf16[448,128]{1,0:T(8,128)(2,1)S(1)}, u32[]{:S(2)}, u32[]{:S(2)}) %collective-permute-start.16) | collective-permute-done | bytes 114720 | tf_op jit(solution)/shard_map/ppermute | solution.py:678
  92.1 6.4 %collective-permute-done.17.refs_1_ = bf16[448,128]{1,0:T(8,128)(2,1)S(1)} collective-permute-done((bf16[448,128]{1,0:T(8,128)(2,1)S(1)}, bf16[448,128]{1,0:T(8,128)(2,1)S(1)}, u32[]{:S(2)}, u32[]{:S(2)}) %collective-permute-start.17) | collective-permute-done | bytes 114720 | tf_op jit(solution)/shard_map/ppermute | solution.py:678
  (92 shorter events, 32.2 us)
Async XLA Ops:
  0.6 8.3 %collective-permute-start = (bf16[1024,128]{1,0:T(8,128)(2,1)}, bf16[1024,128]{1,0:T(8,128)(2,1)S(1)}, u32[]{:S(2)}, u32[]{:S(2)}) collective-permute-start(bf16[1024,128]{1,0:T(8,128)(2,1)} %refs_0_.2), channel_id=1, source_target_pairs={{0,8},{8,16},{16,24},{24,28},{28,20},{20,12},{12,4},{4,0},{1,9},{9... | collective-permute-start | bytes 786440 | tf_op jit(solution)/shard_map/ppermute | solution.py:456
  0.7 8.3 %collective-permute-start.1 = (bf16[1024,128]{1,0:T(8,128)(2,1)}, bf16[1024,128]{1,0:T(8,128)(2,1)S(1)}, u32[]{:S(2)}, u32[]{:S(2)}) collective-permute-start(bf16[1024,128]{1,0:T(8,128)(2,1)} %refs_0_.2), channel_id=1, source_target_pairs={{8,0},{16,8},{24,16},{28,24},{20,28},{12,20},{4,12},{0,4},{9,1},{1... | collective-permute-start | bytes 786440 | tf_op jit(solution)/shard_map/ppermute | solution.py:456
  2.7 6.3 %collective-permute-start.2 = (bf16[1024,128]{1,0:T(8,128)(2,1)}, bf16[1024,128]{1,0:T(8,128)(2,1)S(1)}, u32[]{:S(2)}, u32[]{:S(2)}) collective-permute-start(bf16[1024,128]{1,0:T(8,128)(2,1)} %refs_0_.4), channel_id=1, source_target_pairs={{0,1},{1,0},{2,3},{3,2},{4,5},{5,4},{6,7},{7,6},{8,9},{9,8},{10,11... | collective-permute-start | bytes 786440 | tf_op jit(solution)/shard_map/ppermute | solution.py:459
  2.7 11.9 %collective-permute-start.5 = (bf16[1024,128]{1,0:T(8,128)(2,1)}, bf16[1024,128]{1,0:T(8,128)(2,1)S(1)}, u32[]{:S(2)}, u32[]{:S(2)}) collective-permute-start(bf16[1024,128]{1,0:T(8,128)(2,1)} %refs_0_.4), channel_id=1, source_target_pairs={{0,2},{1,3},{2,0},{3,1},{4,6},{5,7},{6,4},{7,5},{8,10},{9,11},{10,... | collective-permute-start | bytes 786440 | tf_op jit(solution)/shard_map/ppermute | solution.py:459
  9.1 7.6 %collective-permute-start.3 = (bf16[1024,128]{1,0:T(8,128)(2,1)S(1)}, bf16[1024,128]{1,0:T(8,128)(2,1)S(1)}, u32[]{:S(2)}, u32[]{:S(2)}) collective-permute-start(bf16[1024,128]{1,0:T(8,128)(2,1)S(1)} %collective-permute-done.refs_1_), channel_id=1, source_target_pairs={{0,8},{8,16},{16,24},{24,28},{28,20},{20,12},{12,4},{4,0},{1,9},{9... | collective-permute-start | bytes 786440 | tf_op jit(solution)/shard_map/ppermute | solution.py:456
  10.8 6.6 %collective-permute-start.4 = (bf16[1024,128]{1,0:T(8,128)(2,1)S(1)}, bf16[1024,128]{1,0:T(8,128)(2,1)S(1)}, u32[]{:S(2)}, u32[]{:S(2)}) collective-permute-start(bf16[1024,128]{1,0:T(8,128)(2,1)S(1)} %collective-permute-done.1.refs_2_), channel_id=1, source_target_pairs={{8,0},{16,8},{24,16},{28,24},{20,28},{12,20},{4,12},{0,4},{9,1},{1... | collective-permute-start | bytes 786440 | tf_op jit(solution)/shard_map/ppermute | solution.py:456
  17.3 6.4 %collective-permute-start.6 = (bf16[1024,128]{1,0:T(8,128)(2,1)S(1)}, bf16[1024,128]{1,0:T(8,128)(2,1)S(1)}, u32[]{:S(2)}, u32[]{:S(2)}) collective-permute-start(bf16[1024,128]{1,0:T(8,128)(2,1)S(1)} %collective-permute-done.3.refs_0_), channel_id=1, source_target_pairs={{0,8},{8,16},{16,24},{24,28},{28,20},{20,12},{12,4},{4,0},{1,9},{9... | collective-permute-start | bytes 786440 | tf_op jit(solution)/shard_map/ppermute | solution.py:456
  18.9 6.4 %collective-permute-start.7 = (bf16[1024,128]{1,0:T(8,128)(2,1)S(1)}, bf16[1024,128]{1,0:T(8,128)(2,1)S(1)}, u32[]{:S(2)}, u32[]{:S(2)}) collective-permute-start(bf16[1024,128]{1,0:T(8,128)(2,1)S(1)} %collective-permute-done.4.refs_1_), channel_id=1, source_target_pairs={{8,0},{16,8},{24,16},{28,24},{20,28},{12,20},{4,12},{0,4},{9,1},{1... | collective-permute-start | bytes 786440 | tf_op jit(solution)/shard_map/ppermute | solution.py:456
  19.4 5.9 %collective-permute-start.8 = (bf16[1024,128]{1,0:T(8,128)(2,1)S(1)}, bf16[1024,128]{1,0:T(8,128)(2,1)S(1)}, u32[]{:S(2)}, u32[]{:S(2)}) collective-permute-start(bf16[1024,128]{1,0:T(8,128)(2,1)S(1)} %collective-permute-done.5.refs_2_), channel_id=1, source_target_pairs={{0,1},{1,0},{2,3},{3,2},{4,5},{5,4},{6,7},{7,6},{8,9},{9,8},{10,11... | collective-permute-start | bytes 786440 | tf_op jit(solution)/shard_map/ppermute | solution.py:459
  19.4 14.7 %collective-permute-start.10 = (bf16[1280,128]{1,0:T(8,128)(2,1)S(1)}, bf16[1280,128]{1,0:T(8,128)(2,1)S(1)}, u32[]{:S(2)}, u32[]{:S(2)}) collective-permute-start(bf16[1280,128]{1,0:T(8,128)(2,1)S(1)} %pad_maximum_fusion.refs_4_.refs_0_), channel_id=1, source_target_pairs={{0,2},{1,3},{2,0},{3,1},{4,6},{5,7},{6,4},{7,5},{8,10},{9,11},{10,... | collective-permute-start | bytes 983048 | tf_op jit(solution)/shard_map/ppermute | solution.py:459
  20.9 13.2 %collective-permute-start.11 = (bf16[1280,128]{1,0:T(8,128)(2,1)S(1)}, bf16[1280,128]{1,0:T(8,128)(2,1)S(1)}, u32[]{:S(2)}, u32[]{:S(2)}) collective-permute-start(bf16[1280,128]{1,0:T(8,128)(2,1)S(1)} %pad_maximum_fusion.refs_4_.refs_0_), channel_id=1, source_target_pairs={{0,1},{1,0},{2,3},{3,2},{4,5},{5,4},{6,7},{7,6},{8,9},{9,8},{10,11... | collective-permute-start | bytes 983048 | tf_op jit(solution)/shard_map/ppermute | solution.py:459
  25.3 8.7 %collective-permute-start.9 = (bf16[1024,128]{1,0:T(8,128)(2,1)S(1)}, bf16[1024,128]{1,0:T(8,128)(2,1)}, u32[]{:S(2)}, u32[]{:S(2)}) collective-permute-start(bf16[1024,128]{1,0:T(8,128)(2,1)S(1)} %collective-permute-done.6.refs_0_), channel_id=1, source_target_pairs={{0,8},{8,16},{16,24},{24,28},{28,20},{20,12},{12,4},{4,0},{1,9},{9... | collective-permute-start | bytes 786440 | tf_op jit(solution)/shard_map/ppermute | solution.py:516
  27.8 9.9 %all-to-all-start.1 = ((s32[8,4,128]{2,1,0:T(4,128)}), s32[8,4,128]{2,1,0:T(4,128)S(1)}, u32[]{:S(2)}, u32[]{:S(2)}) async-start(s32[8,4,128]{2,1,0:T(4,128)} %get-tuple-element.113), calls=%async_computation.1 | async-start | bytes 32768 | tf_op jit(solution)/shard_map/all_to_all | solution.py:520
  37.7 14.9 %all-to-all-start = ((bf16[32,32,128]{2,1,0:T(8,128)(2,1)}), bf16[32,32,128]{2,1,0:T(8,128)(2,1)S(1)}, u32[]{:S(2)}, u32[]{:S(2)}) async-start(bf16[32,32,128]{2,1,0:T(8,128)(2,1)} %bitcast.4), calls=%async_computation | async-start | bytes 524288 | tf_op jit(solution)/shard_map/all_to_all | solution.py:560
  54.3 13.3 %all-to-all-start.2 = ((bf16[32,32,128]{2,1,0:T(8,128)(2,1)}), bf16[32,32,128]{2,1,0:T(8,128)(2,1)S(1)}, u32[]{:S(2)}, u32[]{:S(2)}) async-start(bf16[32,32,128]{2,1,0:T(8,128)(2,1)} %get-tuple-element.124), calls=%async_computation.2 | async-start | bytes 524288 | tf_op jit(solution)/shard_map/all_to_all | solution.py:586
  58.1 5.8 %collective-permute-start.14 = (bf16[192,128]{1,0:T(8,128)(2,1)S(1)}, bf16[192,128]{1,0:T(8,128)(2,1)S(1)}, u32[]{:S(2)}, u32[]{:S(2)}) collective-permute-start(bf16[192,128]{1,0:T(8,128)(2,1)S(1)} %get-tuple-element.119), channel_id=1, source_target_pairs={{0,2},{1,3},{2,0},{3,1},{4,6},{5,7},{6,4},{7,5},{8,10},{9,11},{10,... | collective-permute-start | bytes 147464 | tf_op jit(solution)/shard_map/ppermute | solution.py:459
  65.3 6.7 %collective-permute-start.18 = (bf16[4,128,128]{2,1,0:T(8,128)(2,1)S(1)}, bf16[4,128,128]{2,1,0:T(8,128)(2,1)S(1)}, u32[]{:S(2)}, u32[]{:S(2)}) collective-permute-start(bf16[4,128,128]{2,1,0:T(8,128)(2,1)S(1)} %get-tuple-element.142), channel_id=1, source_target_pairs={{0,4},{4,0},{8,12},{12,8},{16,20},{20,16},{24,28},{28,24},{1,5},{5... | collective-permute-start | bytes 393224 | tf_op jit(solution)/shard_map/ppermute | solution.py:621
  69.9 9.6 %collective-permute-start.22 = (bf16[448,128]{1,0:T(8,128)(2,1)S(1)}, bf16[448,128]{1,0:T(8,128)(2,1)S(1)}, u32[]{:S(2)}, u32[]{:S(2)}) collective-permute-start(bf16[448,128]{1,0:T(8,128)(2,1)S(1)} %get-tuple-element.145), channel_id=1, source_target_pairs={{0,4},{4,8},{8,12},{12,16},{16,20},{20,24},{24,28},{28,0},{1,5},{5... | collective-permute-start | bytes 344072 | tf_op jit(solution)/shard_map/ppermute | solution.py:678
  71.5 10.5 %collective-permute-start.23 = (bf16[448,128]{1,0:T(8,128)(2,1)S(1)}, bf16[448,128]{1,0:T(8,128)(2,1)S(1)}, u32[]{:S(2)}, u32[]{:S(2)}) collective-permute-start(bf16[448,128]{1,0:T(8,128)(2,1)S(1)} %get-tuple-element.146), channel_id=1, source_target_pairs={{0,28},{4,0},{8,4},{12,8},{16,12},{20,16},{24,20},{28,24},{1,29},{... | collective-permute-start | bytes 344072 | tf_op jit(solution)/shard_map/ppermute | solution.py:678
  72.4 15.6 %collective-permute-start.21 = (bf16[576,128]{1,0:T(8,128)(2,1)S(1)}, bf16[576,128]{1,0:T(8,128)(2,1)S(1)}, u32[]{:S(2)}, u32[]{:S(2)}) collective-permute-start(bf16[576,128]{1,0:T(8,128)(2,1)S(1)} %spread.7), channel_id=1, source_target_pairs={{0,16},{4,20},{8,24},{12,28},{16,0},{20,4},{24,8},{28,12},{1,17},{... | collective-permute-start | bytes 442376 | tf_op jit(solution)/shard_map/ppermute | solution.py:678
  75.1 13.3 %collective-permute-start.19 = (bf16[576,128]{1,0:T(8,128)(2,1)S(1)}, bf16[576,128]{1,0:T(8,128)(2,1)S(1)}, u32[]{:S(2)}, u32[]{:S(2)}) collective-permute-start(bf16[576,128]{1,0:T(8,128)(2,1)S(1)} %get-tuple-element.143), channel_id=1, source_target_pairs={{0,8},{4,12},{8,16},{12,20},{16,24},{20,28},{24,0},{28,4},{1,9},{5... | collective-permute-start | bytes 442376 | tf_op jit(solution)/shard_map/ppermute | solution.py:678
  76.8 12.1 %collective-permute-start.20 = (bf16[576,128]{1,0:T(8,128)(2,1)S(1)}, bf16[576,128]{1,0:T(8,128)(2,1)S(1)}, u32[]{:S(2)}, u32[]{:S(2)}) collective-permute-start(bf16[576,128]{1,0:T(8,128)(2,1)S(1)} %get-tuple-element.144), channel_id=1, source_target_pairs={{0,24},{4,28},{8,0},{12,4},{16,8},{20,12},{24,16},{28,20},{1,25},{... | collective-permute-start | bytes 442376 | tf_op jit(solution)/shard_map/ppermute | solution.py:678
  79.5 12.6 %collective-permute-start.16 = (bf16[448,128]{1,0:T(8,128)(2,1)S(1)}, bf16[448,128]{1,0:T(8,128)(2,1)S(1)}, u32[]{:S(2)}, u32[]{:S(2)}) collective-permute-start(bf16[448,128]{1,0:T(8,128)(2,1)S(1)} %get-tuple-element.138), channel_id=1, source_target_pairs={{0,12},{4,16},{8,20},{12,24},{16,28},{20,0},{24,4},{28,8},{1,13},{... | collective-permute-start | bytes 344072 | tf_op jit(solution)/shard_map/ppermute | solution.py:678
  81.9 16.5 %collective-permute-start.17 = (bf16[448,128]{1,0:T(8,128)(2,1)S(1)}, bf16[448,128]{1,0:T(8,128)(2,1)S(1)}, u32[]{:S(2)}, u32[]{:S(2)}) collective-permute-start(bf16[448,128]{1,0:T(8,128)(2,1)S(1)} %get-tuple-element.139), channel_id=1, source_target_pairs={{0,20},{4,24},{8,28},{12,0},{16,4},{20,8},{24,12},{28,16},{1,21},{... | collective-permute-start | bytes 344072 | tf_op jit(solution)/shard_map/ppermute | solution.py:678
  (21 other events, 115.4 us)
